TPU v7x, 32 devices: a whole 2x2x4 slice. The times are simulated.
32 devices in a mesh: fsdp: 4 (over y, core), replica: 8 (over z, x).
Axes of the slice: x: 2, y: 2, z: 4, core: 2. Of those that a mesh axis runs over, the one named last changes fastest.
Arguments:
- acts: bfloat16 [8, 1024, 4096], P('replica', 'fsdp'), may hold values from -6 to 6
- cotangent: bfloat16 [8, 1024, 512], P('replica', 'fsdp'), may hold values from -0.5 to 0.5
- weight: float32 [8, 4096, 512], P('replica', 'fsdp'), may hold values from -0.09375 to 0.09375
- first_moment: bfloat16 [8, 4096, 512], P('replica', 'fsdp'), may hold values from -6 to 6
- second_moment: bfloat16 [8, 4096, 512], P('replica', 'fsdp'), may hold values from 0.25 to 4
- outer_weight: float32 [4096, 128], P('fsdp'), may hold values from -0.09375 to 0.09375
- outer_momentum: float32 [4096, 128], P('fsdp'), may hold values from -4 to 4
- mantissas: int32 [8, 4096, 128], P('replica', 'fsdp'), may hold values from -127 to 127
- exponents: int32 [8, 4096], P('replica', 'fsdp'), may hold values from -10 to -3, as said below
Outputs:
- weight_out: float32 [8, 4096, 512], P('replica', 'fsdp')
- first_out: bfloat16 [8, 4096, 512], P('replica', 'fsdp')
- second_out: bfloat16 [8, 4096, 512], P('replica', 'fsdp')
- outer_out: float32 [4096, 128], P('fsdp')
- momentum_out: float32 [4096, 128], P('fsdp')
Inputs may be any that keep to these rules, and one draw needn't show every extreme that they name: `exponents`: in every row d exactly one island holds the largest exponent.
All inputs are finite; a program needn't handle non-finite values.
Results may differ from a plain program's by a relative error of at most 0.0055.
Values may be sent and summed in bfloat16 or wider, within the bound.
No kernel may reach another device: no remote copies, remote signals or barrier semaphores. Data moves between devices by JAX's collectives and lax.ppermute only.
A program may use at most 64 MiB of HBM per device.

v0:
```python
import jax
import jax.numpy as jnp
from jax import lax
from jax.sharding import PartitionSpec as P

BETA_ONE = 0.9
BETA_TWO = 0.95
LEARN_RATE = 0.001
DECAY_RATE = 0.1
ADAM_EPSILON = 1e-08
OUTER_RATE = 0.7
OUTER_MOMENTUM = 0.9
MIX_SHARE = 0.5


def decode_words(packed_sum):
    low_part = jnp.remainder(packed_sum + 32768, 65536) - 32768
    high_part = (packed_sum - low_part) // 65536
    return (low_part, high_part)


def outer_step(summed, shared_part, weight_part, momentum_part, islands):
    pseudo = (
        summed.astype(jnp.float32) * jnp.exp2(shared_part.astype(jnp.float32))[:, None] / islands
    )
    momentum_new = OUTER_MOMENTUM * momentum_part + pseudo
    outer_new = weight_part - OUTER_RATE * (pseudo + OUTER_MOMENTUM * momentum_new)
    return (outer_new, momentum_new)


def local(
    acts,
    cotangent,
    weight,
    first_moment,
    second_moment,
    outer_weight,
    outer_momentum,
    mantissas,
    exponents,
):
    tokens = acts[0]
    cot_local = cotangent[0]
    weight_local = weight[0]
    row_total = weight_local.shape[0]
    islands = lax.axis_size("replica")
    gradient = lax.psum_scatter(
        jnp.einsum("tr,tk->rk", tokens, cot_local, preferred_element_type=jnp.float32).astype(
            jnp.bfloat16
        ),
        "fsdp",
        scatter_dimension=0,
        tiled=True,
    ).astype(jnp.float32)
    moment_one = BETA_ONE * first_moment[0].astype(jnp.float32) + (1.0 - BETA_ONE) * gradient
    moment_two = (
        BETA_TWO * second_moment[0].astype(jnp.float32) + (1.0 - BETA_TWO) * gradient * gradient
    )
    updated = weight_local - LEARN_RATE * (
        moment_one / (jnp.sqrt(moment_two) + ADAM_EPSILON) + DECAY_RATE * weight_local
    )
    updated, first_new, second_new = (
        updated,
        moment_one.astype(jnp.bfloat16),
        moment_two.astype(jnp.bfloat16),
    )
    local_exps = exponents[0]
    shared = lax.pmax(local_exps, "replica")
    aligned = jnp.right_shift(mantissas[0], (shared - local_exps)[:, None])
    half_rows = row_total // 2
    packed = aligned[half_rows:] * 65536 + aligned[:half_rows]
    packed_sum = lax.psum(packed, "replica")
    low_part, high_part = decode_words(packed_sum)
    summed = jnp.concatenate([low_part, high_part], axis=0)
    outer_new, momentum_new = outer_step(summed, shared, outer_weight, outer_momentum, islands)
    head_size = outer_new.shape[1]
    head_part = MIX_SHARE * updated[:, :head_size] + (1.0 - MIX_SHARE) * outer_new
    mixed = jnp.concatenate([head_part, updated[:, head_size:]], axis=1)
    return (mixed[None], first_new[None], second_new[None], outer_new, momentum_new)


def solution(mesh):
    in_specs = (
        P("replica", "fsdp", None),
        P("replica", "fsdp", None),
        P("replica", "fsdp", None),
        P("replica", "fsdp", None),
        P("replica", "fsdp", None),
        P("fsdp", None),
        P("fsdp", None),
        P("replica", "fsdp", None),
        P("replica", "fsdp"),
    )
    out_specs = (
        P("replica", "fsdp", None),
        P("replica", "fsdp", None),
        P("replica", "fsdp", None),
        P("fsdp", None),
        P("fsdp", None),
    )
    return jax.shard_map(local, mesh=mesh, in_specs=in_specs, out_specs=out_specs, check_vma=False)
```

profile of v0, /device:TPU:0, one launch (start us, length us, event | category | flops | bytes accessed | tf_op | source)
XLA Modules:
  0.0 111.8 jit_solution(15791119911859966916)
XLA Ops:
  8.0 0.0 copy-start
  8.0 0.0 copy-start.5
  8.0 0.0 all-reduce.2.cloned.1.call-start
  8.1 13.3 %pmax.7 = s32[1024]{0:T(1024)S(1)} all-reduce(s32[1024]{0:T(1024)} %bitcast.40), channel_id=1, replica_groups=mesh['fsdp'=4,'replica'=8] {'replica'}, use_global_device_ids=true, to_apply=%region_1.0 | all-reduce | flops 1024 | bytes 8192 | tf_op jit(solution)/shard_map/pmax | solution.py:68
  21.3 0.7 sub.22
  22.0 1.2 %bitcast_shift-right-arithmetic_fusion = s32[1024,128]{1,0:T(8,128)S(1)} fusion(s32[1,1024,128]{2,1,0:T(8,128)} %param.16, s32[1024]{0:T(1024)S(1)} %sub.22), kind=kLoop, calls=%fused_computation.20 | loop fusion | flops 131072 | bytes 1052672 | tf_op jit(solution)/shard_map/shift_right_arithmetic | solution.py:69
  23.3 0.7 slice_add_fusion.1
  24.0 0.0 all-reduce.2.cloned.1.call-update
  24.0 0.0 reduce-scatter.2.cloned.1.call-start
  24.1 0.0 copy-done
  24.1 0.0 copy-done.5
  24.1 3.2 %convolution_convert_fusion = bf16[4096,512]{1,0:T(8,128)(2,1)} fusion(bf16[1,256,4096]{2,1,0:T(8,128)(2,1)S(1)} %copy-done, bf16[1,256,512]{2,1,0:T(8,128)(2,1)S(1)} %copy-done.5), kind=kOutput, calls=%fused_computation | convolution fusion | flops 1075838976 | bytes 6553600 | tf_op jit(solution)/shard_map/tr,tk->rk/dot_general | solution.py:48
  27.3 0.0 copy-start.1
  27.3 0.0 reduce-scatter.2.cloned.1.call-update
  27.4 65.7 %all-reduce.2.cloned.1.call-done = s32[512,128]{1,0:T(8,128)} async-done(((s32[512,128]{1,0:T(8,128)}), s32[512,128]{1,0:T(8,128)}) %all-reduce.2.cloned.1.call-update) | async-done | bytes 262160 | tf_op jit(solution)/shard_map/psum | solution.py:72
  93.0 1.9 %fusion.13 = (s32[512,128]{1,0:T(8,128)S(1)}, s32[512,128]{1,0:T(8,128)}) fusion(s32[512,128]{1,0:T(8,128)} %all-reduce.2.cloned.1.call-done), kind=kLoop, calls=%fused_computation.31 | loop fusion | flops 1900544 | bytes 786432 | tf_op jit(solution)/shard_map/sub | solution.py:17
  94.9 0.0 reduce-scatter.2.cloned.1.call-done
  95.0 0.0 copy-done.1
  95.0 5.3 %fusion.7 = (bf16[1,1024,512]{2,1,0:T(8,128)(2,1)}, f32[1024,512]{1,0:T(8,128)S(1)}, bf16[1,1024,512]{2,1,0:T(8,128)(2,1)}) fusion(bf16[1024,512]{1,0:T(8,128)(2,1)} %reduce-scatter.2.cloned.1.call-done, bf16[1,1024,512]{2,1,0:T(8,128)(2,1)S(1)} %copy-done.1, bf16[1,1024,512]{2,1,0:T(8,128)(2,1)} %param.12, f32[1,1024,512]{2,1,0:T(8,128)} %param.11), kind=kLoop, calls=%fused_computation.13 | loop fusion | flops 9437184 | bytes 9437184 | tf_op jit(solution)/shard_map/broadcast_in_dim | solution.py:79
  100.2 0.0 copy-start.2
  100.2 0.0 copy-start.3
  100.2 0.0 copy-start.4
  100.2 0.1 slice.19
  100.4 0.8 copy-done.2
  101.2 0.2 copy-done.3
  101.3 0.2 copy-done.4
  101.5 1.2 %fusion.9 = (f32[1024,128]{1,0:T(8,128)S(1)}, f32[1024,128]{1,0:T(8,128)}, f32[1024,128]{1,0:T(8,128)}) fusion(f32[1024,512]{1,0:T(8,128)S(1)} %get-tuple-element.9, f32[1024,128]{1,0:T(8,128)S(1)} %copy-done.3, f32[1024]{0:T(1024)S(1)} %multiply_exponential_fusion, s32[512,128]{1,0:T(8,128)S(1)} %copy-done.2, s32[512,128]{1,0:T(8,128)S(1)} %get-tuple-element.11, ...), kind=kLoop, calls=%fused_computation.16 | loop fusion | flops 1572864 | bytes 3674112 | tf_op jit(solution)/shard_map/add | solution.py:77
  102.7 1.6 %maximum_bitcast_fusion = f32[1,1024,512]{2,1,0:T(8,128)} fusion(f32[1024,384]{1,0:T(8,128)S(1)} %slice.19, f32[1024,128]{1,0:T(8,128)S(1)} %get-tuple-element.5), kind=kLoop, calls=%fused_computation.5 | loop fusion | flops 524288 | bytes 4194304 | tf_op jit(solution)/shard_map/broadcast_in_dim | solution.py:79
  (1 shorter events, 0.0 us)
Async XLA Ops:
  8.0 16.1 %copy-start = (bf16[1,256,4096]{2,1,0:T(8,128)(2,1)S(1)}, bf16[1,256,4096]{2,1,0:T(8,128)(2,1)}, u32[]{:S(2)}) copy-start(bf16[1,256,4096]{2,1,0:T(8,128)(2,1)} %param.9) | copy-start | bytes 6291460
  8.0 16.1 %copy-start.5 = (bf16[1,256,512]{2,1,0:T(8,128)(2,1)S(1)}, bf16[1,256,512]{2,1,0:T(8,128)(2,1)}, u32[]{:S(2)}) copy-start(bf16[1,256,512]{2,1,0:T(8,128)(2,1)} %param.10) | copy-start | bytes 786436
  8.0 85.0 %all-reduce.2.cloned.1.call-start = ((), (), s32[]{:S(2)}) async-start(), calls=%async_computation.2 | async-start | bytes 524288 | tf_op jit(solution)/shard_map/psum | solution.py:72
  24.0 70.9 %reduce-scatter.2.cloned.1.call-start = ((), (), s32[]{:S(2)}) async-start(), calls=%async_computation.1 | async-start | bytes 5242880 | tf_op jit(solution)/shard_map/reduce_scatter | solution.py:47
  27.3 67.6 %copy-start.1 = (bf16[1,1024,512]{2,1,0:T(8,128)(2,1)S(1)}, bf16[1,1024,512]{2,1,0:T(8,128)(2,1)}, u32[]{:S(2)}) copy-start(bf16[1,1024,512]{2,1,0:T(8,128)(2,1)} %param.13) | copy-start | bytes 3145732
  100.2 0.9 copy-start.2
  100.2 1.1 %copy-start.3 = (f32[1024,128]{1,0:T(8,128)S(1)}, f32[1024,128]{1,0:T(8,128)}, u32[]{:S(2)}) copy-start(f32[1024,128]{1,0:T(8,128)} %param.14) | copy-start | bytes 1572868
  100.2 1.3 %copy-start.4 = (f32[1024,128]{1,0:T(8,128)S(1)}, f32[1024,128]{1,0:T(8,128)}, u32[]{:S(2)}) copy-start(f32[1024,128]{1,0:T(8,128)} %param.15) | copy-start | bytes 1572868
Sparse Core Ops, SparseCore 0:
  24.1 68.8 all-reduce.1
Sparse Core Ops, SparseCore 1:
  27.4 42.6 reduce-scatter.1
where the time goes:
time: 112 us
  waiting for transfers between devices  65.7 us (59%)
  between operations  15.5 us (14%)
  blocking collectives  13.3 us (12%)
  other arithmetic  12.7 us (11%)
  matrix products  3.24 us (3%)
  local copies, waits for them, and re-layouts  1.29 us (1%)
    psum x1, waiting for transfers between devices, local(): packed_sum = lax.psum(packed, 'replica')  65.7 us
    pmax x1, blocking collectives, local(): shared = lax.pmax(local_exps, 'replica')  13.3 us
    broadcast_in_dim x1, other arithmetic, local(): second_new[None]  5.26 us
    dot_general x1, matrix products, local(): jnp.einsum('tr,tk->rk', tokens, cot_local, preferred_element_type=jnp.flo...  3.24 us
  transfers between devices with their start and end apart: 2, of which 1 were waited for; matrix products, arithmetic and copies ran while one was open for 5% of the time, Pallas kernels for 0%

commit v1 on v0

v1 whole, which is shorter than its diff:
```python
import functools

import jax
import jax.numpy as jnp
from jax import lax
from jax.experimental import pallas as pl
from jax.experimental.pallas import tpu as pltpu
from jax.sharding import PartitionSpec as P

BETA_ONE = 0.9
BETA_TWO = 0.95
LEARN_RATE = 0.001
DECAY_RATE = 0.1
ADAM_EPSILON = 1e-08
OUTER_RATE = 0.7
OUTER_MOMENTUM = 0.9
MIX_SHARE = 0.5
LEAST_EXPONENT = -10

ANY = pl.BlockSpec(memory_space=pl.ANY)
VMEM = pl.BlockSpec(memory_space=pltpu.VMEM)
LIMIT = 32 * 1024 * 1024
PIECE = 256


def params():
    return pltpu.CompilerParams(vmem_limit_bytes=LIMIT)


def token_product(tokens, cot):
    return lax.dot_general(tokens, cot, (((0,), (0,)), ((), ())), preferred_element_type=jnp.float32)


def load_columns(acts_ref, buf, sems, first):
    copies = []
    for i in range(buf.shape[0]):
        width = buf.shape[2]
        cols = pl.ds(pl.multiple_of(first + i * width, 128), width)
        copies.append(pltpu.make_async_copy(acts_ref.at[:, cols], buf.at[i], sems.at[i]))
        copies[-1].start()
    return copies


def partial_kernel(flip, row, rows, acts_ref, cot_ref, out_ref, buf, sems):
    owner = lax.axis_index("fsdp") ^ flip
    copies = load_columns(acts_ref, buf, sems, owner * rows + row)
    for i, copy in enumerate(copies):
        copy.wait()
        out_ref[i * PIECE:(i + 1) * PIECE, :] = token_product(buf[i], cot_ref[...]).astype(out_ref.dtype)


def partial_sum_kernel(flip, row, rows, acts_ref, cot_ref, other_ref, out_ref, buf, sems):
    owner = lax.axis_index("fsdp") ^ flip
    copies = load_columns(acts_ref, buf, sems, owner * rows + row)
    for i, copy in enumerate(copies):
        copy.wait()
        at = slice(i * PIECE, (i + 1) * PIECE)
        total = token_product(buf[i], cot_ref[...]) + other_ref[at, :].astype(jnp.float32)
        out_ref[at, :] = total.astype(out_ref.dtype)


def partial(acts, cot, flip, row, count, rows, dtype, other=None):
    tokens, width = cot.shape
    kernel = partial_kernel if other is None else partial_sum_kernel
    operands = (acts, cot) + (() if other is None else (other,))
    return pl.pallas_call(
        functools.partial(kernel, flip, row, rows),
        out_shape=jax.ShapeDtypeStruct((count, width), dtype),
        in_specs=[ANY] + [VMEM] * (len(operands) - 1),
        out_specs=VMEM,
        scratch_shapes=[
            pltpu.VMEM((count // PIECE, tokens, PIECE), acts.dtype),
            pltpu.SemaphoreType.DMA((count // PIECE,)),
        ],
        compiler_params=params(),
        cost_estimate=pl.CostEstimate(
            flops=2 * count * tokens * width, bytes_accessed=2 * count * (tokens + width), transcendentals=0
        ),
    )(*operands)


def adam_kernel(own_ref, core_ref, chip_ref, weight_ref, first_ref, second_ref, *rest):
    weight_out, first_out, second_out = rest[-3:]
    gradient = own_ref[...] + core_ref[...].astype(jnp.float32) + chip_ref[...].astype(jnp.float32)
    moment_one = BETA_ONE * first_ref[...].astype(jnp.float32) + (1.0 - BETA_ONE) * gradient
    moment_two = BETA_TWO * second_ref[...].astype(jnp.float32) + (1.0 - BETA_TWO) * gradient * gradient
    weight = weight_ref[...]
    weight_out[...] = weight - LEARN_RATE * (
        moment_one / (jnp.sqrt(moment_two) + ADAM_EPSILON) + DECAY_RATE * weight
    )
    first_out[...] = moment_one.astype(first_out.dtype)
    second_out[...] = moment_two.astype(second_out.dtype)


def adam(own, core, chip, weight, first, second, row, outs):
    block = 128
    rows, width = weight.shape
    count = chip.shape[0]
    here = pl.BlockSpec((block, width), lambda i: (row // block + i, 0))
    operands = [own, core, chip, weight, first, second]
    specs = [here, here, pl.BlockSpec((block, width), lambda i: (i, 0)), here, here, here]
    aliases = {}
    if outs is not None:
        aliases = {len(operands) + i: i for i in range(3)}
        operands += list(outs)
        specs += [ANY] * 3
    return pl.pallas_call(
        adam_kernel,
        out_shape=[jax.ShapeDtypeStruct(a.shape, a.dtype) for a in (weight, first, second)],
        grid=(count // block,),
        in_specs=specs,
        out_specs=[here] * 3,
        input_output_aliases=aliases,
        compiler_params=params(),
        cost_estimate=pl.CostEstimate(
            flops=20 * count * width, bytes_accessed=24 * count * width, transcendentals=2 * count * width
        ),
    )(*operands)


def by_row(exps_ref, at):
    line = exps_ref[pl.ds(at, 1), :]
    return jnp.broadcast_to(line, (128, 128)).T


def code_kernel(parts, group, mant_ref, *refs):
    exps, outs = refs[: len(refs) - parts], refs[len(refs) - parts:]
    where = lax.axis_index("replica") // group
    length = outs[0].shape[0]
    for k in range(parts):
        row = (where ^ k) * length
        for i in range(length // 128):
            line = row // 128 + i
            own = by_row(exps[0], line)
            top = own
            for other in exps[1:]:
                top = jnp.maximum(top, by_row(other, line))
            mant = mant_ref[pl.ds(pl.multiple_of(row + i * 128, 128), 128), :]
            code = mant * 64 + (own - LEAST_EXPONENT) * 8 + (top - LEAST_EXPONENT)
            outs[k][i * 128:(i + 1) * 128, :] = code.astype(outs[k].dtype)


def align_kernel(*refs):
    codes = [r[...].astype(jnp.int32) for r in refs[:-1]]
    top = functools.reduce(jnp.maximum, [c & 7 for c in codes])
    total = sum(jnp.right_shift(c >> 6, top - ((c >> 3) & 7)) for c in codes)
    refs[-1][...] = (total * 8 + top).astype(refs[-1].dtype)


def outer_kernel(group, islands, weight_in, ow_ref, om_ref, *refs):
    parts = len(refs) - 6
    codes = refs[:parts]
    weight_out, outer_out, momentum_out, head, load_sem, store_sems = refs[parts:]
    where = lax.axis_index("replica") // group
    length = codes[0].shape[0]
    width = head.shape[1]
    load = pltpu.make_async_copy(weight_out.at[:, pl.ds(0, width)], head, load_sem)
    load.start()
    load.wait()
    for k in range(parts):
        at = pl.ds(pl.multiple_of((where ^ k) * length, length), length)
        code = codes[k][...].astype(jnp.int32)
        scale = jnp.left_shift(1, code & 7).astype(jnp.float32) * (2.0 ** LEAST_EXPONENT / islands)
        pseudo = (code >> 3).astype(jnp.float32) * scale
        momentum = OUTER_MOMENTUM * om_ref[at, :] + pseudo
        outer = ow_ref[at, :] - OUTER_RATE * (pseudo + OUTER_MOMENTUM * momentum)
        momentum_out[at, :] = momentum
        outer_out[at, :] = outer
        head[at, :] = MIX_SHARE * head[at, :] + (1.0 - MIX_SHARE) * outer
    store = pltpu.make_async_copy(head, weight_out.at[:, pl.ds(0, width)], store_sems)
    store.start()
    store.wait()


def outer_step(weight, outer_weight, outer_momentum, codes, group, islands):
    return pl.pallas_call(
        functools.partial(outer_kernel, group, islands),
        out_shape=[jax.ShapeDtypeStruct(a.shape, a.dtype) for a in (weight, outer_weight, outer_momentum)],
        in_specs=[ANY] + [VMEM] * (2 + len(codes)),
        out_specs=[ANY, VMEM, VMEM],
        input_output_aliases={0: 0},
        scratch_shapes=[
            pltpu.VMEM(outer_weight.shape, jnp.float32),
            pltpu.SemaphoreType.DMA,
            pltpu.SemaphoreType.DMA,
        ],
        compiler_params=params(),
    )(weight, outer_weight, outer_momentum, *codes)


def swap(x, axis, flip):
    size = lax.axis_size(axis)
    return lax.ppermute(x, axis, [(i, i ^ flip) for i in range(size)])


def island_groups(islands):
    inner = 2
    while inner * inner * 4 <= islands:
        inner *= 2
    return islands // inner, inner


def fragment_codes(mant, exps):
    islands = lax.axis_size("replica")
    parts, group = island_groups(islands)
    rows, head = mant.shape
    length = rows // parts
    lines = exps.reshape(rows // 128, 128)
    all_lines = [lines] + [swap(lines, "replica", k) for k in range(1, group)]
    codes = pl.pallas_call(
        functools.partial(code_kernel, parts, group),
        out_shape=[jax.ShapeDtypeStruct((length, head), jnp.int16)] * parts,
        in_specs=[VMEM] * (1 + group),
        out_specs=[VMEM] * parts,
        compiler_params=params(),
    )(mant, *all_lines)
    codes = [codes[0]] + [swap(codes[k], "replica", k * group) for k in range(1, parts)]
    wide = jnp.int16 if islands * 128 * 8 <= 2 ** 15 else jnp.int32
    code = pl.pallas_call(
        align_kernel,
        out_shape=jax.ShapeDtypeStruct((length, head), wide),
        in_specs=[VMEM] * parts,
        out_specs=VMEM,
        compiler_params=params(),
    )(*codes)
    total = code
    for k in range(1, group):
        total = total + (swap(code, "replica", k) & -8)
    return [total] + [swap(total, "replica", k * group) for k in range(1, parts)], group, islands


def local(acts, cotangent, weight, first, second, outer_weight, outer_momentum, mantissas, exponents):
    acts, cot, weight, first, second = acts[0], cotangent[0], weight[0], first[0], second[0]
    rows, width = weight.shape
    bf16 = jnp.bfloat16
    chunks = ((0, rows // 4), (rows // 4, rows // 2), (3 * rows // 4, rows // 4))

    codes, group, islands = fragment_codes(mantissas[0], exponents[0])

    theirs = [partial(acts, cot, 3, row, count, rows, bf16) for row, count in chunks]
    theirs = [swap(part, "fsdp", 1) for part in theirs]
    sends = [
        partial(acts, cot, 2, row, count, rows, bf16, other)
        for (row, count), other in zip(chunks, theirs)
    ]
    arrived = [swap(part, "fsdp", 2) for part in sends]
    core = swap(partial(acts, cot, 1, 0, rows, rows, bf16), "fsdp", 1)
    own = partial(acts, cot, 0, 0, rows, rows, jnp.float32)
    outs = None
    for (row, _), part in zip(chunks, arrived):
        outs = adam(own, core, part, weight, first, second, row, outs)
    weight_new, first_new, second_new = outs
    weight_new, outer_new, momentum_new = outer_step(
        weight_new, outer_weight, outer_momentum, codes, group, islands
    )
    return (weight_new[None], first_new[None], second_new[None], outer_new, momentum_new)


def solution(mesh):
    tall = P("replica", "fsdp", None)
    fragment = P("fsdp", None)
    in_specs = (tall, tall, tall, tall, tall, fragment, fragment, tall, P("replica", "fsdp"))
    out_specs = (tall, tall, tall, fragment, fragment)
    return jax.shard_map(local, mesh=mesh, in_specs=in_specs, out_specs=out_specs, check_vma=False)
```

time: 112 us -> 50.5 us (0.45)
  waiting for transfers between devices: 65.7 us -> 10.7 us
  starting transfers between devices: 0.08 us -> 23.2 us
  between operations: 15.5 us -> 0.82 us
  blocking collectives: 13.3 us -> 0 us
  Pallas kernels: 0 us -> 13 us
  other arithmetic: 12.7 us -> 0.03 us
  matrix products: 3.24 us -> 0 us
  local copies, waits for them, and re-layouts: 1.29 us -> 2.63 us
    psum x1 -> x0, waiting for transfers between devices: 65.7 us -> none  [local(): packed_sum = lax.psum(packed, 'replica')]
    ppermute x0 -> x15, starting transfers between devices: none -> 23.2 us  [swap(): return lax.ppermute(x, axis, [(i, i ^ flip) for i in range(size)])]
    pmax x1 -> x0, blocking collectives: 13.3 us -> none  [local(): shared = lax.pmax(local_exps, 'replica')]
    pallas_call x0 -> x14, Pallas kernels: none -> 13 us  [the longest x3 4.82 us: adam(): pl.pallas_call(adam_kernel, out_shape=[jax.ShapeDtypeStruct(a.shape, a.dt...]
    ppermute x0 -> x15, waiting for transfers between devices: none -> 10.7 us  [swap(): return lax.ppermute(x, axis, [(i, i ^ flip) for i in range(size)])]
    broadcast_in_dim x2 -> x0, other arithmetic: 6.87 us -> none  [the longest x1 5.26 us: local(): second_new[None]]
    dot_general x1 -> x0, matrix products: 3.24 us -> none  [local(): jnp.einsum('tr,tk->rk', tokens, cot_local, preferred_element_type=jnp.flo...]
    sub x2 -> x0, other arithmetic: 2.61 us -> none  [the longest x1 1.92 us: decode_words(): low_part = jnp.remainder(packed_sum + 32768, 65536) - 32768]
  transfers between devices with their start and end apart: 2 -> 15, of which waited for: 1 -> 5; matrix products, arithmetic and copies ran while one was open for 5% -> 0% of each run, Pallas kernels for 0% -> 17%
where the time goes in v1:
time: 50.5 us; the launch traced here: 50.3 us
  starting transfers between devices  23.2 us (46%)
  Pallas kernels  13 us (26%)
  waiting for transfers between devices  10.7 us (21%)
  local copies, waits for them, and re-layouts  2.63 us (5%)
  between operations  0.82 us (2%)
    ppermute x15, starting transfers between devices, swap(): return lax.ppermute(x, axis, [(i, i ^ flip) for i in range(size)])  23.2 us
    ppermute x15, waiting for transfers between devices, swap(): return lax.ppermute(x, axis, [(i, i ^ flip) for i in range(size)])  10.7 us
    pallas_call x3, Pallas kernels, adam(): pl.pallas_call(adam_kernel, out_shape=[jax.ShapeDtypeStruct(a.shape, a.dt...  4.82 us
    pallas_call x8, Pallas kernels, partial(): pl.pallas_call(functools.partial(kernel, flip, row, rows), out_shape=jax....  4.48 us
    pallas_call x1, Pallas kernels, outer_step(): pl.pallas_call(functools.partial(outer_kernel, group, islands), out_shape...  3.16 us
    unnamed x20, local copies, waits for them, and re-layouts  2.63 us
  transfers between devices with their start and end apart: 15, of which 5 were waited for; matrix products, arithmetic and copies ran while one was open for 0% of the time, Pallas kernels for 17%

profile of v1, /device:TPU:0, one launch (start us, length us, event | category | flops | bytes accessed | tf_op | source)
XLA Modules:
  0.0 50.3 jit_solution(17573879474857537920)
XLA Ops:
  0.6 0.0 copy-start
  0.6 1.6 %copy-done = bf16[1,256,4096]{2,1,0:T(8,128)(2,1)S(1)} copy-done((bf16[1,256,4096]{2,1,0:T(8,128)(2,1)S(1)}, bf16[1,256,4096]{2,1,0:T(8,128)(2,1)}, u32[]{:S(2)}) %copy-start) | copy-done | bytes 2097176
  2.2 0.9 %copy-done.3 = bf16[1,256,512]{2,1,0:T(8,128)(2,1)S(1)} copy-done((bf16[1,256,512]{2,1,0:T(8,128)(2,1)S(1)}, bf16[1,256,512]{2,1,0:T(8,128)(2,1)}, u32[]{:S(2)}) %copy-start.3) | copy-done | bytes 262168
  3.2 1.1 %shard_map.129 = bf16[1024,512]{1,0:T(8,128)(2,1)S(1)} custom-call(bf16[256,4096]{1,0:T(8,128)(2,1)S(1)} %bitcast.10, bf16[256,512]{1,0:T(8,128)(2,1)S(1)} %bitcast.21), custom_call_target="tpu_custom_call" | custom-call | flops 268435456 | bytes 1572864 | tf_op jit(solution)/shard_map/pallas_call | solution.py:66
  4.3 0.5 %collective-permute-start = (bf16[1024,512]{1,0:T(8,128)(2,1)S(1)}, bf16[1024,512]{1,0:T(8,128)(2,1)S(1)}, u32[]{:S(2)}, u32[]{:S(2)}) collective-permute-start(bf16[1024,512]{1,0:T(8,128)(2,1)S(1)} %shard_map.129), channel_id=1, source_target_pairs={{0,8},{8,0},{16,24},{24,16},{1,9},{9,1},{17,25},{25,17},{2,10},{10... | collective-permute-start | bytes 3145736 | tf_op jit(solution)/shard_map/ppermute | solution.py:193
  4.8 0.6 %shard_map.132 = bf16[512,512]{1,0:T(8,128)(2,1)S(1)} custom-call(bf16[256,4096]{1,0:T(8,128)(2,1)S(1)} %bitcast.11, bf16[256,512]{1,0:T(8,128)(2,1)S(1)} %bitcast.22), custom_call_target="tpu_custom_call" | custom-call | flops 134217728 | bytes 786432 | tf_op jit(solution)/shard_map/pallas_call | solution.py:66
  5.4 0.0 copy-start.9
  5.4 0.0 copy-start.6
  5.4 0.1 collective-permute-start.3
  5.5 0.3 shard_map.134
  5.8 0.0 copy-start.1
  5.8 0.5 %collective-permute-start.5 = (bf16[256,512]{1,0:T(8,128)(2,1)S(1)}, bf16[256,512]{1,0:T(8,128)(2,1)S(1)}, u32[]{:S(2)}, u32[]{:S(2)}) collective-permute-start(bf16[256,512]{1,0:T(8,128)(2,1)S(1)} %shard_map.134), channel_id=1, source_target_pairs={{0,8},{8,0},{16,24},{24,16},{1,9},{9,1},{17,25},{25,17},{2,10},{10... | collective-permute-start | bytes 786440 | tf_op jit(solution)/shard_map/ppermute | solution.py:193
  6.4 0.3 shard_map.130
  6.6 0.1 collective-permute-start.1
  6.8 2.9 %collective-permute-start.7 = (s32[8,128]{1,0:T(8,128)S(1)}, s32[8,128]{1,0:T(8,128)S(1)}, u32[]{:S(2)}, u32[]{:S(2)}) collective-permute-start(s32[8,128]{1,0:T(8,128)S(1)} %bitcast.36), channel_id=1, source_target_pairs={{0,1},{1,0},{2,3},{3,2},{4,5},{5,4},{6,7},{7,6},{8,9},{9,8},{10,11... | collective-permute-start | bytes 12296 | tf_op jit(solution)/shard_map/ppermute | solution.py:193
  9.7 1.6 %collective-permute-done.7.refs_1_ = s32[8,128]{1,0:T(8,128)S(1)} collective-permute-done((s32[8,128]{1,0:T(8,128)S(1)}, s32[8,128]{1,0:T(8,128)S(1)}, u32[]{:S(2)}, u32[]{:S(2)}) %collective-permute-start.7) | collective-permute-done | bytes 4128 | tf_op jit(solution)/shard_map/ppermute | solution.py:193
  11.3 0.3 shard_map.139
  11.6 4.2 %collective-permute-start.10 = (s16[256,128]{1,0:T(8,128)(2,1)S(1)}, s16[256,128]{1,0:T(8,128)(2,1)S(1)}, u32[]{:S(2)}, u32[]{:S(2)}) collective-permute-start(s16[256,128]{1,0:T(8,128)(2,1)S(1)} %get-tuple-element.31), channel_id=1, source_target_pairs={{0,6},{1,7},{2,4},{3,5},{4,2},{5,3},{6,0},{7,1},{8,14},{9,15},{10,... | collective-permute-start | bytes 196616 | tf_op jit(solution)/shard_map/ppermute | solution.py:193
  15.8 0.0 collective-permute-done.3.other_ref
  15.8 0.6 %shard_map.133 = bf16[512,512]{1,0:T(8,128)(2,1)S(1)} custom-call(bf16[256,4096]{1,0:T(8,128)(2,1)S(1)} %bitcast.14, bf16[256,512]{1,0:T(8,128)(2,1)S(1)} %bitcast.25, bf16[512,512]{1,0:T(8,128)(2,1)S(1)} %collective-permute-done.3.other_ref), custom_call_target="tpu_custom_call" | custom-call | flops 134217728 | bytes 786432 | tf_op jit(solution)/shard_map/pallas_call | solution.py:66
  16.4 1.6 %collective-permute-start.4 = (bf16[512,512]{1,0:T(8,128)(2,1)S(1)}, bf16[512,512]{1,0:T(8,128)(2,1)S(1)}, u32[]{:S(2)}, u32[]{:S(2)}) collective-permute-start(bf16[512,512]{1,0:T(8,128)(2,1)S(1)} %shard_map.133), channel_id=1, source_target_pairs={{0,16},{8,24},{16,0},{24,8},{1,17},{9,25},{17,1},{25,9},{2,18},{10... | collective-permute-start | bytes 1572872 | tf_op jit(solution)/shard_map/ppermute | solution.py:193
  18.0 0.2 collective-permute-done.10.refs_3_
  18.2 0.6 %collective-permute-start.8 = (s16[256,128]{1,0:T(8,128)(2,1)S(1)}, s16[256,128]{1,0:T(8,128)(2,1)S(1)}, u32[]{:S(2)}, u32[]{:S(2)}) collective-permute-start(s16[256,128]{1,0:T(8,128)(2,1)S(1)} %get-tuple-element.29), channel_id=1, source_target_pairs={{0,2},{1,3},{2,0},{3,1},{4,6},{5,7},{6,4},{7,5},{8,10},{9,11},{10,... | collective-permute-start | bytes 196616 | tf_op jit(solution)/shard_map/ppermute | solution.py:193
  18.8 3.7 %collective-permute-done.8.refs_1_ = s16[256,128]{1,0:T(8,128)(2,1)S(1)} collective-permute-done((s16[256,128]{1,0:T(8,128)(2,1)S(1)}, s16[256,128]{1,0:T(8,128)(2,1)S(1)}, u32[]{:S(2)}, u32[]{:S(2)}) %collective-permute-start.8) | collective-permute-done | bytes 65568 | tf_op jit(solution)/shard_map/ppermute | solution.py:193
  22.5 3.4 %collective-permute-start.9 = (s16[256,128]{1,0:T(8,128)(2,1)S(1)}, s16[256,128]{1,0:T(8,128)(2,1)S(1)}, u32[]{:S(2)}, u32[]{:S(2)}) collective-permute-start(s16[256,128]{1,0:T(8,128)(2,1)S(1)} %get-tuple-element.30), channel_id=1, source_target_pairs={{0,4},{1,5},{2,6},{3,7},{4,0},{5,1},{6,2},{7,3},{8,12},{9,13},{10,... | collective-permute-start | bytes 196616 | tf_op jit(solution)/shard_map/ppermute | solution.py:193
  25.9 2.2 %collective-permute-done.9.refs_2_ = s16[256,128]{1,0:T(8,128)(2,1)S(1)} collective-permute-done((s16[256,128]{1,0:T(8,128)(2,1)S(1)}, s16[256,128]{1,0:T(8,128)(2,1)S(1)}, u32[]{:S(2)}, u32[]{:S(2)}) %collective-permute-start.9) | collective-permute-done | bytes 65568 | tf_op jit(solution)/shard_map/ppermute | solution.py:193
  28.1 0.2 shard_map.140
  28.3 1.6 %collective-permute-start.11 = (s16[256,128]{1,0:T(8,128)(2,1)S(1)}, s16[256,128]{1,0:T(8,128)(2,1)S(1)}, u32[]{:S(2)}, u32[]{:S(2)}) collective-permute-start(s16[256,128]{1,0:T(8,128)(2,1)S(1)} %shard_map.140), channel_id=1, source_target_pairs={{0,1},{1,0},{2,3},{3,2},{4,5},{5,4},{6,7},{7,6},{8,9},{9,8},{10,11... | collective-permute-start | bytes 196616 | tf_op jit(solution)/shard_map/ppermute | solution.py:193
  29.8 0.0 collective-permute-done.5.other_ref
  29.8 0.3 shard_map.135
  30.1 1.2 %collective-permute-start.6 = (bf16[256,512]{1,0:T(8,128)(2,1)S(1)}, bf16[256,512]{1,0:T(8,128)(2,1)S(1)}, u32[]{:S(2)}, u32[]{:S(2)}) collective-permute-start(bf16[256,512]{1,0:T(8,128)(2,1)S(1)} %shard_map.135), channel_id=1, source_target_pairs={{0,16},{8,24},{16,0},{24,8},{1,17},{9,25},{17,1},{25,9},{2,18},{10... | collective-permute-start | bytes 786440 | tf_op jit(solution)/shard_map/ppermute | solution.py:193
  31.4 0.0 collective-permute-done.1.other_ref
  31.4 0.3 shard_map.131
  31.6 0.9 %collective-permute-start.2 = (bf16[256,512]{1,0:T(8,128)(2,1)S(1)}, bf16[256,512]{1,0:T(8,128)(2,1)S(1)}, u32[]{:S(2)}, u32[]{:S(2)}) collective-permute-start(bf16[256,512]{1,0:T(8,128)(2,1)S(1)} %shard_map.131), channel_id=1, source_target_pairs={{0,16},{8,24},{16,0},{24,8},{1,17},{9,25},{17,1},{25,9},{2,18},{10... | collective-permute-start | bytes 786440 | tf_op jit(solution)/shard_map/ppermute | solution.py:193
  32.6 0.0 collective-permute-done.11
  32.6 0.0 copy-start.2
  32.6 0.0 copy-start.4
  32.7 0.0 copy-start.5
  32.7 1.8 %collective-permute-start.12 = (s16[256,128]{1,0:T(8,128)(2,1)S(1)}, s16[256,128]{1,0:T(8,128)(2,1)S(1)}, u32[]{:S(2)}, u32[]{:S(2)}) collective-permute-start(s16[256,128]{1,0:T(8,128)(2,1)S(1)} %and_add_fusion.refs_0_), channel_id=1, source_target_pairs={{0,2},{1,3},{2,0},{3,1},{4,6},{5,7},{6,4},{7,5},{8,10},{9,11},{10,... | collective-permute-start | bytes 196616 | tf_op jit(solution)/shard_map/ppermute | solution.py:193
  34.5 2.9 %collective-permute-done.6.chip_ref = bf16[256,512]{1,0:T(8,128)(2,1)S(1)} collective-permute-done((bf16[256,512]{1,0:T(8,128)(2,1)S(1)}, bf16[256,512]{1,0:T(8,128)(2,1)S(1)}, u32[]{:S(2)}, u32[]{:S(2)}) %collective-permute-start.6) | collective-permute-done | bytes 262176 | tf_op jit(solution)/shard_map/ppermute | solution.py:193
  37.4 2.2 %collective-permute-start.13 = (s16[256,128]{1,0:T(8,128)(2,1)S(1)}, s16[256,128]{1,0:T(8,128)(2,1)S(1)}, u32[]{:S(2)}, u32[]{:S(2)}) collective-permute-start(s16[256,128]{1,0:T(8,128)(2,1)S(1)} %and_add_fusion.refs_0_), channel_id=1, source_target_pairs={{0,4},{1,5},{2,6},{3,7},{4,0},{5,1},{6,2},{7,3},{8,12},{9,13},{10,... | collective-permute-start | bytes 196616 | tf_op jit(solution)/shard_map/ppermute | solution.py:193
  39.6 1.5 %collective-permute-start.14 = (s16[256,128]{1,0:T(8,128)(2,1)S(1)}, s16[256,128]{1,0:T(8,128)(2,1)S(1)}, u32[]{:S(2)}, u32[]{:S(2)}) collective-permute-start(s16[256,128]{1,0:T(8,128)(2,1)S(1)} %and_add_fusion.refs_0_), channel_id=1, source_target_pairs={{0,6},{1,7},{2,4},{3,5},{4,2},{5,3},{6,0},{7,1},{8,14},{9,15},{10,... | collective-permute-start | bytes 196616 | tf_op jit(solution)/shard_map/ppermute | solution.py:193
  41.1 1.1 %shard_map.128.own_ref = f32[1024,512]{1,0:T(8,128)S(1)} custom-call(bf16[256,4096]{1,0:T(8,128)(2,1)S(1)} %bitcast.17, bf16[256,512]{1,0:T(8,128)(2,1)S(1)} %bitcast.28), custom_call_target="tpu_custom_call" | custom-call | flops 268435456 | bytes 1572864 | tf_op jit(solution)/shard_map/pallas_call | solution.py:66
  42.2 1.3 %shard_map.136 = (f32[1024,512]{1,0:T(8,128)}, bf16[1024,512]{1,0:T(8,128)(2,1)}, bf16[1024,512]{1,0:T(8,128)(2,1)}) custom-call(f32[1024,512]{1,0:T(8,128)S(1)} %shard_map.128.own_ref, bf16[1024,512]{1,0:T(8,128)(2,1)S(1)} %collective-permute-done.core_ref, bf16[256,512]{1,0:T(8,128)(2,1)S(1)} %collective-permute-done.6.chip_ref, f32[1024,512]{1,0:T(8,128)S(1)} %bitcast.18, ...), custom_call_target="tpu_custom_call" | custom-call | flops 2621440 | bytes 3145728 | tf_op jit(solution)/shard_map/pallas_call | solution.py:107
  43.5 2.2 %shard_map.137 = (f32[1024,512]{1,0:T(8,128)}, bf16[1024,512]{1,0:T(8,128)(2,1)}, bf16[1024,512]{1,0:T(8,128)(2,1)}) custom-call(f32[1024,512]{1,0:T(8,128)S(1)} %shard_map.128.own_ref, bf16[1024,512]{1,0:T(8,128)(2,1)S(1)} %collective-permute-done.core_ref, ...), custom_call_target="tpu_custom_call", output_to_operand_aliasing={{0}: (6, {}), {1}: (7, {}), {2}: (8, {})} | custom-call | flops 5242880 | bytes 6291456 | tf_op jit(solution)/shard_map/pallas_call | solution.py:107
  45.8 1.3 %shard_map.138 = (f32[1024,512]{1,0:T(8,128)}, bf16[1024,512]{1,0:T(8,128)(2,1)}, bf16[1024,512]{1,0:T(8,128)(2,1)}) custom-call(f32[1024,512]{1,0:T(8,128)S(1)} %shard_map.128.own_ref, bf16[1024,512]{1,0:T(8,128)(2,1)S(1)} %collective-permute-done.core_ref, ...), custom_call_target="tpu_custom_call", output_to_operand_aliasing={{0}: (6, {}), {1}: (7, {}), {2}: (8, {})} | custom-call | flops 2621440 | bytes 3145728 | tf_op jit(solution)/shard_map/pallas_call | solution.py:107
  47.1 0.0 copy-done.8
  47.1 3.2 %shard_map.141 = (f32[1024,512]{1,0:T(8,128)}, f32[1024,128]{1,0:T(8,128)}, f32[1024,128]{1,0:T(8,128)}) custom-call(f32[1024,512]{1,0:T(8,128)} %get-tuple-element.27.weight_in, f32[1024,128]{1,0:T(8,128)S(1)} %copy-done.7, f32[1024,128]{1,0:T(8,128)S(1)} %copy-done.8, s16[256,128]{1,0:T(8,128)(2,1)S(1)} %and_add_fusion.refs_0_, ...), custom_call_target="tpu_custom_call", output_to_operand_aliasing={{0}: (0, {})} | custom-call | tf_op jit(solution)/shard_map/pallas_call | solution.py:176
  (17 shorter events, 0.1 us)
Async XLA Ops:
  0.6 1.6 %copy-start = (bf16[1,256,4096]{2,1,0:T(8,128)(2,1)S(1)}, bf16[1,256,4096]{2,1,0:T(8,128)(2,1)}, u32[]{:S(2)}) copy-start(bf16[1,256,4096]{2,1,0:T(8,128)(2,1)} %param.9) | copy-start | bytes 6291460
  2.2 0.9 %copy-start.3 = (bf16[1,256,512]{2,1,0:T(8,128)(2,1)S(1)}, bf16[1,256,512]{2,1,0:T(8,128)(2,1)}, u32[]{:S(2)}) copy-start(bf16[1,256,512]{2,1,0:T(8,128)(2,1)} %param.10) | copy-start | bytes 786436
  4.3 35.3 %collective-permute-start = (bf16[1024,512]{1,0:T(8,128)(2,1)S(1)}, bf16[1024,512]{1,0:T(8,128)(2,1)S(1)}, u32[]{:S(2)}, u32[]{:S(2)}) collective-permute-start(bf16[1024,512]{1,0:T(8,128)(2,1)S(1)} %shard_map.129), channel_id=1, source_target_pairs={{0,8},{8,0},{16,24},{24,16},{1,9},{9,1},{17,25},{25,17},{2,10},{10... | collective-permute-start | bytes 3145736 | tf_op jit(solution)/shard_map/ppermute | solution.py:193
  5.4 1.4 %copy-start.9 = (s32[1,1024]{1,0:T(1,128)S(1)}, s32[1,1024]{1,0:T(1,128)}, u32[]{:S(2)}) copy-start(s32[1,1024]{1,0:T(1,128)} %param.17) | copy-start | bytes 12292
  5.4 5.9 %copy-start.6 = (s32[1,1024,128]{2,1,0:T(8,128)S(1)}, s32[1,1024,128]{2,1,0:T(8,128)}, u32[]{:S(2)}) copy-start(s32[1,1024,128]{2,1,0:T(8,128)} %param.16) | copy-start | bytes 1572868
  5.4 10.4 %collective-permute-start.3 = (bf16[512,512]{1,0:T(8,128)(2,1)S(1)}, bf16[512,512]{1,0:T(8,128)(2,1)S(1)}, u32[]{:S(2)}, u32[]{:S(2)}) collective-permute-start(bf16[512,512]{1,0:T(8,128)(2,1)S(1)} %shard_map.132), channel_id=1, source_target_pairs={{0,8},{8,0},{16,24},{24,16},{1,9},{9,1},{17,25},{25,17},{2,10},{10... | collective-permute-start | bytes 1572872 | tf_op jit(solution)/shard_map/ppermute | solution.py:193
  5.8 10.0 %copy-start.1 = (bf16[1,256,4096]{2,1,0:T(8,128)(2,1)S(1)}, bf16[1,256,4096]{2,1,0:T(8,128)(2,1)}, u32[]{:S(2)}) copy-start(bf16[1,256,4096]{2,1,0:T(8,128)(2,1)} %param.9) | copy-start | bytes 6291460
  5.8 24.0 %collective-permute-start.5 = (bf16[256,512]{1,0:T(8,128)(2,1)S(1)}, bf16[256,512]{1,0:T(8,128)(2,1)S(1)}, u32[]{:S(2)}, u32[]{:S(2)}) collective-permute-start(bf16[256,512]{1,0:T(8,128)(2,1)S(1)} %shard_map.134), channel_id=1, source_target_pairs={{0,8},{8,0},{16,24},{24,16},{1,9},{9,1},{17,25},{25,17},{2,10},{10... | collective-permute-start | bytes 786440 | tf_op jit(solution)/shard_map/ppermute | solution.py:193
  6.6 24.7 %collective-permute-start.1 = (bf16[256,512]{1,0:T(8,128)(2,1)S(1)}, bf16[256,512]{1,0:T(8,128)(2,1)S(1)}, u32[]{:S(2)}, u32[]{:S(2)}) collective-permute-start(bf16[256,512]{1,0:T(8,128)(2,1)S(1)} %shard_map.130), channel_id=1, source_target_pairs={{0,8},{8,0},{16,24},{24,16},{1,9},{9,1},{17,25},{25,17},{2,10},{10... | collective-permute-start | bytes 786440 | tf_op jit(solution)/shard_map/ppermute | solution.py:193
  6.8 4.5 %collective-permute-start.7 = (s32[8,128]{1,0:T(8,128)S(1)}, s32[8,128]{1,0:T(8,128)S(1)}, u32[]{:S(2)}, u32[]{:S(2)}) collective-permute-start(s32[8,128]{1,0:T(8,128)S(1)} %bitcast.36), channel_id=1, source_target_pairs={{0,1},{1,0},{2,3},{3,2},{4,5},{5,4},{6,7},{7,6},{8,9},{9,8},{10,11... | collective-permute-start | bytes 12296 | tf_op jit(solution)/shard_map/ppermute | solution.py:193
  11.6 6.6 %collective-permute-start.10 = (s16[256,128]{1,0:T(8,128)(2,1)S(1)}, s16[256,128]{1,0:T(8,128)(2,1)S(1)}, u32[]{:S(2)}, u32[]{:S(2)}) collective-permute-start(s16[256,128]{1,0:T(8,128)(2,1)S(1)} %get-tuple-element.31), channel_id=1, source_target_pairs={{0,6},{1,7},{2,4},{3,5},{4,2},{5,3},{6,0},{7,1},{8,14},{9,15},{10,... | collective-permute-start | bytes 196616 | tf_op jit(solution)/shard_map/ppermute | solution.py:193
  16.4 27.1 %collective-permute-start.4 = (bf16[512,512]{1,0:T(8,128)(2,1)S(1)}, bf16[512,512]{1,0:T(8,128)(2,1)S(1)}, u32[]{:S(2)}, u32[]{:S(2)}) collective-permute-start(bf16[512,512]{1,0:T(8,128)(2,1)S(1)} %shard_map.133), channel_id=1, source_target_pairs={{0,16},{8,24},{16,0},{24,8},{1,17},{9,25},{17,1},{25,9},{2,18},{10... | collective-permute-start | bytes 1572872 | tf_op jit(solution)/shard_map/ppermute | solution.py:193
  18.2 4.3 %collective-permute-start.8 = (s16[256,128]{1,0:T(8,128)(2,1)S(1)}, s16[256,128]{1,0:T(8,128)(2,1)S(1)}, u32[]{:S(2)}, u32[]{:S(2)}) collective-permute-start(s16[256,128]{1,0:T(8,128)(2,1)S(1)} %get-tuple-element.29), channel_id=1, source_target_pairs={{0,2},{1,3},{2,0},{3,1},{4,6},{5,7},{6,4},{7,5},{8,10},{9,11},{10,... | collective-permute-start | bytes 196616 | tf_op jit(solution)/shard_map/ppermute | solution.py:193
  22.5 5.6 %collective-permute-start.9 = (s16[256,128]{1,0:T(8,128)(2,1)S(1)}, s16[256,128]{1,0:T(8,128)(2,1)S(1)}, u32[]{:S(2)}, u32[]{:S(2)}) collective-permute-start(s16[256,128]{1,0:T(8,128)(2,1)S(1)} %get-tuple-element.30), channel_id=1, source_target_pairs={{0,4},{1,5},{2,6},{3,7},{4,0},{5,1},{6,2},{7,3},{8,12},{9,13},{10,... | collective-permute-start | bytes 196616 | tf_op jit(solution)/shard_map/ppermute | solution.py:193
  28.3 4.3 %collective-permute-start.11 = (s16[256,128]{1,0:T(8,128)(2,1)S(1)}, s16[256,128]{1,0:T(8,128)(2,1)S(1)}, u32[]{:S(2)}, u32[]{:S(2)}) collective-permute-start(s16[256,128]{1,0:T(8,128)(2,1)S(1)} %shard_map.140), channel_id=1, source_target_pairs={{0,1},{1,0},{2,3},{3,2},{4,5},{5,4},{6,7},{7,6},{8,9},{9,8},{10,11... | collective-permute-start | bytes 196616 | tf_op jit(solution)/shard_map/ppermute | solution.py:193
  30.1 7.3 %collective-permute-start.6 = (bf16[256,512]{1,0:T(8,128)(2,1)S(1)}, bf16[256,512]{1,0:T(8,128)(2,1)S(1)}, u32[]{:S(2)}, u32[]{:S(2)}) collective-permute-start(bf16[256,512]{1,0:T(8,128)(2,1)S(1)} %shard_map.135), channel_id=1, source_target_pairs={{0,16},{8,24},{16,0},{24,8},{1,17},{9,25},{17,1},{25,9},{2,18},{10... | collective-permute-start | bytes 786440 | tf_op jit(solution)/shard_map/ppermute | solution.py:193
  31.6 14.1 %collective-permute-start.2 = (bf16[256,512]{1,0:T(8,128)(2,1)S(1)}, bf16[256,512]{1,0:T(8,128)(2,1)S(1)}, u32[]{:S(2)}, u32[]{:S(2)}) collective-permute-start(bf16[256,512]{1,0:T(8,128)(2,1)S(1)} %shard_map.131), channel_id=1, source_target_pairs={{0,16},{8,24},{16,0},{24,8},{1,17},{9,25},{17,1},{25,9},{2,18},{10... | collective-permute-start | bytes 786440 | tf_op jit(solution)/shard_map/ppermute | solution.py:193
  32.6 9.6 %copy-start.2 = (f32[1,1024,512]{2,1,0:T(8,128)S(1)}, f32[1,1024,512]{2,1,0:T(8,128)}, u32[]{:S(2)}) copy-start(f32[1,1024,512]{2,1,0:T(8,128)} %param.11) | copy-start | bytes 6291460
  32.6 9.6 %copy-start.4 = (bf16[1,1024,512]{2,1,0:T(8,128)(2,1)S(1)}, bf16[1,1024,512]{2,1,0:T(8,128)(2,1)}, u32[]{:S(2)}) copy-start(bf16[1,1024,512]{2,1,0:T(8,128)(2,1)} %param.12) | copy-start | bytes 3145732
  32.7 9.6 %copy-start.5 = (bf16[1,1024,512]{2,1,0:T(8,128)(2,1)S(1)}, bf16[1,1024,512]{2,1,0:T(8,128)(2,1)}, u32[]{:S(2)}) copy-start(bf16[1,1024,512]{2,1,0:T(8,128)(2,1)} %param.13) | copy-start | bytes 3145732
  32.7 14.4 %collective-permute-start.12 = (s16[256,128]{1,0:T(8,128)(2,1)S(1)}, s16[256,128]{1,0:T(8,128)(2,1)S(1)}, u32[]{:S(2)}, u32[]{:S(2)}) collective-permute-start(s16[256,128]{1,0:T(8,128)(2,1)S(1)} %and_add_fusion.refs_0_), channel_id=1, source_target_pairs={{0,2},{1,3},{2,0},{3,1},{4,6},{5,7},{6,4},{7,5},{8,10},{9,11},{10,... | collective-permute-start | bytes 196616 | tf_op jit(solution)/shard_map/ppermute | solution.py:193
  37.4 9.7 %collective-permute-start.13 = (s16[256,128]{1,0:T(8,128)(2,1)S(1)}, s16[256,128]{1,0:T(8,128)(2,1)S(1)}, u32[]{:S(2)}, u32[]{:S(2)}) collective-permute-start(s16[256,128]{1,0:T(8,128)(2,1)S(1)} %and_add_fusion.refs_0_), channel_id=1, source_target_pairs={{0,4},{1,5},{2,6},{3,7},{4,0},{5,1},{6,2},{7,3},{8,12},{9,13},{10,... | collective-permute-start | bytes 196616 | tf_op jit(solution)/shard_map/ppermute | solution.py:193
  39.6 7.5 %collective-permute-start.14 = (s16[256,128]{1,0:T(8,128)(2,1)S(1)}, s16[256,128]{1,0:T(8,128)(2,1)S(1)}, u32[]{:S(2)}, u32[]{:S(2)}) collective-permute-start(s16[256,128]{1,0:T(8,128)(2,1)S(1)} %and_add_fusion.refs_0_), channel_id=1, source_target_pairs={{0,6},{1,7},{2,4},{3,5},{4,2},{5,3},{6,0},{7,1},{8,14},{9,15},{10,... | collective-permute-start | bytes 196616 | tf_op jit(solution)/shard_map/ppermute | solution.py:193
  45.8 1.3 %copy-start.7 = (f32[1024,128]{1,0:T(8,128)S(1)}, f32[1024,128]{1,0:T(8,128)}, u32[]{:S(2)}) copy-start(f32[1024,128]{1,0:T(8,128)} %ow_ref.1) | copy-start | bytes 1572868
  45.8 1.4 %copy-start.8 = (f32[1024,128]{1,0:T(8,128)S(1)}, f32[1024,128]{1,0:T(8,128)}, u32[]{:S(2)}) copy-start(f32[1024,128]{1,0:T(8,128)} %om_ref.1) | copy-start | bytes 1572868

commit v2 on v1

v2 whole, which is shorter than its diff:
```python
import functools

import jax
import jax.numpy as jnp
from jax import lax
from jax.experimental import pallas as pl
from jax.experimental.pallas import tpu as pltpu
from jax.sharding import PartitionSpec as P

BETA_ONE = 0.9
BETA_TWO = 0.95
LEARN_RATE = 0.001
DECAY_RATE = 0.1
ADAM_EPSILON = 1e-08
OUTER_RATE = 0.7
OUTER_MOMENTUM = 0.9
MIX_SHARE = 0.5
LEAST_EXPONENT = -10

ANY = pl.BlockSpec(memory_space=pl.ANY)
VMEM = pl.BlockSpec(memory_space=pltpu.VMEM)
COST = (0, 0, 0, 5)
OPT = (1, 0)
UNITS = (2, 3, 3)
FILL = (0, 20, 20, 20, 20, 20)
LIMIT = 32 * 1024 * 1024


def params():
    return pltpu.CompilerParams(vmem_limit_bytes=LIMIT)


def cost(us):
    return pl.CostEstimate(flops=int(us * 1.15e9), bytes_accessed=0, transcendentals=0)


def token_product(tokens, cot):
    return lax.dot_general(tokens, cot, (((0,), (0,)), ((), ())), preferred_element_type=jnp.float32)


def product_kernel(flip, row, rows, summed, acts_ref, cot_ref, *refs):
    out_ref, buf, cot, sems, cot_sem = refs[-5:]
    owner = lax.axis_index("fsdp") ^ flip
    cot_copy = pltpu.make_async_copy(cot_ref, cot, cot_sem)
    cot_copy.start()
    pieces, _, width = buf.shape
    copies = []
    for i in range(pieces):
        cols = pl.ds(pl.multiple_of(owner * rows + row + i * width, 128), width)
        copies.append(pltpu.make_async_copy(acts_ref.at[:, cols], buf.at[i], sems.at[i]))
        copies[-1].start()
    cot_copy.wait()
    for i, copy in enumerate(copies):
        copy.wait()
        at = slice(i * width, (i + 1) * width)
        total = token_product(buf[i], cot[...])
        if summed:
            total = total + refs[0][at, :].astype(jnp.float32)
        out_ref[at, :] = total.astype(out_ref.dtype)


def product(acts, cot, flip, row, count, rows, dtype, other=None, after=(), us=0):
    tokens, width = cot.shape
    piece = next(p for p in (256, 384, 128, count) if count % p == 0)
    shares = () if other is None else (other,)
    return pl.pallas_call(
        functools.partial(product_kernel, flip, row, rows, len(shares)),
        out_shape=jax.ShapeDtypeStruct((count, width), dtype),
        in_specs=[ANY, ANY] + [VMEM] * len(shares) + [ANY] * len(after),
        out_specs=VMEM,
        scratch_shapes=[
            pltpu.VMEM((count // piece, tokens, piece), acts.dtype),
            pltpu.VMEM(cot.shape, cot.dtype),
            pltpu.SemaphoreType.DMA((count // piece,)),
            pltpu.SemaphoreType.DMA,
        ],
        compiler_params=params(),
        cost_estimate=cost(us),
    )(acts, cot, *shares, *after)


def adam_step(gradient, weight, first, second):
    moment_one = BETA_ONE * first.astype(jnp.float32) + (1.0 - BETA_ONE) * gradient
    moment_two = BETA_TWO * second.astype(jnp.float32) + (1.0 - BETA_TWO) * gradient * gradient
    updated = weight - LEARN_RATE * (
        moment_one / (jnp.sqrt(moment_two) + ADAM_EPSILON) + DECAY_RATE * weight
    )
    return updated, moment_one.astype(first.dtype), moment_two.astype(second.dtype)


def adam_kernel(own_ref, core_ref, chip_ref, weight_ref, first_ref, second_ref, *rest):
    weight_out, first_out, second_out, head_out = rest[-4:]
    gradient = own_ref[...] + core_ref[...].astype(jnp.float32) + chip_ref[...].astype(jnp.float32)
    weight_out[...], first_out[...], second_out[...] = adam_step(
        gradient, weight_ref[...], first_ref[...], second_ref[...]
    )
    head_out[...] = weight_out[:, : head_out.shape[1]]


def adam(own, core, chip, weight, first, second, row, head, outs=(), us=0, after=()):
    block = 128
    rows, width = weight.shape
    count = chip.shape[0]
    here = pl.BlockSpec((block, width), lambda i: (row // block + i, 0))
    operands = [own, core, chip, weight, first, second]
    specs = [here, here, pl.BlockSpec((block, width), lambda i: (i, 0)), here, here, here]
    aliases = {len(operands) + i: i for i in range(len(outs))}
    operands += list(outs)
    operands += list(after)
    specs += [ANY] * (len(outs) + len(after))
    return pl.pallas_call(
        adam_kernel,
        out_shape=[jax.ShapeDtypeStruct(a.shape, a.dtype) for a in (weight, first, second)]
        + [jax.ShapeDtypeStruct((count, head), weight.dtype)],
        grid=(count // block,),
        in_specs=specs,
        out_specs=[here] * 3 + [pl.BlockSpec((block, head), lambda i: (i, 0))],
        input_output_aliases=aliases,
        compiler_params=params(),
        cost_estimate=cost(us),
    )(*operands)


def by_row(exps_ref, at):
    line = exps_ref[pl.ds(at, 1), :]
    return jnp.broadcast_to(line, (128, 128)).T


def code_kernel(parts, group, mant_ref, *refs):
    exps, outs = refs[:group], refs[len(refs) - parts:]
    where = lax.axis_index("replica") // group
    length = outs[0].shape[0]
    for k in range(parts):
        row = (where ^ k) * length
        for i in range(length // 128):
            line = row // 128 + i
            own = by_row(exps[0], line)
            top = own
            for other in exps[1:]:
                top = jnp.maximum(top, by_row(other, line))
            mant = mant_ref[pl.ds(pl.multiple_of(row + i * 128, 128), 128), :]
            code = mant * 64 + (own - LEAST_EXPONENT) * 8 + (top - LEAST_EXPONENT)
            outs[k][i * 128:(i + 1) * 128, :] = code.astype(outs[k].dtype)


def align_kernel(parts, *refs):
    codes = [r[...].astype(jnp.int32) for r in refs[:parts]]
    top = functools.reduce(jnp.maximum, [c & 7 for c in codes])
    total = sum(jnp.right_shift(c >> 6, top - ((c >> 3) & 7)) for c in codes)
    refs[-1][...] = (total * 8 + top).astype(refs[-1].dtype)


def finish_kernel(group, islands, parts, early, *refs):
    weight_ref, first_ref, second_ref, own_ref, core_ref, chip_ref, ow_ref, om_ref = refs[:8]
    codes, heads = refs[8:8 + parts], refs[8 + parts:8 + parts + early]
    weight_out, first_out, second_out, outer_out, momentum_out = refs[8 + parts + early + 3:-7]
    weight_new, first_new, second_new, outer, momentum, mixed, sems = refs[-7:]
    where = lax.axis_index("replica") // group
    length = codes[0].shape[0]
    count = chip_ref.shape[0]
    last = weight_ref.shape[0] - count
    width = mixed.shape[1]
    stores = []

    def store(source, target):
        stores.append(pltpu.make_async_copy(source, target, sems.at[len(stores)]))
        stores[-1].start()

    for k in range(parts):
        at = pl.ds(pl.multiple_of((where ^ k) * length, length), length)
        code = codes[k][...].astype(jnp.int32)
        scale = jnp.left_shift(1, code & 7).astype(jnp.float32) * (2.0 ** LEAST_EXPONENT / islands)
        pseudo = (code >> 3).astype(jnp.float32) * scale
        moved = OUTER_MOMENTUM * om_ref[at, :] + pseudo
        momentum[at, :] = moved
        outer[at, :] = ow_ref[at, :] - OUTER_RATE * (pseudo + OUTER_MOMENTUM * moved)
    store(momentum, momentum_out)
    store(outer, outer_out)
    row = 0
    for head in heads:
        at = slice(row, row + head.shape[0])
        mixed[at, :] = MIX_SHARE * head[...] + (1.0 - MIX_SHARE) * outer[at, :]
        row += head.shape[0]
    store(mixed, weight_out.at[pl.ds(0, last), pl.ds(0, width)])
    block = 128
    for i in range(count // block):
        here, there = slice(i * block, (i + 1) * block), slice(last + i * block, last + (i + 1) * block)
        gradient = own_ref[there, :] + core_ref[there, :].astype(jnp.float32) + chip_ref[here, :].astype(jnp.float32)
        updated, first_new[here, :], second_new[here, :] = adam_step(
            gradient, weight_ref[there, :], first_ref[there, :], second_ref[there, :]
        )
        weight_new[here, width:] = updated[:, width:]
        weight_new[here, :width] = MIX_SHARE * updated[:, :width] + (1.0 - MIX_SHARE) * outer[there, :]
        for new, out in ((weight_new, weight_out), (first_new, first_out), (second_new, second_out)):
            store(new.at[pl.ds(i * block, block)], out.at[pl.ds(last + i * block, block)])
    for copy in stores:
        copy.wait()


def finish(weight, first, second, own, core, chip, outer_weight, outer_momentum, codes, heads, outs, group, islands):
    parts, early = len(codes), len(heads)
    count, width = chip.shape
    fragment = outer_weight.shape
    operands = [weight, first, second, own, core, chip, outer_weight, outer_momentum, *codes, *heads]
    return pl.pallas_call(
        functools.partial(finish_kernel, group, islands, parts, early),
        out_shape=[
            jax.ShapeDtypeStruct(a.shape, a.dtype) for a in (weight, first, second, outer_weight, outer_momentum)
        ],
        in_specs=[VMEM] * len(operands) + [ANY] * 3,
        out_specs=[ANY] * 5,
        input_output_aliases={len(operands) + i: i for i in range(3)},
        scratch_shapes=[
            pltpu.VMEM((count, width), weight.dtype),
            pltpu.VMEM((count, width), first.dtype),
            pltpu.VMEM((count, width), second.dtype),
            pltpu.VMEM(fragment, jnp.float32),
            pltpu.VMEM(fragment, jnp.float32),
            pltpu.VMEM((weight.shape[0] - count, fragment[1]), jnp.float32),
            pltpu.SemaphoreType.DMA((3 + 3 * (count // 128),)),
        ],
        compiler_params=params(),
        cost_estimate=cost(0),
    )(*operands, *outs)


def swap(x, axis, flip):
    size = lax.axis_size(axis)
    return lax.ppermute(x, axis, [(i, i ^ flip) for i in range(size)])


def island_groups(islands):
    inner = 2
    while inner * inner * 4 <= islands:
        inner *= 2
    return islands // inner, inner


def copy_kernel(x_ref, out_ref):
    out_ref[...] = x_ref[...]


def held(x, us):
    return pl.pallas_call(
        copy_kernel,
        out_shape=jax.ShapeDtypeStruct(x.shape, x.dtype),
        in_specs=[VMEM],
        out_specs=VMEM,
        compiler_params=params(),
        cost_estimate=cost(us),
    )(x)


def join_kernel(others, code_ref, *refs):
    total = code_ref[...]
    for other in refs[:others]:
        total += other[...] & -8
    refs[-1][...] = total


def local(acts, cotangent, weight, first, second, outer_weight, outer_momentum, mantissas, exponents):
    acts, cot, weight, first, second = acts[0], cotangent[0], weight[0], first[0], second[0]
    mant, lines = mantissas[0], exponents[0].reshape(-1, 128)
    rows, width = weight.shape
    bf16 = jnp.bfloat16
    islands = lax.axis_size("replica")
    parts, group = island_groups(islands)
    length, head = rows // parts, mant.shape[1]
    unit = rows // 8
    chunks, row = [], 0
    for units in UNITS:
        chunks.append((row * unit, units * unit))
        row += units

    lines = held(lines, COST[3])
    all_lines = [lines] + [swap(lines, "replica", k) for k in range(1, group)]
    first_part = all_lines[1:] if OPT[1] else all_lines[:1]
    theirs = []
    for row, count in chunks:
        theirs.append(
            product(acts, cot, 3, row, count, rows, bf16, after=theirs[-1:] or first_part, us=FILL[3] if theirs else 0)
        )
    shares = [swap(part, "fsdp", 1) for part in theirs]
    sends = []
    for n, ((row, count), other) in enumerate(zip(chunks, shares)):
        sends.append(
            product(acts, cot, 2, row, count, rows, bf16, other, after=sends[-1:] or theirs[-1:], us=FILL[5 if n > 1 else 4])
        )
    arrived = [swap(part, "fsdp", 2) for part in sends]

    codes = pl.pallas_call(
        functools.partial(code_kernel, parts, group),
        out_shape=[jax.ShapeDtypeStruct((length, head), jnp.int16)] * parts,
        in_specs=[VMEM] * (1 + group) + [ANY],
        out_specs=[VMEM] * parts,
        compiler_params=params(),
        cost_estimate=cost(COST[0]),
    )(mant, *all_lines, sends[OPT[0]])
    core = product(acts, cot, 1, 0, rows, rows, bf16, after=codes[:1], us=FILL[0])
    codes = [codes[0]] + [swap(codes[k], "replica", k * group) for k in range(1, parts)]
    wide = jnp.int16 if islands * 128 * 8 <= 2 ** 15 else jnp.int32
    code = pl.pallas_call(
        functools.partial(align_kernel, parts),
        out_shape=jax.ShapeDtypeStruct((length, head), wide),
        in_specs=[VMEM] * parts + [ANY] * 2,
        out_specs=VMEM,
        compiler_params=params(),
        cost_estimate=cost(0),
    )(*codes, core, sends[-1])
    core = swap(core, "fsdp", 1)
    others = [swap(code, "replica", k) for k in range(1, group)]
    own = product(acts, cot, 0, 0, rows, rows, jnp.float32, after=(code,), us=FILL[1])
    *outs, part_head = adam(own, core, arrived[0], weight, first, second, 0, head, us=FILL[1], after=(code,))
    heads = [part_head]
    total = pl.pallas_call(
        functools.partial(join_kernel, group - 1),
        out_shape=jax.ShapeDtypeStruct((length, head), wide),
        in_specs=[VMEM] * group + [ANY],
        out_specs=VMEM,
        compiler_params=params(),
        cost_estimate=cost(0),
    )(code, *others, part_head)
    codes = [total] + [swap(total, "replica", k * group) for k in range(1, parts)]
    for (row, _), part in zip(chunks[1:-1], arrived[1:]):
        *outs, part_head = adam(own, core, part, weight, first, second, row, head, outs, us=FILL[2])
        heads.append(part_head)
    weight_new, first_new, second_new, outer_new, momentum_new = finish(
        weight, first, second, own, core, arrived[-1], outer_weight, outer_momentum, codes, heads, outs, group, islands
    )
    return (weight_new[None], first_new[None], second_new[None], outer_new, momentum_new)


def solution(mesh):
    tall = P("replica", "fsdp", None)
    fragment = P("fsdp", None)
    in_specs = (tall, tall, tall, tall, tall, fragment, fragment, tall, P("replica", "fsdp"))
    out_specs = (tall, tall, tall, fragment, fragment)
    return jax.shard_map(local, mesh=mesh, in_specs=in_specs, out_specs=out_specs, check_vma=False)
```

time: 50.5 us -> 35 us (0.69)
  waiting for transfers between devices: 10.7 us -> 4.64 us
  starting transfers between devices: 23.2 us -> 17.9 us
  Pallas kernels: 13 us -> 10.7 us
  local copies, waits for them, and re-layouts: 2.63 us -> 0.72 us
    ppermute x15, waiting for transfers between devices: 10.7 us -> 4.64 us  [swap(): return lax.ppermute(x, axis, [(i, i ^ flip) for i in range(size)])]
    ppermute x15, starting transfers between devices: 23.2 us -> 17.9 us  [swap(): return lax.ppermute(x, axis, [(i, i ^ flip) for i in range(size)])]
    unnamed x20 -> x18, local copies, waits for them, and re-layouts: 2.63 us -> 0.72 us
    pallas_call x3 -> x2, Pallas kernels: 4.82 us -> 3.55 us  [adam(): pl.pallas_call(adam_kernel, out_shape=[jax.ShapeDtypeStruct(a.shape, a.dt...]
    pallas_call x11 -> x13, Pallas kernels: 8.16 us -> 7.12 us  [the longest x8 4.37 us: product(): pl.pallas_call(functools.partial(product_kernel, flip, row, rows, len(sha...]
  transfers between devices with their start and end apart: 15 -> 15, of which waited for: 5 -> 6; matrix products, arithmetic and copies ran while one was open for 0% -> 0% of each run, Pallas kernels for 17% -> 24%
where the time goes in v2:
time: 35 us; the launch traced here: 34.8 us
  starting transfers between devices  17.9 us (51%)
  Pallas kernels  10.7 us (31%)
  waiting for transfers between devices  4.64 us (13%)
  between operations  0.82 us (2%)
  local copies, waits for them, and re-layouts  0.72 us (2%)
    ppermute x15, starting transfers between devices, swap(): return lax.ppermute(x, axis, [(i, i ^ flip) for i in range(size)])  17.9 us
    ppermute x15, waiting for transfers between devices, swap(): return lax.ppermute(x, axis, [(i, i ^ flip) for i in range(size)])  4.64 us
    pallas_call x8, Pallas kernels, product(): pl.pallas_call(functools.partial(product_kernel, flip, row, rows, len(sha...  4.37 us
    pallas_call x2, Pallas kernels, adam(): pl.pallas_call(adam_kernel, out_shape=[jax.ShapeDtypeStruct(a.shape, a.dt...  3.55 us
    pallas_call x1, Pallas kernels, finish(): pl.pallas_call(functools.partial(finish_kernel, group, islands, parts, ea...  2.21 us
    unnamed x18, local copies, waits for them, and re-layouts  0.72 us
  transfers between devices with their start and end apart: 15, of which 6 were waited for; matrix products, arithmetic and copies ran while one was open for 0% of the time, Pallas kernels for 24%

profile of v2, /device:TPU:0, one launch (start us, length us, event | category | flops | bytes accessed | tf_op | source)
XLA Modules:
  0.0 34.8 jit_solution(14238341466302911697)
XLA Ops:
  0.6 0.7 %copy-done.8 = s32[1,1024]{1,0:T(1,128)S(1)} copy-done((s32[1,1024]{1,0:T(1,128)S(1)}, s32[1,1024]{1,0:T(1,128)}, u32[]{:S(2)}) %copy-start.8) | copy-done | bytes 4120
  1.3 2.9 %collective-permute-start = (s32[8,128]{1,0:T(8,128)S(1)}, s32[8,128]{1,0:T(8,128)S(1)}, u32[]{:S(2)}, u32[]{:S(2)}) collective-permute-start(s32[8,128]{1,0:T(8,128)S(1)} %shard_map.128.refs_0_), channel_id=1, source_target_pairs={{0,1},{1,0},{2,3},{3,2},{4,5},{5,4},{6,7},{7,6},{8,9},{9,8},{10,11... | collective-permute-start | bytes 12296 | tf_op jit(solution)/shard_map/ppermute | solution.py:229
  4.3 0.3 shard_map.129.refs_0_
  4.6 0.1 collective-permute-start.2
  4.7 0.4 %shard_map.130.refs_0_ = bf16[384,512]{1,0:T(8,128)(2,1)S(1)} custom-call(bf16[256,4096]{1,0:T(8,128)(2,1)S(1)} %bitcast.11, bf16[256,512]{1,0:T(8,128)(2,1)S(1)} %bitcast.28, bf16[256,512]{1,0:T(8,128)(2,1)S(1)} %shard_map.129.refs_0_), custom_call_target="tpu_custom_call" | custom-call | flops 23000000512 | tf_op jit(solution)/shard_map/pallas_call | solution.py:66
  5.0 0.5 %collective-permute-start.1 = (bf16[384,512]{1,0:T(8,128)(2,1)S(1)}, bf16[384,512]{1,0:T(8,128)(2,1)S(1)}, u32[]{:S(2)}, u32[]{:S(2)}) collective-permute-start(bf16[384,512]{1,0:T(8,128)(2,1)S(1)} %shard_map.130.refs_0_), channel_id=1, source_target_pairs={{0,8},{8,0},{16,24},{24,16},{1,9},{9,1},{17,25},{25,17},{2,10},{10... | collective-permute-start | bytes 1179656 | tf_op jit(solution)/shard_map/ppermute | solution.py:229
  5.6 0.4 %shard_map.131.refs_1_ = bf16[384,512]{1,0:T(8,128)(2,1)S(1)} custom-call(bf16[256,4096]{1,0:T(8,128)(2,1)S(1)} %bitcast.12, bf16[256,512]{1,0:T(8,128)(2,1)S(1)} %bitcast.29, bf16[384,512]{1,0:T(8,128)(2,1)S(1)} %shard_map.130.refs_0_), custom_call_target="tpu_custom_call" | custom-call | flops 23000000512 | tf_op jit(solution)/shard_map/pallas_call | solution.py:66
  6.0 0.1 collective-permute-start.6
  6.0 0.1 collective-permute-done.2.refs_0_
  6.2 0.3 shard_map.132.refs_1_
  6.5 0.0 copy-start.7
  6.5 1.7 %collective-permute-start.10 = (bf16[256,512]{1,0:T(8,128)(2,1)S(1)}, bf16[256,512]{1,0:T(8,128)(2,1)S(1)}, u32[]{:S(2)}, u32[]{:S(2)}) collective-permute-start(bf16[256,512]{1,0:T(8,128)(2,1)S(1)} %shard_map.132.refs_1_), channel_id=1, source_target_pairs={{0,16},{8,24},{16,0},{24,8},{1,17},{9,25},{17,1},{25,9},{2,18},{10... | collective-permute-start | bytes 786440 | tf_op jit(solution)/shard_map/ppermute | solution.py:229
  8.2 0.0 collective-permute-done.1.refs_0_
  8.2 0.4 %shard_map.133.refs_2_.refs_1_ = bf16[384,512]{1,0:T(8,128)(2,1)S(1)} custom-call(bf16[256,4096]{1,0:T(8,128)(2,1)S(1)} %bitcast.14, bf16[256,512]{1,0:T(8,128)(2,1)S(1)} %bitcast.31, bf16[384,512]{1,0:T(8,128)(2,1)S(1)} %collective-permute-done.1.refs_0_, bf16[256,512]{1,0:T(8,128)(2,1)S(1)} %shard_map.132.refs_1_), custom_call_target="tpu_custom_call" | custom-call | flops 23000000512 | tf_op jit(solution)/shard_map/pallas_call | solution.py:66
  8.6 0.5 %collective-permute-start.14 = (bf16[384,512]{1,0:T(8,128)(2,1)S(1)}, bf16[384,512]{1,0:T(8,128)(2,1)S(1)}, u32[]{:S(2)}, u32[]{:S(2)}) collective-permute-start(bf16[384,512]{1,0:T(8,128)(2,1)S(1)} %shard_map.133.refs_2_.refs_1_), channel_id=1, source_target_pairs={{0,16},{8,24},{16,0},{24,8},{1,17},{9,25},{17,1},{25,9},{2,18},{10... | collective-permute-start | bytes 1179656 | tf_op jit(solution)/shard_map/ppermute | solution.py:229
  9.0 0.0 collective-permute-done.refs_1_
  9.1 0.3 shard_map.134
  9.4 1.7 %collective-permute-start.3 = (s16[256,128]{1,0:T(8,128)(2,1)S(1)}, s16[256,128]{1,0:T(8,128)(2,1)S(1)}, u32[]{:S(2)}, u32[]{:S(2)}) collective-permute-start(s16[256,128]{1,0:T(8,128)(2,1)S(1)} %get-tuple-element.23), channel_id=1, source_target_pairs={{0,2},{1,3},{2,0},{3,1},{4,6},{5,7},{6,4},{7,5},{8,10},{9,11},{10,... | collective-permute-start | bytes 196616 | tf_op jit(solution)/shard_map/ppermute | solution.py:229
  11.1 2.6 %collective-permute-start.4 = (s16[256,128]{1,0:T(8,128)(2,1)S(1)}, s16[256,128]{1,0:T(8,128)(2,1)S(1)}, u32[]{:S(2)}, u32[]{:S(2)}) collective-permute-start(s16[256,128]{1,0:T(8,128)(2,1)S(1)} %get-tuple-element.24), channel_id=1, source_target_pairs={{0,4},{1,5},{2,6},{3,7},{4,0},{5,1},{6,2},{7,3},{8,12},{9,13},{10,... | collective-permute-start | bytes 196616 | tf_op jit(solution)/shard_map/ppermute | solution.py:229
  13.7 0.0 collective-permute-done.6.refs_0_
  13.7 0.1 collective-permute-start.5
  13.9 0.4 %shard_map.136.refs_5_ = bf16[384,512]{1,0:T(8,128)(2,1)S(1)} custom-call(bf16[256,4096]{1,0:T(8,128)(2,1)S(1)} %bitcast.15, bf16[256,512]{1,0:T(8,128)(2,1)S(1)} %bitcast.32, bf16[384,512]{1,0:T(8,128)(2,1)S(1)} %collective-permute-done.6.refs_0_, bf16[384,512]{1,0:T(8,128)(2,1)S(1)} %shard_map.133.refs_2_.refs_1_), custom_call_target="tpu_custom_call" | custom-call | flops 23000000512 | tf_op jit(solution)/shard_map/pallas_call | solution.py:66
  14.2 1.2 %shard_map.135.refs_4_ = bf16[1024,512]{1,0:T(8,128)(2,1)S(1)} custom-call(bf16[256,4096]{1,0:T(8,128)(2,1)S(1)} %bitcast.16, bf16[256,512]{1,0:T(8,128)(2,1)S(1)} %bitcast.33, s16[256,128]{1,0:T(8,128)(2,1)S(1)} %get-tuple-element.22.refs_0_), custom_call_target="tpu_custom_call" | custom-call | tf_op jit(solution)/shard_map/pallas_call | solution.py:66
  15.4 0.0 collective-permute-done.3.refs_1_
  15.4 1.7 %collective-permute-start.8 = (bf16[384,512]{1,0:T(8,128)(2,1)S(1)}, bf16[384,512]{1,0:T(8,128)(2,1)S(1)}, u32[]{:S(2)}, u32[]{:S(2)}) collective-permute-start(bf16[384,512]{1,0:T(8,128)(2,1)S(1)} %shard_map.136.refs_5_), channel_id=1, source_target_pairs={{0,16},{8,24},{16,0},{24,8},{1,17},{9,25},{17,1},{25,9},{2,18},{10... | collective-permute-start | bytes 1179656 | tf_op jit(solution)/shard_map/ppermute | solution.py:229
  17.1 1.5 %collective-permute-done.4.refs_2_ = s16[256,128]{1,0:T(8,128)(2,1)S(1)} collective-permute-done((s16[256,128]{1,0:T(8,128)(2,1)S(1)}, s16[256,128]{1,0:T(8,128)(2,1)S(1)}, u32[]{:S(2)}, u32[]{:S(2)}) %collective-permute-start.4) | collective-permute-done | bytes 65568 | tf_op jit(solution)/shard_map/ppermute | solution.py:229
  18.5 0.0 collective-permute-start.7
  18.5 1.3 %collective-permute-done.5.refs_3_ = s16[256,128]{1,0:T(8,128)(2,1)S(1)} collective-permute-done((s16[256,128]{1,0:T(8,128)(2,1)S(1)}, s16[256,128]{1,0:T(8,128)(2,1)S(1)}, u32[]{:S(2)}, u32[]{:S(2)}) %collective-permute-start.5) | collective-permute-done | bytes 65568 | tf_op jit(solution)/shard_map/ppermute | solution.py:229
  19.9 0.2 shard_map.137.refs_0_.rest_0_.code_ref
  20.1 0.0 copy-start.1
  20.1 0.0 copy-start.2
  20.1 0.0 copy-start.3
  20.1 1.6 %collective-permute-start.9 = (s16[256,128]{1,0:T(8,128)(2,1)S(1)}, s16[256,128]{1,0:T(8,128)(2,1)S(1)}, u32[]{:S(2)}, u32[]{:S(2)}) collective-permute-start(s16[256,128]{1,0:T(8,128)(2,1)S(1)} %shard_map.137.refs_0_.rest_0_.code_ref), channel_id=1, source_target_pairs={{0,1},{1,0},{2,3},{3,2},{4,5},{5,4},{6,7},{7,6},{8,9},{9,8},{10,11... | collective-permute-start | bytes 196616 | tf_op jit(solution)/shard_map/ppermute | solution.py:229
  21.7 1.1 %shard_map.138.own_ref.refs_3_ = f32[1024,512]{1,0:T(8,128)S(1)} custom-call(bf16[256,4096]{1,0:T(8,128)(2,1)S(1)} %bitcast.17, bf16[256,512]{1,0:T(8,128)(2,1)S(1)} %bitcast.34, s16[256,128]{1,0:T(8,128)(2,1)S(1)} %shard_map.137.refs_0_.rest_0_.code_ref), custom_call_target="tpu_custom_call" | custom-call | flops 23000000512 | tf_op jit(solution)/shard_map/pallas_call | solution.py:66
  22.8 0.0 collective-permute-done.10.chip_ref
  22.8 0.0 collective-permute-done.7.core_ref.refs_4_
  22.9 1.4 %shard_map.139 = (f32[1024,512]{1,0:T(8,128)}, bf16[1024,512]{1,0:T(8,128)(2,1)}, bf16[1024,512]{1,0:T(8,128)(2,1)}, f32[256,128]{1,0:T(8,128)S(1)}) custom-call(f32[1024,512]{1,0:T(8,128)S(1)} %shard_map.138.own_ref.refs_3_, bf16[1024,512]{1,0:T(8,128)(2,1)S(1)} %collective-permute-done.7.core_ref.refs_4_, ...), custom_call_target="tpu_custom_call" | custom-call | flops 23000000512 | tf_op jit(solution)/shard_map/pallas_call | solution.py:111
  24.3 0.1 collective-permute-done.9.refs_0_
  24.5 2.1 %collective-permute-start.13 = (s16[256,128]{1,0:T(8,128)(2,1)S(1)}, s16[256,128]{1,0:T(8,128)(2,1)S(1)}, u32[]{:S(2)}, u32[]{:S(2)}) collective-permute-start(s16[256,128]{1,0:T(8,128)(2,1)S(1)} %shard_map.140.refs_8_), channel_id=1, source_target_pairs={{0,6},{1,7},{2,4},{3,5},{4,2},{5,3},{6,0},{7,1},{8,14},{9,15},{10,... | collective-permute-start | bytes 196616 | tf_op jit(solution)/shard_map/ppermute | solution.py:229
  26.6 0.1 collective-permute-start.12
  26.6 2.3 %collective-permute-start.11 = (s16[256,128]{1,0:T(8,128)(2,1)S(1)}, s16[256,128]{1,0:T(8,128)(2,1)S(1)}, u32[]{:S(2)}, u32[]{:S(2)}) collective-permute-start(s16[256,128]{1,0:T(8,128)(2,1)S(1)} %shard_map.140.refs_8_), channel_id=1, source_target_pairs={{0,2},{1,3},{2,0},{3,1},{4,6},{5,7},{6,4},{7,5},{8,10},{9,11},{10,... | collective-permute-start | bytes 196616 | tf_op jit(solution)/shard_map/ppermute | solution.py:229
  28.9 0.0 collective-permute-done.14.chip_ref
  28.9 2.1 %shard_map.141 = (f32[1024,512]{1,0:T(8,128)}, bf16[1024,512]{1,0:T(8,128)(2,1)}, bf16[1024,512]{1,0:T(8,128)(2,1)}, f32[384,128]{1,0:T(8,128)S(1)}) custom-call(f32[1024,512]{1,0:T(8,128)S(1)} %shard_map.138.own_ref.refs_3_, ...), custom_call_target="tpu_custom_call", output_to_operand_aliasing={{0}: (6, {}), {1}: (7, {}), {2}: (8, {})} | custom-call | flops 23000000512 | tf_op jit(solution)/shard_map/pallas_call | solution.py:111
  31.1 0.9 %collective-permute-done.8.refs_5_ = bf16[384,512]{1,0:T(8,128)(2,1)S(1)} collective-permute-done((bf16[384,512]{1,0:T(8,128)(2,1)S(1)}, bf16[384,512]{1,0:T(8,128)(2,1)S(1)}, u32[]{:S(2)}, u32[]{:S(2)}) %collective-permute-start.8) | collective-permute-done | bytes 393248 | tf_op jit(solution)/shard_map/ppermute | solution.py:229
  32.0 0.0 collective-permute-done.13.refs_11_
  32.0 0.6 %collective-permute-done.12.refs_10_ = s16[256,128]{1,0:T(8,128)(2,1)S(1)} collective-permute-done((s16[256,128]{1,0:T(8,128)(2,1)S(1)}, s16[256,128]{1,0:T(8,128)(2,1)S(1)}, u32[]{:S(2)}, u32[]{:S(2)}) %collective-permute-start.12) | collective-permute-done | bytes 65568 | tf_op jit(solution)/shard_map/ppermute | solution.py:229
  32.6 0.0 collective-permute-done.11.refs_9_
  32.6 2.2 %shard_map.142 = (f32[1024,512]{1,0:T(8,128)}, bf16[1024,512]{1,0:T(8,128)(2,1)}, bf16[1024,512]{1,0:T(8,128)(2,1)}, f32[1024,128]{1,0:T(8,128)}, f32[1024,128]{1,0:T(8,128)}) custom-call(f32[1024,512]{1,0:T(8,128)S(1)} %bitcast.20, bf16[1024,512]{1,0:T(8,128)(2,1)S(1)} %bitcast.23, ...), custom_call_target="tpu_custom_call", output_to_operand_aliasing={{0}: (14, {}), {1}: (15, {}), {2}: (16, {})} | custom-call | tf_op jit(solution)/shard_map/pallas_call | solution.py:205
  (15 shorter events, 0.1 us)
Async XLA Ops:
  0.6 0.7 %copy-start.8 = (s32[1,1024]{1,0:T(1,128)S(1)}, s32[1,1024]{1,0:T(1,128)}, u32[]{:S(2)}) copy-start(s32[1,1024]{1,0:T(1,128)} %param.17) | copy-start | bytes 12292
  1.3 2.9 %copy-start = (bf16[1,256,4096]{2,1,0:T(8,128)(2,1)S(1)}, bf16[1,256,4096]{2,1,0:T(8,128)(2,1)}, u32[]{:S(2)}) copy-start(bf16[1,256,4096]{2,1,0:T(8,128)(2,1)} %param.9) | copy-start | bytes 6291460
  1.3 2.9 %copy-start.4 = (bf16[1,256,512]{2,1,0:T(8,128)(2,1)S(1)}, bf16[1,256,512]{2,1,0:T(8,128)(2,1)}, u32[]{:S(2)}) copy-start(bf16[1,256,512]{2,1,0:T(8,128)(2,1)} %param.10) | copy-start | bytes 786436
  1.3 7.7 %collective-permute-start = (s32[8,128]{1,0:T(8,128)S(1)}, s32[8,128]{1,0:T(8,128)S(1)}, u32[]{:S(2)}, u32[]{:S(2)}) collective-permute-start(s32[8,128]{1,0:T(8,128)S(1)} %shard_map.128.refs_0_), channel_id=1, source_target_pairs={{0,1},{1,0},{2,3},{3,2},{4,5},{5,4},{6,7},{7,6},{8,9},{9,8},{10,11... | collective-permute-start | bytes 12296 | tf_op jit(solution)/shard_map/ppermute | solution.py:229
  4.6 1.6 %collective-permute-start.2 = (bf16[256,512]{1,0:T(8,128)(2,1)S(1)}, bf16[256,512]{1,0:T(8,128)(2,1)S(1)}, u32[]{:S(2)}, u32[]{:S(2)}) collective-permute-start(bf16[256,512]{1,0:T(8,128)(2,1)S(1)} %shard_map.129.refs_0_), channel_id=1, source_target_pairs={{0,8},{8,0},{16,24},{24,16},{1,9},{9,1},{17,25},{25,17},{2,10},{10... | collective-permute-start | bytes 786440 | tf_op jit(solution)/shard_map/ppermute | solution.py:229
  5.0 3.2 %collective-permute-start.1 = (bf16[384,512]{1,0:T(8,128)(2,1)S(1)}, bf16[384,512]{1,0:T(8,128)(2,1)S(1)}, u32[]{:S(2)}, u32[]{:S(2)}) collective-permute-start(bf16[384,512]{1,0:T(8,128)(2,1)S(1)} %shard_map.130.refs_0_), channel_id=1, source_target_pairs={{0,8},{8,0},{16,24},{24,16},{1,9},{9,1},{17,25},{25,17},{2,10},{10... | collective-permute-start | bytes 1179656 | tf_op jit(solution)/shard_map/ppermute | solution.py:229
  6.0 7.8 %collective-permute-start.6 = (bf16[384,512]{1,0:T(8,128)(2,1)S(1)}, bf16[384,512]{1,0:T(8,128)(2,1)S(1)}, u32[]{:S(2)}, u32[]{:S(2)}) collective-permute-start(bf16[384,512]{1,0:T(8,128)(2,1)S(1)} %shard_map.131.refs_1_), channel_id=1, source_target_pairs={{0,8},{8,0},{16,24},{24,16},{1,9},{9,1},{17,25},{25,17},{2,10},{10... | collective-permute-start | bytes 1179656 | tf_op jit(solution)/shard_map/ppermute | solution.py:229
  6.5 2.5 %copy-start.7 = (s32[1,1024,128]{2,1,0:T(8,128)S(1)}, s32[1,1024,128]{2,1,0:T(8,128)}, u32[]{:S(2)}) copy-start(s32[1,1024,128]{2,1,0:T(8,128)} %param.16) | copy-start | bytes 1572868
  6.5 16.3 %collective-permute-start.10 = (bf16[256,512]{1,0:T(8,128)(2,1)S(1)}, bf16[256,512]{1,0:T(8,128)(2,1)S(1)}, u32[]{:S(2)}, u32[]{:S(2)}) collective-permute-start(bf16[256,512]{1,0:T(8,128)(2,1)S(1)} %shard_map.132.refs_1_), channel_id=1, source_target_pairs={{0,16},{8,24},{16,0},{24,8},{1,17},{9,25},{17,1},{25,9},{2,18},{10... | collective-permute-start | bytes 786440 | tf_op jit(solution)/shard_map/ppermute | solution.py:229
  8.6 20.4 %collective-permute-start.14 = (bf16[384,512]{1,0:T(8,128)(2,1)S(1)}, bf16[384,512]{1,0:T(8,128)(2,1)S(1)}, u32[]{:S(2)}, u32[]{:S(2)}) collective-permute-start(bf16[384,512]{1,0:T(8,128)(2,1)S(1)} %shard_map.133.refs_2_.refs_1_), channel_id=1, source_target_pairs={{0,16},{8,24},{16,0},{24,8},{1,17},{9,25},{17,1},{25,9},{2,18},{10... | collective-permute-start | bytes 1179656 | tf_op jit(solution)/shard_map/ppermute | solution.py:229
  9.4 6.0 %collective-permute-start.3 = (s16[256,128]{1,0:T(8,128)(2,1)S(1)}, s16[256,128]{1,0:T(8,128)(2,1)S(1)}, u32[]{:S(2)}, u32[]{:S(2)}) collective-permute-start(s16[256,128]{1,0:T(8,128)(2,1)S(1)} %get-tuple-element.23), channel_id=1, source_target_pairs={{0,2},{1,3},{2,0},{3,1},{4,6},{5,7},{6,4},{7,5},{8,10},{9,11},{10,... | collective-permute-start | bytes 196616 | tf_op jit(solution)/shard_map/ppermute | solution.py:229
  11.1 7.4 %collective-permute-start.4 = (s16[256,128]{1,0:T(8,128)(2,1)S(1)}, s16[256,128]{1,0:T(8,128)(2,1)S(1)}, u32[]{:S(2)}, u32[]{:S(2)}) collective-permute-start(s16[256,128]{1,0:T(8,128)(2,1)S(1)} %get-tuple-element.24), channel_id=1, source_target_pairs={{0,4},{1,5},{2,6},{3,7},{4,0},{5,1},{6,2},{7,3},{8,12},{9,13},{10,... | collective-permute-start | bytes 196616 | tf_op jit(solution)/shard_map/ppermute | solution.py:229
  13.7 6.2 %collective-permute-start.5 = (s16[256,128]{1,0:T(8,128)(2,1)S(1)}, s16[256,128]{1,0:T(8,128)(2,1)S(1)}, u32[]{:S(2)}, u32[]{:S(2)}) collective-permute-start(s16[256,128]{1,0:T(8,128)(2,1)S(1)} %get-tuple-element.25), channel_id=1, source_target_pairs={{0,6},{1,7},{2,4},{3,5},{4,2},{5,3},{6,0},{7,1},{8,14},{9,15},{10,... | collective-permute-start | bytes 196616 | tf_op jit(solution)/shard_map/ppermute | solution.py:229
  15.4 16.6 %collective-permute-start.8 = (bf16[384,512]{1,0:T(8,128)(2,1)S(1)}, bf16[384,512]{1,0:T(8,128)(2,1)S(1)}, u32[]{:S(2)}, u32[]{:S(2)}) collective-permute-start(bf16[384,512]{1,0:T(8,128)(2,1)S(1)} %shard_map.136.refs_5_), channel_id=1, source_target_pairs={{0,16},{8,24},{16,0},{24,8},{1,17},{9,25},{17,1},{25,9},{2,18},{10... | collective-permute-start | bytes 1179656 | tf_op jit(solution)/shard_map/ppermute | solution.py:229
  18.5 4.3 %collective-permute-start.7 = (bf16[1024,512]{1,0:T(8,128)(2,1)S(1)}, bf16[1024,512]{1,0:T(8,128)(2,1)S(1)}, u32[]{:S(2)}, u32[]{:S(2)}) collective-permute-start(bf16[1024,512]{1,0:T(8,128)(2,1)S(1)} %shard_map.135.refs_4_), channel_id=1, source_target_pairs={{0,8},{8,0},{16,24},{24,16},{1,9},{9,1},{17,25},{25,17},{2,10},{10... | collective-permute-start | bytes 3145736 | tf_op jit(solution)/shard_map/ppermute | solution.py:229
  20.1 2.8 %copy-start.1 = (f32[1,1024,512]{2,1,0:T(8,128)S(1)}, f32[1,1024,512]{2,1,0:T(8,128)}, u32[]{:S(2)}) copy-start(f32[1,1024,512]{2,1,0:T(8,128)} %param.11) | copy-start | bytes 6291460
  20.1 2.8 %copy-start.2 = (bf16[1,1024,512]{2,1,0:T(8,128)(2,1)S(1)}, bf16[1,1024,512]{2,1,0:T(8,128)(2,1)}, u32[]{:S(2)}) copy-start(bf16[1,1024,512]{2,1,0:T(8,128)(2,1)} %param.12) | copy-start | bytes 3145732
  20.1 2.8 %copy-start.3 = (bf16[1,1024,512]{2,1,0:T(8,128)(2,1)S(1)}, bf16[1,1024,512]{2,1,0:T(8,128)(2,1)}, u32[]{:S(2)}) copy-start(bf16[1,1024,512]{2,1,0:T(8,128)(2,1)} %param.13) | copy-start | bytes 3145732
  20.1 4.3 %collective-permute-start.9 = (s16[256,128]{1,0:T(8,128)(2,1)S(1)}, s16[256,128]{1,0:T(8,128)(2,1)S(1)}, u32[]{:S(2)}, u32[]{:S(2)}) collective-permute-start(s16[256,128]{1,0:T(8,128)(2,1)S(1)} %shard_map.137.refs_0_.rest_0_.code_ref), channel_id=1, source_target_pairs={{0,1},{1,0},{2,3},{3,2},{4,5},{5,4},{6,7},{7,6},{8,9},{9,8},{10,11... | collective-permute-start | bytes 196616 | tf_op jit(solution)/shard_map/ppermute | solution.py:229
  24.5 7.5 %collective-permute-start.13 = (s16[256,128]{1,0:T(8,128)(2,1)S(1)}, s16[256,128]{1,0:T(8,128)(2,1)S(1)}, u32[]{:S(2)}, u32[]{:S(2)}) collective-permute-start(s16[256,128]{1,0:T(8,128)(2,1)S(1)} %shard_map.140.refs_8_), channel_id=1, source_target_pairs={{0,6},{1,7},{2,4},{3,5},{4,2},{5,3},{6,0},{7,1},{8,14},{9,15},{10,... | collective-permute-start | bytes 196616 | tf_op jit(solution)/shard_map/ppermute | solution.py:229
  26.6 6.0 %collective-permute-start.12 = (s16[256,128]{1,0:T(8,128)(2,1)S(1)}, s16[256,128]{1,0:T(8,128)(2,1)S(1)}, u32[]{:S(2)}, u32[]{:S(2)}) collective-permute-start(s16[256,128]{1,0:T(8,128)(2,1)S(1)} %shard_map.140.refs_8_), channel_id=1, source_target_pairs={{0,4},{1,5},{2,6},{3,7},{4,0},{5,1},{6,2},{7,3},{8,12},{9,13},{10,... | collective-permute-start | bytes 196616 | tf_op jit(solution)/shard_map/ppermute | solution.py:229
  26.6 6.0 %collective-permute-start.11 = (s16[256,128]{1,0:T(8,128)(2,1)S(1)}, s16[256,128]{1,0:T(8,128)(2,1)S(1)}, u32[]{:S(2)}, u32[]{:S(2)}) collective-permute-start(s16[256,128]{1,0:T(8,128)(2,1)S(1)} %shard_map.140.refs_8_), channel_id=1, source_target_pairs={{0,2},{1,3},{2,0},{3,1},{4,6},{5,7},{6,4},{7,5},{8,10},{9,11},{10,... | collective-permute-start | bytes 196616 | tf_op jit(solution)/shard_map/ppermute | solution.py:229
  28.9 3.7 %copy-start.5 = (f32[1024,128]{1,0:T(8,128)S(1)}, f32[1024,128]{1,0:T(8,128)}, u32[]{:S(2)}) copy-start(f32[1024,128]{1,0:T(8,128)} %refs_6_.1) | copy-start | bytes 1572868
  28.9 3.7 %copy-start.6 = (f32[1024,128]{1,0:T(8,128)S(1)}, f32[1024,128]{1,0:T(8,128)}, u32[]{:S(2)}) copy-start(f32[1024,128]{1,0:T(8,128)} %refs_7_.1) | copy-start | bytes 1572868

commit v3 on v2

--- a/solution.py
+++ b/solution.py
@@ -19,9 +19,9 @@
 
 ANY = pl.BlockSpec(memory_space=pl.ANY)
 VMEM = pl.BlockSpec(memory_space=pltpu.VMEM)
-COST = (0, 0, 0, 5)
-OPT = (1, 0)
-UNITS = (2, 3, 3)
+COST = (0, 0, 0, 1)
+OPT = (1, 0, 0)
+UNITS = (2, 4, 2)
 FILL = (0, 20, 20, 20, 20, 20)
 LIMIT = 32 * 1024 * 1024
 
@@ -38,40 +38,42 @@
     return lax.dot_general(tokens, cot, (((0,), (0,)), ((), ())), preferred_element_type=jnp.float32)
 
 
-def product_kernel(flip, row, rows, summed, acts_ref, cot_ref, *refs):
+def pieces(count):
+    size = next(s for s in (256, 384, 128) if count % s == 0)
+    return [(at, size) for at in range(0, count, size)]
+
+
+def product_kernel(flip, row, rows, summed, skip, acts_ref, cot_ref, *refs):
     out_ref, buf, cot, sems, cot_sem = refs[-5:]
     owner = lax.axis_index("fsdp") ^ flip
     cot_copy = pltpu.make_async_copy(cot_ref, cot, cot_sem)
     cot_copy.start()
-    pieces, _, width = buf.shape
     copies = []
-    for i in range(pieces):
-        cols = pl.ds(pl.multiple_of(owner * rows + row + i * width, 128), width)
-        copies.append(pltpu.make_async_copy(acts_ref.at[:, cols], buf.at[i], sems.at[i]))
+    for n, (at, size) in enumerate(pieces(out_ref.shape[0])):
+        cols = pl.ds(pl.multiple_of(owner * rows + row + at, 128), size)
+        copies.append(pltpu.make_async_copy(acts_ref.at[:, cols], buf.at[:, pl.ds(at, size)], sems.at[n]))
         copies[-1].start()
     cot_copy.wait()
-    for i, copy in enumerate(copies):
+    for copy, (at, size) in zip(copies, pieces(out_ref.shape[0])):
         copy.wait()
-        at = slice(i * width, (i + 1) * width)
-        total = token_product(buf[i], cot[...])
+        total = token_product(buf[:, at:at + size], cot[...])
         if summed:
-            total = total + refs[0][at, :].astype(jnp.float32)
-        out_ref[at, :] = total.astype(out_ref.dtype)
-
-
-def product(acts, cot, flip, row, count, rows, dtype, other=None, after=(), us=0):
+            total = total + refs[0][skip + at:skip + at + size, :].astype(jnp.float32)
+        out_ref[at:at + size, :] = total.astype(out_ref.dtype)
+
+
+def product(acts, cot, flip, row, count, rows, dtype, other=None, skip=0, after=(), us=0):
     tokens, width = cot.shape
-    piece = next(p for p in (256, 384, 128, count) if count % p == 0)
     shares = () if other is None else (other,)
     return pl.pallas_call(
-        functools.partial(product_kernel, flip, row, rows, len(shares)),
+        functools.partial(product_kernel, flip, row, rows, len(shares), skip),
         out_shape=jax.ShapeDtypeStruct((count, width), dtype),
         in_specs=[ANY, ANY] + [VMEM] * len(shares) + [ANY] * len(after),
         out_specs=VMEM,
         scratch_shapes=[
-            pltpu.VMEM((count // piece, tokens, piece), acts.dtype),
+            pltpu.VMEM((tokens, count), acts.dtype),
             pltpu.VMEM(cot.shape, cot.dtype),
-            pltpu.SemaphoreType.DMA((count // piece,)),
+            pltpu.SemaphoreType.DMA((len(pieces(count)),)),
             pltpu.SemaphoreType.DMA,
         ],
         compiler_params=params(),
@@ -174,8 +176,8 @@
         moved = OUTER_MOMENTUM * om_ref[at, :] + pseudo
         momentum[at, :] = moved
         outer[at, :] = ow_ref[at, :] - OUTER_RATE * (pseudo + OUTER_MOMENTUM * moved)
-    store(momentum, momentum_out)
-    store(outer, outer_out)
+        store(momentum.at[at], momentum_out.at[at])
+        store(outer.at[at], outer_out.at[at])
     row = 0
     for head in heads:
         at = slice(row, row + head.shape[0])
@@ -217,7 +219,7 @@
             pltpu.VMEM(fragment, jnp.float32),
             pltpu.VMEM(fragment, jnp.float32),
             pltpu.VMEM((weight.shape[0] - count, fragment[1]), jnp.float32),
-            pltpu.SemaphoreType.DMA((3 + 3 * (count // 128),)),
+            pltpu.SemaphoreType.DMA((2 * parts + 1 + 3 * (count // 128),)),
         ],
         compiler_params=params(),
         cost_estimate=cost(0),
@@ -236,19 +238,12 @@
     return islands // inner, inner
 
 
-def copy_kernel(x_ref, out_ref):
-    out_ref[...] = x_ref[...]
-
-
-def held(x, us):
-    return pl.pallas_call(
-        copy_kernel,
-        out_shape=jax.ShapeDtypeStruct(x.shape, x.dtype),
-        in_specs=[VMEM],
-        out_specs=VMEM,
-        compiler_params=params(),
-        cost_estimate=cost(us),
-    )(x)
+def add_kernel(mine_ref, other_ref, out_ref):
+    out_ref[...] = (mine_ref[...] + other_ref[...].astype(jnp.float32)).astype(out_ref.dtype)
+
+
+def start_kernel(out_ref):
+    out_ref[...] = jnp.zeros_like(out_ref)
 
 
 def join_kernel(others, code_ref, *refs):
@@ -272,22 +267,32 @@
         chunks.append((row * unit, units * unit))
         row += units
 
-    lines = held(lines, COST[3])
+    ready = pl.pallas_call(
+        start_kernel,
+        out_shape=jax.ShapeDtypeStruct((8, 128), jnp.int32),
+        out_specs=VMEM,
+        compiler_params=params(),
+        cost_estimate=cost(COST[3]),
+    )()
     all_lines = [lines] + [swap(lines, "replica", k) for k in range(1, group)]
-    first_part = all_lines[1:] if OPT[1] else all_lines[:1]
-    theirs = []
-    for row, count in chunks:
-        theirs.append(
-            product(acts, cot, 3, row, count, rows, bf16, after=theirs[-1:] or first_part, us=FILL[3] if theirs else 0)
-        )
-    shares = [swap(part, "fsdp", 1) for part in theirs]
-    sends = []
-    for n, ((row, count), other) in enumerate(zip(chunks, shares)):
-        sends.append(
-            product(acts, cot, 2, row, count, rows, bf16, other, after=sends[-1:] or theirs[-1:], us=FILL[5 if n > 1 else 4])
-        )
-    arrived = [swap(part, "fsdp", 2) for part in sends]
-
+
+    first_count, rest = chunks[0][1], rows - chunks[0][1]
+    theirs = [product(acts, cot, 3, 0, first_count, rows, bf16, after=(ready,))]
+    shares = [swap(theirs[0], "fsdp", 1)]
+    if OPT[0]:
+        theirs.append(product(acts, cot, 3, first_count, rest, rows, bf16, after=theirs, us=FILL[3]))
+
+    mine = product(acts, cot, 2, 0, first_count, rows, jnp.float32, after=theirs[-1:], us=FILL[4])
+    sends = [
+        pl.pallas_call(
+            add_kernel,
+            out_shape=jax.ShapeDtypeStruct(mine.shape, bf16),
+            in_specs=[VMEM, VMEM],
+            out_specs=VMEM,
+            compiler_params=params(),
+            cost_estimate=cost(0),
+        )(mine, shares[0])
+    ]
     codes = pl.pallas_call(
         functools.partial(code_kernel, parts, group),
         out_shape=[jax.ShapeDtypeStruct((length, head), jnp.int16)] * parts,
@@ -295,9 +300,22 @@
         out_specs=[VMEM] * parts,
         compiler_params=params(),
         cost_estimate=cost(COST[0]),
-    )(mant, *all_lines, sends[OPT[0]])
-    core = product(acts, cot, 1, 0, rows, rows, bf16, after=codes[:1], us=FILL[0])
-    codes = [codes[0]] + [swap(codes[k], "replica", k * group) for k in range(1, parts)]
+    )(mant, *all_lines, sends[0])
+    if not OPT[0]:
+        theirs.append(product(acts, cot, 3, first_count, rest, rows, bf16, after=sends[:1], us=FILL[3]))
+    shares.append(swap(theirs[1], "fsdp", 1))
+    for n, (row, count) in enumerate(chunks[1:]):
+        sends.append(
+            product(acts, cot, 2, row, count, rows, bf16, shares[1], row - first_count, after=sends[-1:], us=FILL[5])
+        )
+    arrived = [swap(part, "fsdp", 2) for part in sends]
+    core = product(acts, cot, 1, 0, rows, rows, bf16, after=sends[1:2], us=FILL[0])
+    if OPT[1]:
+        own = product(acts, cot, 0, 0, rows, rows, jnp.float32, after=(core,))
+    codes = list(codes)
+    for k in (1,):
+        codes[k], _ = lax.optimization_barrier((codes[k], sends[1]))
+    codes = [codes[0]] + [swap(codes[k], "replica", k * group) for k in range(parts - 1, 0, -1)]
     wide = jnp.int16 if islands * 128 * 8 <= 2 ** 15 else jnp.int32
     code = pl.pallas_call(
         functools.partial(align_kernel, parts),
@@ -306,10 +324,11 @@
         out_specs=VMEM,
         compiler_params=params(),
         cost_estimate=cost(0),
-    )(*codes, core, sends[-1])
+    )(*codes, own if OPT[1] else core, sends[-1])
     core = swap(core, "fsdp", 1)
     others = [swap(code, "replica", k) for k in range(1, group)]
-    own = product(acts, cot, 0, 0, rows, rows, jnp.float32, after=(code,), us=FILL[1])
+    if not OPT[1]:
+        own = product(acts, cot, 0, 0, rows, rows, jnp.float32, after=(code,), us=FILL[1])
     *outs, part_head = adam(own, core, arrived[0], weight, first, second, 0, head, us=FILL[1], after=(code,))
     heads = [part_head]
     total = pl.pallas_call(
@@ -319,7 +338,7 @@
         out_specs=VMEM,
         compiler_params=params(),
         cost_estimate=cost(0),
-    )(code, *others, part_head)
+    )(code, *others, own if OPT[2] else part_head)
     codes = [total] + [swap(total, "replica", k * group) for k in range(1, parts)]
     for (row, _), part in zip(chunks[1:-1], arrived[1:]):
         *outs, part_head = adam(own, core, part, weight, first, second, row, head, outs, us=FILL[2])

time: 35 us -> 33.2 us (0.949)
  waiting for transfers between devices: 4.64 us -> 3.19 us
  local copies, waits for them, and re-layouts: 0.72 us -> 0.05 us
  Pallas kernels: 10.7 us -> 11.1 us
    ppermute x15 -> x14, waiting for transfers between devices: 4.64 us -> 3.19 us  [swap(): return lax.ppermute(x, axis, [(i, i ^ flip) for i in range(size)])]
    unnamed x18, local copies, waits for them, and re-layouts: 0.72 us -> 0.05 us
    pallas_call x8 -> x7, Pallas kernels: 4.37 us -> 4.76 us  [product(): pl.pallas_call(functools.partial(product_kernel, flip, row, rows, len(sha...]
    ppermute x15 -> x14, starting transfers between devices: 17.9 us -> 17.8 us  [swap(): return lax.ppermute(x, axis, [(i, i ^ flip) for i in range(size)])]
  transfers between devices with their start and end apart: 15 -> 14, of which waited for: 6 -> 5; matrix products, arithmetic and copies ran while one was open for 0% -> 0% of each run, Pallas kernels for 24% -> 28%
where the time goes in v3:
time: 33.2 us; the launch traced here: 33.1 us
  starting transfers between devices  17.8 us (54%)
  Pallas kernels  11.1 us (33%)
  waiting for transfers between devices  3.19 us (10%)
  between operations  0.86 us (3%)
    ppermute x14, starting transfers between devices, swap(): return lax.ppermute(x, axis, [(i, i ^ flip) for i in range(size)])  17.8 us
    pallas_call x7, Pallas kernels, product(): pl.pallas_call(functools.partial(product_kernel, flip, row, rows, len(sha...  4.76 us
    pallas_call x2, Pallas kernels, adam(): pl.pallas_call(adam_kernel, out_shape=[jax.ShapeDtypeStruct(a.shape, a.dt...  3.86 us
    ppermute x14, waiting for transfers between devices, swap(): return lax.ppermute(x, axis, [(i, i ^ flip) for i in range(size)])  3.19 us
    pallas_call x1, Pallas kernels, finish(): pl.pallas_call(functools.partial(finish_kernel, group, islands, parts, ea...  1.92 us
  transfers between devices with their start and end apart: 14, of which 5 were waited for; matrix products, arithmetic and copies ran while one was open for 0% of the time, Pallas kernels for 28%

profile of v3, /device:TPU:0, one launch (start us, length us, event | category | flops | bytes accessed | tf_op | source)
XLA Modules:
  0.0 33.1 jit_solution(7243480394738606260)
XLA Ops:
  0.6 0.0 copy-start
  0.7 3.0 %collective-permute-start = (s32[8,128]{1,0:T(8,128)}, s32[8,128]{1,0:T(8,128)S(1)}, u32[]{:S(2)}, u32[]{:S(2)}) collective-permute-start(s32[8,128]{1,0:T(8,128)} %bitcast.34), channel_id=1, source_target_pairs={{0,1},{1,0},{2,3},{3,2},{4,5},{5,4},{6,7},{7,6},{8,9},{9,8},{10,11... | collective-permute-start | bytes 12296 | tf_op jit(solution)/shard_map/ppermute | solution.py:231
  3.7 0.0 copy-done.4
  3.7 0.3 shard_map.129.refs_0_
  4.0 0.1 collective-permute-start.1
  4.1 0.9 %shard_map.130.refs_0_ = bf16[768,512]{1,0:T(8,128)(2,1)S(1)} custom-call(bf16[256,4096]{1,0:T(8,128)(2,1)S(1)} %bitcast.11, bf16[256,512]{1,0:T(8,128)(2,1)S(1)} %bitcast.27, bf16[256,512]{1,0:T(8,128)(2,1)S(1)} %shard_map.129.refs_0_), custom_call_target="tpu_custom_call" | custom-call | flops 23000000512 | tf_op jit(solution)/shard_map/pallas_call | solution.py:68
  4.9 0.0 copy-start.7
  5.0 0.0 copy-start.8
  5.0 0.6 %collective-permute-start.4 = (bf16[768,512]{1,0:T(8,128)(2,1)S(1)}, bf16[768,512]{1,0:T(8,128)(2,1)S(1)}, u32[]{:S(2)}, u32[]{:S(2)}) collective-permute-start(bf16[768,512]{1,0:T(8,128)(2,1)S(1)} %shard_map.130.refs_0_), channel_id=1, source_target_pairs={{0,8},{8,0},{16,24},{24,16},{1,9},{9,1},{17,25},{25,17},{2,10},{10... | collective-permute-start | bytes 2359304 | tf_op jit(solution)/shard_map/ppermute | solution.py:231
  5.5 0.3 shard_map.131.mine_ref
  5.8 0.0 collective-permute-done.1.other_ref
  5.9 1.6 %collective-permute-start.9 = (bf16[256,512]{1,0:T(8,128)(2,1)S(1)}, bf16[256,512]{1,0:T(8,128)(2,1)S(1)}, u32[]{:S(2)}, u32[]{:S(2)}) collective-permute-start(bf16[256,512]{1,0:T(8,128)(2,1)S(1)} %shard_map.132.refs_2_.refs_1_), channel_id=1, source_target_pairs={{0,16},{8,24},{16,0},{24,8},{1,17},{9,25},{17,1},{25,9},{2,18},{10... | collective-permute-start | bytes 786440 | tf_op jit(solution)/shard_map/ppermute | solution.py:231
  7.5 0.0 collective-permute-done.refs_1_
  7.5 0.0 copy-done.8
  7.5 0.4 %shard_map.133 = (s16[256,128]{1,0:T(8,128)(2,1)S(1)}, s16[256,128]{1,0:T(8,128)(2,1)S(1)}, s16[256,128]{1,0:T(8,128)(2,1)S(1)}, s16[256,128]{1,0:T(8,128)(2,1)S(1)}) custom-call(s32[1024,128]{1,0:T(8,128)S(1)} %bitcast.33, s32[8,128]{1,0:T(8,128)S(1)} %bitcast.35, s32[8,128]{1,0:T(8,128)S(1)} %collective-permute-done.refs_1_, ...), custom_call_target="tpu_custom_call" | custom-call | tf_op jit(solution)/shard_map/pallas_call | solution.py:296
  7.9 3.7 %collective-permute-start.2 = (s16[256,128]{1,0:T(8,128)(2,1)S(1)}, s16[256,128]{1,0:T(8,128)(2,1)S(1)}, u32[]{:S(2)}, u32[]{:S(2)}) collective-permute-start(s16[256,128]{1,0:T(8,128)(2,1)S(1)} %get-tuple-element.24), channel_id=1, source_target_pairs={{0,6},{1,7},{2,4},{3,5},{4,2},{5,3},{6,0},{7,1},{8,14},{9,15},{10,... | collective-permute-start | bytes 196616 | tf_op jit(solution)/shard_map/ppermute | solution.py:231
  11.5 0.0 collective-permute-start.3
  11.6 0.0 collective-permute-done.4.refs_0_
  11.6 0.6 %shard_map.134.refs_0_.refs_1_ = bf16[512,512]{1,0:T(8,128)(2,1)S(1)} custom-call(bf16[256,4096]{1,0:T(8,128)(2,1)S(1)} %bitcast.13, bf16[256,512]{1,0:T(8,128)(2,1)S(1)} %bitcast.29, bf16[768,512]{1,0:T(8,128)(2,1)S(1)} %collective-permute-done.4.refs_0_, bf16[256,512]{1,0:T(8,128)(2,1)S(1)} %shard_map.132.refs_2_.refs_1_), custom_call_target="tpu_custom_call" | custom-call | flops 23000000512 | tf_op jit(solution)/shard_map/pallas_call | solution.py:68
  12.2 0.6 %collective-permute-start.13 = (bf16[512,512]{1,0:T(8,128)(2,1)S(1)}, bf16[512,512]{1,0:T(8,128)(2,1)S(1)}, u32[]{:S(2)}, u32[]{:S(2)}) collective-permute-start(bf16[512,512]{1,0:T(8,128)(2,1)S(1)} %shard_map.134.refs_0_.refs_1_), channel_id=1, source_target_pairs={{0,16},{8,24},{16,0},{24,8},{1,17},{9,25},{17,1},{25,9},{2,18},{10... | collective-permute-start | bytes 1572872 | tf_op jit(solution)/shard_map/ppermute | solution.py:231
  12.7 0.8 %collective-permute-start.5 = (s16[256,128]{1,0:T(8,128)(2,1)S(1)}, s16[256,128]{1,0:T(8,128)(2,1)S(1)}, u32[]{:S(2)}, u32[]{:S(2)}) collective-permute-start(s16[256,128]{1,0:T(8,128)(2,1)S(1)} %get-tuple-element.27), channel_id=1, source_target_pairs={{0,2},{1,3},{2,0},{3,1},{4,6},{5,7},{6,4},{7,5},{8,10},{9,11},{10,... | collective-permute-start | bytes 196616 | tf_op jit(solution)/shard_map/ppermute | solution.py:231
  13.5 0.3 shard_map.136.refs_5_
  13.8 1.2 %shard_map.135.refs_4_ = bf16[1024,512]{1,0:T(8,128)(2,1)S(1)} custom-call(bf16[256,4096]{1,0:T(8,128)(2,1)S(1)} %bitcast.15, bf16[256,512]{1,0:T(8,128)(2,1)S(1)} %bitcast.31, bf16[512,512]{1,0:T(8,128)(2,1)S(1)} %shard_map.134.refs_0_.refs_1_), custom_call_target="tpu_custom_call" | custom-call | tf_op jit(solution)/shard_map/pallas_call | solution.py:68
  15.0 0.0 collective-permute-done.2.refs_1_
  15.0 1.6 %collective-permute-start.7 = (bf16[256,512]{1,0:T(8,128)(2,1)S(1)}, bf16[256,512]{1,0:T(8,128)(2,1)S(1)}, u32[]{:S(2)}, u32[]{:S(2)}) collective-permute-start(bf16[256,512]{1,0:T(8,128)(2,1)S(1)} %shard_map.136.refs_5_), channel_id=1, source_target_pairs={{0,16},{8,24},{16,0},{24,8},{1,17},{9,25},{17,1},{25,9},{2,18},{10... | collective-permute-start | bytes 786440 | tf_op jit(solution)/shard_map/ppermute | solution.py:231
  16.6 0.5 %collective-permute-done.3.refs_2_ = s16[256,128]{1,0:T(8,128)(2,1)S(1)} collective-permute-done((s16[256,128]{1,0:T(8,128)(2,1)S(1)}, s16[256,128]{1,0:T(8,128)(2,1)S(1)}, u32[]{:S(2)}, u32[]{:S(2)}) %collective-permute-start.3) | collective-permute-done | bytes 65568 | tf_op jit(solution)/shard_map/ppermute | solution.py:231
  17.1 0.0 collective-permute-start.6
  17.1 0.6 %collective-permute-done.5.refs_3_ = s16[256,128]{1,0:T(8,128)(2,1)S(1)} collective-permute-done((s16[256,128]{1,0:T(8,128)(2,1)S(1)}, s16[256,128]{1,0:T(8,128)(2,1)S(1)}, u32[]{:S(2)}, u32[]{:S(2)}) %collective-permute-start.5) | collective-permute-done | bytes 65568 | tf_op jit(solution)/shard_map/ppermute | solution.py:231
  17.8 0.2 shard_map.137.refs_0_.rest_0_.code_ref
  17.9 0.0 copy-start.1
  18.0 0.0 copy-start.2
  18.0 0.0 copy-start.3
  18.0 1.6 %collective-permute-start.8 = (s16[256,128]{1,0:T(8,128)(2,1)S(1)}, s16[256,128]{1,0:T(8,128)(2,1)S(1)}, u32[]{:S(2)}, u32[]{:S(2)}) collective-permute-start(s16[256,128]{1,0:T(8,128)(2,1)S(1)} %shard_map.137.refs_0_.rest_0_.code_ref), channel_id=1, source_target_pairs={{0,1},{1,0},{2,3},{3,2},{4,5},{5,4},{6,7},{7,6},{8,9},{9,8},{10,11... | collective-permute-start | bytes 196616 | tf_op jit(solution)/shard_map/ppermute | solution.py:231
  19.5 1.2 %shard_map.138.own_ref.refs_3_ = f32[1024,512]{1,0:T(8,128)S(1)} custom-call(bf16[256,4096]{1,0:T(8,128)(2,1)S(1)} %bitcast.16, bf16[256,512]{1,0:T(8,128)(2,1)S(1)} %bitcast.32, s16[256,128]{1,0:T(8,128)(2,1)S(1)} %shard_map.137.refs_0_.rest_0_.code_ref), custom_call_target="tpu_custom_call" | custom-call | flops 23000000512 | tf_op jit(solution)/shard_map/pallas_call | solution.py:68
  20.7 0.0 collective-permute-done.9.chip_ref
  20.7 0.0 collective-permute-done.6.core_ref.refs_4_
  20.8 1.4 %shard_map.139 = (f32[1024,512]{1,0:T(8,128)}, bf16[1024,512]{1,0:T(8,128)(2,1)}, bf16[1024,512]{1,0:T(8,128)(2,1)}, f32[256,128]{1,0:T(8,128)S(1)}) custom-call(f32[1024,512]{1,0:T(8,128)S(1)} %shard_map.138.own_ref.refs_3_, bf16[1024,512]{1,0:T(8,128)(2,1)S(1)} %collective-permute-done.6.core_ref.refs_4_, ...), custom_call_target="tpu_custom_call" | custom-call | flops 23000000512 | tf_op jit(solution)/shard_map/pallas_call | solution.py:113
  22.2 0.1 collective-permute-done.8.refs_0_
  22.3 2.8 %collective-permute-start.12 = (s16[256,128]{1,0:T(8,128)(2,1)S(1)}, s16[256,128]{1,0:T(8,128)(2,1)S(1)}, u32[]{:S(2)}, u32[]{:S(2)}) collective-permute-start(s16[256,128]{1,0:T(8,128)(2,1)S(1)} %shard_map.140.refs_8_), channel_id=1, source_target_pairs={{0,6},{1,7},{2,4},{3,5},{4,2},{5,3},{6,0},{7,1},{8,14},{9,15},{10,... | collective-permute-start | bytes 196616 | tf_op jit(solution)/shard_map/ppermute | solution.py:231
  25.1 0.0 collective-permute-start.11
  25.1 1.7 %collective-permute-start.10 = (s16[256,128]{1,0:T(8,128)(2,1)S(1)}, s16[256,128]{1,0:T(8,128)(2,1)S(1)}, u32[]{:S(2)}, u32[]{:S(2)}) collective-permute-start(s16[256,128]{1,0:T(8,128)(2,1)S(1)} %shard_map.140.refs_8_), channel_id=1, source_target_pairs={{0,2},{1,3},{2,0},{3,1},{4,6},{5,7},{6,4},{7,5},{8,10},{9,11},{10,... | collective-permute-start | bytes 196616 | tf_op jit(solution)/shard_map/ppermute | solution.py:231
  26.8 0.3 collective-permute-done.13.chip_ref
  27.1 2.4 %shard_map.141 = (f32[1024,512]{1,0:T(8,128)}, bf16[1024,512]{1,0:T(8,128)(2,1)}, bf16[1024,512]{1,0:T(8,128)(2,1)}, f32[512,128]{1,0:T(8,128)S(1)}) custom-call(f32[1024,512]{1,0:T(8,128)S(1)} %shard_map.138.own_ref.refs_3_, ...), custom_call_target="tpu_custom_call", output_to_operand_aliasing={{0}: (6, {}), {1}: (7, {}), {2}: (8, {})} | custom-call | flops 23000000512 | tf_op jit(solution)/shard_map/pallas_call | solution.py:113
  29.5 1.6 %collective-permute-done.7.refs_5_ = bf16[256,512]{1,0:T(8,128)(2,1)S(1)} collective-permute-done((bf16[256,512]{1,0:T(8,128)(2,1)S(1)}, bf16[256,512]{1,0:T(8,128)(2,1)S(1)}, u32[]{:S(2)}, u32[]{:S(2)}) %collective-permute-start.7) | collective-permute-done | bytes 262176 | tf_op jit(solution)/shard_map/ppermute | solution.py:231
  31.1 0.0 collective-permute-done.12.refs_11_
  31.1 0.0 collective-permute-done.11.refs_10_
  31.1 0.0 collective-permute-done.10.refs_9_
  31.2 1.9 %shard_map.142 = (f32[1024,512]{1,0:T(8,128)}, bf16[1024,512]{1,0:T(8,128)(2,1)}, bf16[1024,512]{1,0:T(8,128)(2,1)}, f32[1024,128]{1,0:T(8,128)}, f32[1024,128]{1,0:T(8,128)}) custom-call(f32[1024,512]{1,0:T(8,128)S(1)} %bitcast.19, bf16[1024,512]{1,0:T(8,128)(2,1)S(1)} %bitcast.22, ...), custom_call_target="tpu_custom_call", output_to_operand_aliasing={{0}: (14, {}), {1}: (15, {}), {2}: (16, {})} | custom-call | tf_op jit(solution)/shard_map/pallas_call | solution.py:207
  (13 shorter events, 0.1 us)
Async XLA Ops:
  0.6 3.0 %copy-start = (bf16[1,256,4096]{2,1,0:T(8,128)(2,1)S(1)}, bf16[1,256,4096]{2,1,0:T(8,128)(2,1)}, u32[]{:S(2)}) copy-start(bf16[1,256,4096]{2,1,0:T(8,128)(2,1)} %param.9) | copy-start | bytes 6291460
  0.6 3.0 %copy-start.4 = (bf16[1,256,512]{2,1,0:T(8,128)(2,1)S(1)}, bf16[1,256,512]{2,1,0:T(8,128)(2,1)}, u32[]{:S(2)}) copy-start(bf16[1,256,512]{2,1,0:T(8,128)(2,1)} %param.10) | copy-start | bytes 786436
  0.7 6.9 %collective-permute-start = (s32[8,128]{1,0:T(8,128)}, s32[8,128]{1,0:T(8,128)S(1)}, u32[]{:S(2)}, u32[]{:S(2)}) collective-permute-start(s32[8,128]{1,0:T(8,128)} %bitcast.34), channel_id=1, source_target_pairs={{0,1},{1,0},{2,3},{3,2},{4,5},{5,4},{6,7},{7,6},{8,9},{9,8},{10,11... | collective-permute-start | bytes 12296 | tf_op jit(solution)/shard_map/ppermute | solution.py:231
  4.0 1.9 %collective-permute-start.1 = (bf16[256,512]{1,0:T(8,128)(2,1)S(1)}, bf16[256,512]{1,0:T(8,128)(2,1)S(1)}, u32[]{:S(2)}, u32[]{:S(2)}) collective-permute-start(bf16[256,512]{1,0:T(8,128)(2,1)S(1)} %shard_map.129.refs_0_), channel_id=1, source_target_pairs={{0,8},{8,0},{16,24},{24,16},{1,9},{9,1},{17,25},{25,17},{2,10},{10... | collective-permute-start | bytes 786440 | tf_op jit(solution)/shard_map/ppermute | solution.py:231
  4.9 2.6 %copy-start.7 = (s32[1,1024,128]{2,1,0:T(8,128)S(1)}, s32[1,1024,128]{2,1,0:T(8,128)}, u32[]{:S(2)}) copy-start(s32[1,1024,128]{2,1,0:T(8,128)} %param.16) | copy-start | bytes 1572868
  5.0 2.5 %copy-start.8 = (s32[1,1024]{1,0:T(1,128)S(1)}, s32[1,1024]{1,0:T(1,128)}, u32[]{:S(2)}) copy-start(s32[1,1024]{1,0:T(1,128)} %param.17) | copy-start | bytes 12292
  5.0 6.6 %collective-permute-start.4 = (bf16[768,512]{1,0:T(8,128)(2,1)S(1)}, bf16[768,512]{1,0:T(8,128)(2,1)S(1)}, u32[]{:S(2)}, u32[]{:S(2)}) collective-permute-start(bf16[768,512]{1,0:T(8,128)(2,1)S(1)} %shard_map.130.refs_0_), channel_id=1, source_target_pairs={{0,8},{8,0},{16,24},{24,16},{1,9},{9,1},{17,25},{25,17},{2,10},{10... | collective-permute-start | bytes 2359304 | tf_op jit(solution)/shard_map/ppermute | solution.py:231
  5.9 14.8 %collective-permute-start.9 = (bf16[256,512]{1,0:T(8,128)(2,1)S(1)}, bf16[256,512]{1,0:T(8,128)(2,1)S(1)}, u32[]{:S(2)}, u32[]{:S(2)}) collective-permute-start(bf16[256,512]{1,0:T(8,128)(2,1)S(1)} %shard_map.132.refs_2_.refs_1_), channel_id=1, source_target_pairs={{0,16},{8,24},{16,0},{24,8},{1,17},{9,25},{17,1},{25,9},{2,18},{10... | collective-permute-start | bytes 786440 | tf_op jit(solution)/shard_map/ppermute | solution.py:231
  7.9 7.1 %collective-permute-start.2 = (s16[256,128]{1,0:T(8,128)(2,1)S(1)}, s16[256,128]{1,0:T(8,128)(2,1)S(1)}, u32[]{:S(2)}, u32[]{:S(2)}) collective-permute-start(s16[256,128]{1,0:T(8,128)(2,1)S(1)} %get-tuple-element.24), channel_id=1, source_target_pairs={{0,6},{1,7},{2,4},{3,5},{4,2},{5,3},{6,0},{7,1},{8,14},{9,15},{10,... | collective-permute-start | bytes 196616 | tf_op jit(solution)/shard_map/ppermute | solution.py:231
  11.5 5.6 %collective-permute-start.3 = (s16[256,128]{1,0:T(8,128)(2,1)S(1)}, s16[256,128]{1,0:T(8,128)(2,1)S(1)}, u32[]{:S(2)}, u32[]{:S(2)}) collective-permute-start(s16[256,128]{1,0:T(8,128)(2,1)S(1)} %get-tuple-element.25), channel_id=1, source_target_pairs={{0,4},{1,5},{2,6},{3,7},{4,0},{5,1},{6,2},{7,3},{8,12},{9,13},{10,... | collective-permute-start | bytes 196616 | tf_op jit(solution)/shard_map/ppermute | solution.py:231
  12.2 14.9 %collective-permute-start.13 = (bf16[512,512]{1,0:T(8,128)(2,1)S(1)}, bf16[512,512]{1,0:T(8,128)(2,1)S(1)}, u32[]{:S(2)}, u32[]{:S(2)}) collective-permute-start(bf16[512,512]{1,0:T(8,128)(2,1)S(1)} %shard_map.134.refs_0_.refs_1_), channel_id=1, source_target_pairs={{0,16},{8,24},{16,0},{24,8},{1,17},{9,25},{17,1},{25,9},{2,18},{10... | collective-permute-start | bytes 1572872 | tf_op jit(solution)/shard_map/ppermute | solution.py:231
  12.7 5.0 %collective-permute-start.5 = (s16[256,128]{1,0:T(8,128)(2,1)S(1)}, s16[256,128]{1,0:T(8,128)(2,1)S(1)}, u32[]{:S(2)}, u32[]{:S(2)}) collective-permute-start(s16[256,128]{1,0:T(8,128)(2,1)S(1)} %get-tuple-element.27), channel_id=1, source_target_pairs={{0,2},{1,3},{2,0},{3,1},{4,6},{5,7},{6,4},{7,5},{8,10},{9,11},{10,... | collective-permute-start | bytes 196616 | tf_op jit(solution)/shard_map/ppermute | solution.py:231
  15.0 16.1 %collective-permute-start.7 = (bf16[256,512]{1,0:T(8,128)(2,1)S(1)}, bf16[256,512]{1,0:T(8,128)(2,1)S(1)}, u32[]{:S(2)}, u32[]{:S(2)}) collective-permute-start(bf16[256,512]{1,0:T(8,128)(2,1)S(1)} %shard_map.136.refs_5_), channel_id=1, source_target_pairs={{0,16},{8,24},{16,0},{24,8},{1,17},{9,25},{17,1},{25,9},{2,18},{10... | collective-permute-start | bytes 786440 | tf_op jit(solution)/shard_map/ppermute | solution.py:231
  17.1 3.6 %collective-permute-start.6 = (bf16[1024,512]{1,0:T(8,128)(2,1)S(1)}, bf16[1024,512]{1,0:T(8,128)(2,1)S(1)}, u32[]{:S(2)}, u32[]{:S(2)}) collective-permute-start(bf16[1024,512]{1,0:T(8,128)(2,1)S(1)} %shard_map.135.refs_4_), channel_id=1, source_target_pairs={{0,8},{8,0},{16,24},{24,16},{1,9},{9,1},{17,25},{25,17},{2,10},{10... | collective-permute-start | bytes 3145736 | tf_op jit(solution)/shard_map/ppermute | solution.py:231
  17.9 2.8 %copy-start.1 = (f32[1,1024,512]{2,1,0:T(8,128)S(1)}, f32[1,1024,512]{2,1,0:T(8,128)}, u32[]{:S(2)}) copy-start(f32[1,1024,512]{2,1,0:T(8,128)} %param.11) | copy-start | bytes 6291460
  18.0 2.8 %copy-start.2 = (bf16[1,1024,512]{2,1,0:T(8,128)(2,1)S(1)}, bf16[1,1024,512]{2,1,0:T(8,128)(2,1)}, u32[]{:S(2)}) copy-start(bf16[1,1024,512]{2,1,0:T(8,128)(2,1)} %param.12) | copy-start | bytes 3145732
  18.0 2.8 %copy-start.3 = (bf16[1,1024,512]{2,1,0:T(8,128)(2,1)S(1)}, bf16[1,1024,512]{2,1,0:T(8,128)(2,1)}, u32[]{:S(2)}) copy-start(bf16[1,1024,512]{2,1,0:T(8,128)(2,1)} %param.13) | copy-start | bytes 3145732
  18.0 4.3 %collective-permute-start.8 = (s16[256,128]{1,0:T(8,128)(2,1)S(1)}, s16[256,128]{1,0:T(8,128)(2,1)S(1)}, u32[]{:S(2)}, u32[]{:S(2)}) collective-permute-start(s16[256,128]{1,0:T(8,128)(2,1)S(1)} %shard_map.137.refs_0_.rest_0_.code_ref), channel_id=1, source_target_pairs={{0,1},{1,0},{2,3},{3,2},{4,5},{5,4},{6,7},{7,6},{8,9},{9,8},{10,11... | collective-permute-start | bytes 196616 | tf_op jit(solution)/shard_map/ppermute | solution.py:231
  22.3 8.8 %collective-permute-start.12 = (s16[256,128]{1,0:T(8,128)(2,1)S(1)}, s16[256,128]{1,0:T(8,128)(2,1)S(1)}, u32[]{:S(2)}, u32[]{:S(2)}) collective-permute-start(s16[256,128]{1,0:T(8,128)(2,1)S(1)} %shard_map.140.refs_8_), channel_id=1, source_target_pairs={{0,6},{1,7},{2,4},{3,5},{4,2},{5,3},{6,0},{7,1},{8,14},{9,15},{10,... | collective-permute-start | bytes 196616 | tf_op jit(solution)/shard_map/ppermute | solution.py:231
  25.1 6.0 %collective-permute-start.11 = (s16[256,128]{1,0:T(8,128)(2,1)S(1)}, s16[256,128]{1,0:T(8,128)(2,1)S(1)}, u32[]{:S(2)}, u32[]{:S(2)}) collective-permute-start(s16[256,128]{1,0:T(8,128)(2,1)S(1)} %shard_map.140.refs_8_), channel_id=1, source_target_pairs={{0,4},{1,5},{2,6},{3,7},{4,0},{5,1},{6,2},{7,3},{8,12},{9,13},{10,... | collective-permute-start | bytes 196616 | tf_op jit(solution)/shard_map/ppermute | solution.py:231
  25.1 6.0 %collective-permute-start.10 = (s16[256,128]{1,0:T(8,128)(2,1)S(1)}, s16[256,128]{1,0:T(8,128)(2,1)S(1)}, u32[]{:S(2)}, u32[]{:S(2)}) collective-permute-start(s16[256,128]{1,0:T(8,128)(2,1)S(1)} %shard_map.140.refs_8_), channel_id=1, source_target_pairs={{0,2},{1,3},{2,0},{3,1},{4,6},{5,7},{6,4},{7,5},{8,10},{9,11},{10,... | collective-permute-start | bytes 196616 | tf_op jit(solution)/shard_map/ppermute | solution.py:231
  27.1 4.1 %copy-start.5 = (f32[1024,128]{1,0:T(8,128)S(1)}, f32[1024,128]{1,0:T(8,128)}, u32[]{:S(2)}) copy-start(f32[1024,128]{1,0:T(8,128)} %refs_6_.1) | copy-start | bytes 1572868
  27.1 4.1 %copy-start.6 = (f32[1024,128]{1,0:T(8,128)S(1)}, f32[1024,128]{1,0:T(8,128)}, u32[]{:S(2)}) copy-start(f32[1024,128]{1,0:T(8,128)} %refs_7_.1) | copy-start | bytes 1572868

commit v4 on v3

--- a/solution.py
+++ b/solution.py
@@ -19,10 +19,8 @@
 
 ANY = pl.BlockSpec(memory_space=pl.ANY)
 VMEM = pl.BlockSpec(memory_space=pltpu.VMEM)
-COST = (0, 0, 0, 1)
-OPT = (1, 0, 0)
-UNITS = (2, 4, 2)
-FILL = (0, 20, 20, 20, 20, 20)
+BLOCK = 128
+FILL = 20
 LIMIT = 32 * 1024 * 1024
 
 
@@ -38,44 +36,26 @@
     return lax.dot_general(tokens, cot, (((0,), (0,)), ((), ())), preferred_element_type=jnp.float32)
 
 
-def pieces(count):
-    size = next(s for s in (256, 384, 128) if count % s == 0)
-    return [(at, size) for at in range(0, count, size)]
-
-
 def product_kernel(flip, row, rows, summed, skip, acts_ref, cot_ref, *refs):
-    out_ref, buf, cot, sems, cot_sem = refs[-5:]
+    out_ref = refs[-1]
     owner = lax.axis_index("fsdp") ^ flip
-    cot_copy = pltpu.make_async_copy(cot_ref, cot, cot_sem)
-    cot_copy.start()
-    copies = []
-    for n, (at, size) in enumerate(pieces(out_ref.shape[0])):
+    for at in range(0, out_ref.shape[0], 128):
+        size = min(128, out_ref.shape[0] - at)
         cols = pl.ds(pl.multiple_of(owner * rows + row + at, 128), size)
-        copies.append(pltpu.make_async_copy(acts_ref.at[:, cols], buf.at[:, pl.ds(at, size)], sems.at[n]))
-        copies[-1].start()
-    cot_copy.wait()
-    for copy, (at, size) in zip(copies, pieces(out_ref.shape[0])):
-        copy.wait()
-        total = token_product(buf[:, at:at + size], cot[...])
+        total = token_product(acts_ref[:, cols], cot_ref[...])
         if summed:
             total = total + refs[0][skip + at:skip + at + size, :].astype(jnp.float32)
         out_ref[at:at + size, :] = total.astype(out_ref.dtype)
 
 
 def product(acts, cot, flip, row, count, rows, dtype, other=None, skip=0, after=(), us=0):
-    tokens, width = cot.shape
+    width = cot.shape[1]
     shares = () if other is None else (other,)
     return pl.pallas_call(
         functools.partial(product_kernel, flip, row, rows, len(shares), skip),
         out_shape=jax.ShapeDtypeStruct((count, width), dtype),
-        in_specs=[ANY, ANY] + [VMEM] * len(shares) + [ANY] * len(after),
+        in_specs=[VMEM] * (2 + len(shares)) + [ANY] * len(after),
         out_specs=VMEM,
-        scratch_shapes=[
-            pltpu.VMEM((tokens, count), acts.dtype),
-            pltpu.VMEM(cot.shape, cot.dtype),
-            pltpu.SemaphoreType.DMA((len(pieces(count)),)),
-            pltpu.SemaphoreType.DMA,
-        ],
         compiler_params=params(),
         cost_estimate=cost(us),
     )(acts, cot, *shares, *after)
@@ -114,7 +94,7 @@
         adam_kernel,
         out_shape=[jax.ShapeDtypeStruct(a.shape, a.dtype) for a in (weight, first, second)]
         + [jax.ShapeDtypeStruct((count, head), weight.dtype)],
-        grid=(count // block,),
+        grid=(count // BLOCK,),
         in_specs=specs,
         out_specs=[here] * 3 + [pl.BlockSpec((block, head), lambda i: (i, 0))],
         input_output_aliases=aliases,
@@ -184,9 +164,8 @@
         mixed[at, :] = MIX_SHARE * head[...] + (1.0 - MIX_SHARE) * outer[at, :]
         row += head.shape[0]
     store(mixed, weight_out.at[pl.ds(0, last), pl.ds(0, width)])
-    block = 128
-    for i in range(count // block):
-        here, there = slice(i * block, (i + 1) * block), slice(last + i * block, last + (i + 1) * block)
+    for i in range(count // BLOCK):
+        here, there = slice(i * BLOCK, (i + 1) * BLOCK), slice(last + i * BLOCK, last + (i + 1) * BLOCK)
         gradient = own_ref[there, :] + core_ref[there, :].astype(jnp.float32) + chip_ref[here, :].astype(jnp.float32)
         updated, first_new[here, :], second_new[here, :] = adam_step(
             gradient, weight_ref[there, :], first_ref[there, :], second_ref[there, :]
@@ -194,7 +173,7 @@
         weight_new[here, width:] = updated[:, width:]
         weight_new[here, :width] = MIX_SHARE * updated[:, :width] + (1.0 - MIX_SHARE) * outer[there, :]
         for new, out in ((weight_new, weight_out), (first_new, first_out), (second_new, second_out)):
-            store(new.at[pl.ds(i * block, block)], out.at[pl.ds(last + i * block, block)])
+            store(new.at[pl.ds(i * BLOCK, BLOCK)], out.at[pl.ds(last + i * BLOCK, BLOCK)])
     for copy in stores:
         copy.wait()
 
@@ -219,7 +198,7 @@
             pltpu.VMEM(fragment, jnp.float32),
             pltpu.VMEM(fragment, jnp.float32),
             pltpu.VMEM((weight.shape[0] - count, fragment[1]), jnp.float32),
-            pltpu.SemaphoreType.DMA((2 * parts + 1 + 3 * (count // 128),)),
+            pltpu.SemaphoreType.DMA((2 * parts + 1 + 3 * (count // BLOCK),)),
         ],
         compiler_params=params(),
         cost_estimate=cost(0),
@@ -262,27 +241,22 @@
     parts, group = island_groups(islands)
     length, head = rows // parts, mant.shape[1]
     unit = rows // 8
-    chunks, row = [], 0
-    for units in UNITS:
-        chunks.append((row * unit, units * unit))
-        row += units
+    chunks = ((0, 2 * unit), (2 * unit, 4 * unit), (6 * unit, 2 * unit))
+    late = rows - chunks[0][1]
 
     ready = pl.pallas_call(
         start_kernel,
         out_shape=jax.ShapeDtypeStruct((8, 128), jnp.int32),
         out_specs=VMEM,
         compiler_params=params(),
-        cost_estimate=cost(COST[3]),
+        cost_estimate=cost(1),
     )()
     all_lines = [lines] + [swap(lines, "replica", k) for k in range(1, group)]
 
-    first_count, rest = chunks[0][1], rows - chunks[0][1]
-    theirs = [product(acts, cot, 3, 0, first_count, rows, bf16, after=(ready,))]
-    shares = [swap(theirs[0], "fsdp", 1)]
-    if OPT[0]:
-        theirs.append(product(acts, cot, 3, first_count, rest, rows, bf16, after=theirs, us=FILL[3]))
-
-    mine = product(acts, cot, 2, 0, first_count, rows, jnp.float32, after=theirs[-1:], us=FILL[4])
+    theirs = [product(acts, cot, 3, *chunks[0], rows, bf16, after=(ready,))]
+    theirs.append(product(acts, cot, 3, chunks[1][0], late, rows, bf16, after=theirs, us=FILL))
+    shares = [swap(part, "fsdp", 1) for part in theirs]
+    mine = product(acts, cot, 2, *chunks[0], rows, jnp.float32, after=theirs[1:], us=FILL)
     sends = [
         pl.pallas_call(
             add_kernel,
@@ -299,23 +273,18 @@
         in_specs=[VMEM] * (1 + group) + [ANY],
         out_specs=[VMEM] * parts,
         compiler_params=params(),
-        cost_estimate=cost(COST[0]),
+        cost_estimate=cost(0),
     )(mant, *all_lines, sends[0])
-    if not OPT[0]:
-        theirs.append(product(acts, cot, 3, first_count, rest, rows, bf16, after=sends[:1], us=FILL[3]))
-    shares.append(swap(theirs[1], "fsdp", 1))
-    for n, (row, count) in enumerate(chunks[1:]):
+    for row, count in chunks[1:]:
         sends.append(
-            product(acts, cot, 2, row, count, rows, bf16, shares[1], row - first_count, after=sends[-1:], us=FILL[5])
+            product(acts, cot, 2, row, count, rows, bf16, shares[1], row - chunks[1][0], after=sends[-1:], us=FILL)
         )
     arrived = [swap(part, "fsdp", 2) for part in sends]
-    core = product(acts, cot, 1, 0, rows, rows, bf16, after=sends[1:2], us=FILL[0])
-    if OPT[1]:
-        own = product(acts, cot, 0, 0, rows, rows, jnp.float32, after=(core,))
+
+    core = product(acts, cot, 1, 0, rows, rows, bf16, after=sends[1:2])
     codes = list(codes)
-    for k in (1,):
-        codes[k], _ = lax.optimization_barrier((codes[k], sends[1]))
-    codes = [codes[0]] + [swap(codes[k], "replica", k * group) for k in range(parts - 1, 0, -1)]
+    codes[1], _ = lax.optimization_barrier((codes[1], sends[1]))
+    codes = codes[:1] + [swap(codes[k], "replica", k * group) for k in range(parts - 1, 0, -1)]
     wide = jnp.int16 if islands * 128 * 8 <= 2 ** 15 else jnp.int32
     code = pl.pallas_call(
         functools.partial(align_kernel, parts),
@@ -324,13 +293,10 @@
         out_specs=VMEM,
         compiler_params=params(),
         cost_estimate=cost(0),
-    )(*codes, own if OPT[1] else core, sends[-1])
+    )(*codes, core, sends[2])
     core = swap(core, "fsdp", 1)
     others = [swap(code, "replica", k) for k in range(1, group)]
-    if not OPT[1]:
-        own = product(acts, cot, 0, 0, rows, rows, jnp.float32, after=(code,), us=FILL[1])
-    *outs, part_head = adam(own, core, arrived[0], weight, first, second, 0, head, us=FILL[1], after=(code,))
-    heads = [part_head]
+    own = product(acts, cot, 0, 0, rows, rows, jnp.float32, after=(code,), us=FILL)
     total = pl.pallas_call(
         functools.partial(join_kernel, group - 1),
         out_shape=jax.ShapeDtypeStruct((length, head), wide),
@@ -338,10 +304,15 @@
         out_specs=VMEM,
         compiler_params=params(),
         cost_estimate=cost(0),
-    )(code, *others, own if OPT[2] else part_head)
-    codes = [total] + [swap(total, "replica", k * group) for k in range(1, parts)]
-    for (row, _), part in zip(chunks[1:-1], arrived[1:]):
-        *outs, part_head = adam(own, core, part, weight, first, second, row, head, outs, us=FILL[2])
+    )(code, *others, own)
+    received = {k: swap(total, "replica", k * group) for k in range(parts - 1, 0, -1)}
+    codes = [total] + [received[k] for k in range(1, parts)]
+
+    outs, heads = (), []
+    for (row, _), part in zip(chunks[:-1], arrived):
+        *outs, part_head = adam(
+            own, core, part, weight, first, second, row, head, outs, us=FILL, after=() if outs else (total,)
+        )
         heads.append(part_head)
     weight_new, first_new, second_new, outer_new, momentum_new = finish(
         weight, first, second, own, core, arrived[-1], outer_weight, outer_momentum, codes, heads, outs, group, islands

time: 33.2 us -> 32.9 us (level)
  waiting for transfers between devices: 3.19 us -> 5.58 us
  Pallas kernels: 11.1 us -> 8.95 us
  starting transfers between devices: 17.8 us -> 17.4 us
    ppermute x14, waiting for transfers between devices: 3.19 us -> 5.58 us  [swap(): return lax.ppermute(x, axis, [(i, i ^ flip) for i in range(size)])]
    pallas_call x7, Pallas kernels: 4.76 us -> 2.53 us  [product(): pl.pallas_call(functools.partial(product_kernel, flip, row, rows, len(sha...]
    ppermute x14, starting transfers between devices: 17.8 us -> 17.4 us  [swap(): return lax.ppermute(x, axis, [(i, i ^ flip) for i in range(size)])]
  transfers between devices with their start and end apart: 14 -> 14, of which waited for: 5 -> 6; matrix products, arithmetic and copies ran while one was open for 0% -> 0% of each run, Pallas kernels for 28% -> 21%
where the time goes in v4:
time: 32.9 us; the launch traced here: 32.8 us
  starting transfers between devices  17.4 us (53%)
  Pallas kernels  8.95 us (27%)
  waiting for transfers between devices  5.58 us (17%)
  between operations  0.77 us (2%)
    ppermute x14, starting transfers between devices, swap(): return lax.ppermute(x, axis, [(i, i ^ flip) for i in range(size)])  17.4 us
    ppermute x14, waiting for transfers between devices, swap(): return lax.ppermute(x, axis, [(i, i ^ flip) for i in range(size)])  5.58 us
    pallas_call x2, Pallas kernels, adam(): pl.pallas_call(adam_kernel, out_shape=[jax.ShapeDtypeStruct(a.shape, a.dt...  3.89 us
    pallas_call x7, Pallas kernels, product(): pl.pallas_call(functools.partial(product_kernel, flip, row, rows, len(sha...  2.53 us
    pallas_call x1, Pallas kernels, finish(): pl.pallas_call(functools.partial(finish_kernel, group, islands, parts, ea...  1.91 us
  transfers between devices with their start and end apart: 14, of which 6 were waited for; matrix products, arithmetic and copies ran while one was open for 0% of the time, Pallas kernels for 21%

profile of v4, /device:TPU:0, one launch (start us, length us, event | category | flops | bytes accessed | tf_op | source)
XLA Modules:
  0.0 32.8 jit_solution(13719774736872710540)
XLA Ops:
  0.6 0.0 copy-start
  0.6 0.0 copy-start.4
  0.7 3.0 %collective-permute-start = (s32[8,128]{1,0:T(8,128)}, s32[8,128]{1,0:T(8,128)S(1)}, u32[]{:S(2)}, u32[]{:S(2)}) collective-permute-start(s32[8,128]{1,0:T(8,128)} %bitcast.34), channel_id=1, source_target_pairs={{0,1},{1,0},{2,3},{3,2},{4,5},{5,4},{6,7},{7,6},{8,9},{9,8},{10,11... | collective-permute-start | bytes 12296 | tf_op jit(solution)/shard_map/ppermute | solution.py:210
  3.7 0.0 copy-done
  3.7 0.3 shard_map.129.refs_0_
  3.9 0.1 collective-permute-start.1
  4.0 0.4 %shard_map.130.refs_0_ = bf16[768,512]{1,0:T(8,128)(2,1)S(1)} custom-call(bf16[256,4096]{1,0:T(8,128)(2,1)S(1)} %bitcast.11, bf16[256,512]{1,0:T(8,128)(2,1)S(1)} %bitcast.27, bf16[256,512]{1,0:T(8,128)(2,1)S(1)} %shard_map.129.refs_0_), custom_call_target="tpu_custom_call" | custom-call | flops 23000000512 | tf_op jit(solution)/shard_map/pallas_call | solution.py:54
  4.4 0.0 copy-start.7
  4.4 0.0 copy-start.8
  4.5 0.6 %collective-permute-start.4 = (bf16[768,512]{1,0:T(8,128)(2,1)S(1)}, bf16[768,512]{1,0:T(8,128)(2,1)S(1)}, u32[]{:S(2)}, u32[]{:S(2)}) collective-permute-start(bf16[768,512]{1,0:T(8,128)(2,1)S(1)} %shard_map.130.refs_0_), channel_id=1, source_target_pairs={{0,8},{8,0},{16,24},{24,16},{1,9},{9,1},{17,25},{25,17},{2,10},{10... | collective-permute-start | bytes 2359304 | tf_op jit(solution)/shard_map/ppermute | solution.py:210
  5.0 0.3 shard_map.131.mine_ref
  5.3 0.2 collective-permute-done.1.other_ref
  5.6 1.6 %collective-permute-start.12 = (bf16[256,512]{1,0:T(8,128)(2,1)S(1)}, bf16[256,512]{1,0:T(8,128)(2,1)S(1)}, u32[]{:S(2)}, u32[]{:S(2)}) collective-permute-start(bf16[256,512]{1,0:T(8,128)(2,1)S(1)} %shard_map.132.refs_2_.refs_1_), channel_id=1, source_target_pairs={{0,16},{8,24},{16,0},{24,8},{1,17},{9,25},{17,1},{25,9},{2,18},{10... | collective-permute-start | bytes 786440 | tf_op jit(solution)/shard_map/ppermute | solution.py:210
  7.2 0.0 collective-permute-done.refs_1_
  7.2 0.0 copy-done.7
  7.2 0.4 %shard_map.133 = (s16[256,128]{1,0:T(8,128)(2,1)S(1)}, s16[256,128]{1,0:T(8,128)(2,1)S(1)}, s16[256,128]{1,0:T(8,128)(2,1)S(1)}, s16[256,128]{1,0:T(8,128)(2,1)S(1)}) custom-call(s32[1024,128]{1,0:T(8,128)S(1)} %bitcast.33, s32[8,128]{1,0:T(8,128)S(1)} %bitcast.35, s32[8,128]{1,0:T(8,128)S(1)} %collective-permute-done.refs_1_, ...), custom_call_target="tpu_custom_call" | custom-call | tf_op jit(solution)/shard_map/pallas_call | solution.py:270
  7.6 3.7 %collective-permute-start.2 = (s16[256,128]{1,0:T(8,128)(2,1)S(1)}, s16[256,128]{1,0:T(8,128)(2,1)S(1)}, u32[]{:S(2)}, u32[]{:S(2)}) collective-permute-start(s16[256,128]{1,0:T(8,128)(2,1)S(1)} %get-tuple-element.24), channel_id=1, source_target_pairs={{0,6},{1,7},{2,4},{3,5},{4,2},{5,3},{6,0},{7,1},{8,14},{9,15},{10,... | collective-permute-start | bytes 196616 | tf_op jit(solution)/shard_map/ppermute | solution.py:210
  11.2 0.0 collective-permute-start.3
  11.2 0.0 collective-permute-done.4.refs_0_
  11.2 0.3 %shard_map.134.refs_0_.refs_1_ = bf16[512,512]{1,0:T(8,128)(2,1)S(1)} custom-call(bf16[256,4096]{1,0:T(8,128)(2,1)S(1)} %bitcast.13, bf16[256,512]{1,0:T(8,128)(2,1)S(1)} %bitcast.29, bf16[768,512]{1,0:T(8,128)(2,1)S(1)} %collective-permute-done.4.refs_0_, bf16[256,512]{1,0:T(8,128)(2,1)S(1)} %shard_map.132.refs_2_.refs_1_), custom_call_target="tpu_custom_call" | custom-call | flops 23000000512 | tf_op jit(solution)/shard_map/pallas_call | solution.py:54
  11.6 0.6 %collective-permute-start.13 = (bf16[512,512]{1,0:T(8,128)(2,1)S(1)}, bf16[512,512]{1,0:T(8,128)(2,1)S(1)}, u32[]{:S(2)}, u32[]{:S(2)}) collective-permute-start(bf16[512,512]{1,0:T(8,128)(2,1)S(1)} %shard_map.134.refs_0_.refs_1_), channel_id=1, source_target_pairs={{0,16},{8,24},{16,0},{24,8},{1,17},{9,25},{17,1},{25,9},{2,18},{10... | collective-permute-start | bytes 1572872 | tf_op jit(solution)/shard_map/ppermute | solution.py:210
  12.2 0.8 %collective-permute-start.5 = (s16[256,128]{1,0:T(8,128)(2,1)S(1)}, s16[256,128]{1,0:T(8,128)(2,1)S(1)}, u32[]{:S(2)}, u32[]{:S(2)}) collective-permute-start(s16[256,128]{1,0:T(8,128)(2,1)S(1)} %get-tuple-element.27), channel_id=1, source_target_pairs={{0,2},{1,3},{2,0},{3,1},{4,6},{5,7},{6,4},{7,5},{8,10},{9,11},{10,... | collective-permute-start | bytes 196616 | tf_op jit(solution)/shard_map/ppermute | solution.py:210
  12.9 0.3 shard_map.136.refs_5_
  13.2 0.5 %shard_map.135.refs_4_ = bf16[1024,512]{1,0:T(8,128)(2,1)S(1)} custom-call(bf16[256,4096]{1,0:T(8,128)(2,1)S(1)} %bitcast.15, bf16[256,512]{1,0:T(8,128)(2,1)S(1)} %bitcast.31, bf16[512,512]{1,0:T(8,128)(2,1)S(1)} %shard_map.134.refs_0_.refs_1_), custom_call_target="tpu_custom_call" | custom-call | tf_op jit(solution)/shard_map/pallas_call | solution.py:54
  13.7 0.4 %collective-permute-done.2.refs_1_ = s16[256,128]{1,0:T(8,128)(2,1)S(1)} collective-permute-done((s16[256,128]{1,0:T(8,128)(2,1)S(1)}, s16[256,128]{1,0:T(8,128)(2,1)S(1)}, u32[]{:S(2)}, u32[]{:S(2)}) %collective-permute-start.2) | collective-permute-done | bytes 65568 | tf_op jit(solution)/shard_map/ppermute | solution.py:210
  14.1 1.2 %collective-permute-start.7 = (bf16[256,512]{1,0:T(8,128)(2,1)S(1)}, bf16[256,512]{1,0:T(8,128)(2,1)S(1)}, u32[]{:S(2)}, u32[]{:S(2)}) collective-permute-start(bf16[256,512]{1,0:T(8,128)(2,1)S(1)} %shard_map.136.refs_5_), channel_id=1, source_target_pairs={{0,16},{8,24},{16,0},{24,8},{1,17},{9,25},{17,1},{25,9},{2,18},{10... | collective-permute-start | bytes 786440 | tf_op jit(solution)/shard_map/ppermute | solution.py:210
  15.3 1.6 %collective-permute-done.3.refs_2_ = s16[256,128]{1,0:T(8,128)(2,1)S(1)} collective-permute-done((s16[256,128]{1,0:T(8,128)(2,1)S(1)}, s16[256,128]{1,0:T(8,128)(2,1)S(1)}, u32[]{:S(2)}, u32[]{:S(2)}) %collective-permute-start.3) | collective-permute-done | bytes 65568 | tf_op jit(solution)/shard_map/ppermute | solution.py:210
  17.0 0.0 collective-permute-start.6
  17.0 0.6 %collective-permute-done.5.refs_3_ = s16[256,128]{1,0:T(8,128)(2,1)S(1)} collective-permute-done((s16[256,128]{1,0:T(8,128)(2,1)S(1)}, s16[256,128]{1,0:T(8,128)(2,1)S(1)}, u32[]{:S(2)}, u32[]{:S(2)}) %collective-permute-start.5) | collective-permute-done | bytes 65568 | tf_op jit(solution)/shard_map/ppermute | solution.py:210
  17.6 0.2 shard_map.137.refs_0_.code_ref
  17.7 1.6 %collective-permute-start.8 = (s16[256,128]{1,0:T(8,128)(2,1)S(1)}, s16[256,128]{1,0:T(8,128)(2,1)S(1)}, u32[]{:S(2)}, u32[]{:S(2)}) collective-permute-start(s16[256,128]{1,0:T(8,128)(2,1)S(1)} %shard_map.137.refs_0_.code_ref), channel_id=1, source_target_pairs={{0,1},{1,0},{2,3},{3,2},{4,5},{5,4},{6,7},{7,6},{8,9},{9,8},{10,11... | collective-permute-start | bytes 196616 | tf_op jit(solution)/shard_map/ppermute | solution.py:210
  19.3 0.5 %shard_map.138.refs_1_.own_ref.refs_3_ = f32[1024,512]{1,0:T(8,128)S(1)} custom-call(bf16[256,4096]{1,0:T(8,128)(2,1)S(1)} %bitcast.16, bf16[256,512]{1,0:T(8,128)(2,1)S(1)} %bitcast.32, s16[256,128]{1,0:T(8,128)(2,1)S(1)} %shard_map.137.refs_0_.code_ref), custom_call_target="tpu_custom_call" | custom-call | flops 23000000512 | tf_op jit(solution)/shard_map/pallas_call | solution.py:54
  19.8 0.0 copy-start.1
  19.8 2.3 %collective-permute-done.8.refs_0_ = s16[256,128]{1,0:T(8,128)(2,1)S(1)} collective-permute-done((s16[256,128]{1,0:T(8,128)(2,1)S(1)}, s16[256,128]{1,0:T(8,128)(2,1)S(1)}, u32[]{:S(2)}, u32[]{:S(2)}) %collective-permute-start.8) | collective-permute-done | bytes 65568 | tf_op jit(solution)/shard_map/ppermute | solution.py:210
  22.1 2.3 %collective-permute-start.11 = (s16[256,128]{1,0:T(8,128)(2,1)S(1)}, s16[256,128]{1,0:T(8,128)(2,1)S(1)}, u32[]{:S(2)}, u32[]{:S(2)}) collective-permute-start(s16[256,128]{1,0:T(8,128)(2,1)S(1)} %shard_map.139.rest_0_.refs_8_), channel_id=1, source_target_pairs={{0,6},{1,7},{2,4},{3,5},{4,2},{5,3},{6,0},{7,1},{8,14},{9,15},{10,... | collective-permute-start | bytes 196616 | tf_op jit(solution)/shard_map/ppermute | solution.py:210
  24.4 0.0 collective-permute-done.12.chip_ref
  24.4 0.0 collective-permute-start.10
  24.4 0.0 collective-permute-done.6.core_ref.refs_4_
  24.4 2.1 %collective-permute-start.9 = (s16[256,128]{1,0:T(8,128)(2,1)S(1)}, s16[256,128]{1,0:T(8,128)(2,1)S(1)}, u32[]{:S(2)}, u32[]{:S(2)}) collective-permute-start(s16[256,128]{1,0:T(8,128)(2,1)S(1)} %shard_map.139.rest_0_.refs_8_), channel_id=1, source_target_pairs={{0,2},{1,3},{2,0},{3,1},{4,6},{5,7},{6,4},{7,5},{8,10},{9,11},{10,... | collective-permute-start | bytes 196616 | tf_op jit(solution)/shard_map/ppermute | solution.py:210
  26.6 0.0 copy-done.2
  26.6 1.4 %shard_map.140 = (f32[1024,512]{1,0:T(8,128)}, bf16[1024,512]{1,0:T(8,128)(2,1)}, bf16[1024,512]{1,0:T(8,128)(2,1)}, f32[256,128]{1,0:T(8,128)S(1)}) custom-call(f32[1024,512]{1,0:T(8,128)S(1)} %shard_map.138.refs_1_.own_ref.refs_3_, bf16[1024,512]{1,0:T(8,128)(2,1)S(1)} %collective-permute-done.6.core_ref.refs_4_, ...), custom_call_target="tpu_custom_call" | custom-call | flops 23000000512 | tf_op jit(solution)/shard_map/pallas_call | solution.py:93
  28.0 0.0 collective-permute-done.13.chip_ref
  28.0 2.5 %shard_map.141 = (f32[1024,512]{1,0:T(8,128)}, bf16[1024,512]{1,0:T(8,128)(2,1)}, bf16[1024,512]{1,0:T(8,128)(2,1)}, f32[512,128]{1,0:T(8,128)S(1)}) custom-call(f32[1024,512]{1,0:T(8,128)S(1)} %shard_map.138.refs_1_.own_ref.refs_3_, ...), custom_call_target="tpu_custom_call", output_to_operand_aliasing={{0}: (6, {}), {1}: (7, {}), {2}: (8, {})} | custom-call | flops 23000000512 | tf_op jit(solution)/shard_map/pallas_call | solution.py:93
  30.5 0.0 collective-permute-done.11.refs_11_
  30.5 0.0 collective-permute-done.10.refs_10_
  30.5 0.0 collective-permute-done.9.refs_9_
  30.5 0.4 %collective-permute-done.7.refs_5_ = bf16[256,512]{1,0:T(8,128)(2,1)S(1)} collective-permute-done((bf16[256,512]{1,0:T(8,128)(2,1)S(1)}, bf16[256,512]{1,0:T(8,128)(2,1)S(1)}, u32[]{:S(2)}, u32[]{:S(2)}) %collective-permute-start.7) | collective-permute-done | bytes 262176 | tf_op jit(solution)/shard_map/ppermute | solution.py:210
  30.9 1.9 %shard_map.142 = (f32[1024,512]{1,0:T(8,128)}, bf16[1024,512]{1,0:T(8,128)(2,1)}, bf16[1024,512]{1,0:T(8,128)(2,1)}, f32[1024,128]{1,0:T(8,128)}, f32[1024,128]{1,0:T(8,128)}) custom-call(f32[1024,512]{1,0:T(8,128)S(1)} %bitcast.19, bf16[1024,512]{1,0:T(8,128)(2,1)S(1)} %bitcast.22, ...), custom_call_target="tpu_custom_call", output_to_operand_aliasing={{0}: (14, {}), {1}: (15, {}), {2}: (16, {})} | custom-call | tf_op jit(solution)/shard_map/pallas_call | solution.py:186
  (13 shorter events, 0.1 us)
Async XLA Ops:
  0.6 3.0 %copy-start = (bf16[1,256,4096]{2,1,0:T(8,128)(2,1)S(1)}, bf16[1,256,4096]{2,1,0:T(8,128)(2,1)}, u32[]{:S(2)}) copy-start(bf16[1,256,4096]{2,1,0:T(8,128)(2,1)} %param.9) | copy-start | bytes 6291460
  0.6 3.0 %copy-start.4 = (bf16[1,256,512]{2,1,0:T(8,128)(2,1)S(1)}, bf16[1,256,512]{2,1,0:T(8,128)(2,1)}, u32[]{:S(2)}) copy-start(bf16[1,256,512]{2,1,0:T(8,128)(2,1)} %param.10) | copy-start | bytes 786436
  0.7 6.5 %collective-permute-start = (s32[8,128]{1,0:T(8,128)}, s32[8,128]{1,0:T(8,128)S(1)}, u32[]{:S(2)}, u32[]{:S(2)}) collective-permute-start(s32[8,128]{1,0:T(8,128)} %bitcast.34), channel_id=1, source_target_pairs={{0,1},{1,0},{2,3},{3,2},{4,5},{5,4},{6,7},{7,6},{8,9},{9,8},{10,11... | collective-permute-start | bytes 12296 | tf_op jit(solution)/shard_map/ppermute | solution.py:210
  3.9 1.6 %collective-permute-start.1 = (bf16[256,512]{1,0:T(8,128)(2,1)S(1)}, bf16[256,512]{1,0:T(8,128)(2,1)S(1)}, u32[]{:S(2)}, u32[]{:S(2)}) collective-permute-start(bf16[256,512]{1,0:T(8,128)(2,1)S(1)} %shard_map.129.refs_0_), channel_id=1, source_target_pairs={{0,8},{8,0},{16,24},{24,16},{1,9},{9,1},{17,25},{25,17},{2,10},{10... | collective-permute-start | bytes 786440 | tf_op jit(solution)/shard_map/ppermute | solution.py:210
  4.4 2.7 %copy-start.7 = (s32[1,1024,128]{2,1,0:T(8,128)S(1)}, s32[1,1024,128]{2,1,0:T(8,128)}, u32[]{:S(2)}) copy-start(s32[1,1024,128]{2,1,0:T(8,128)} %param.16) | copy-start | bytes 1572868
  4.4 2.7 %copy-start.8 = (s32[1,1024]{1,0:T(1,128)S(1)}, s32[1,1024]{1,0:T(1,128)}, u32[]{:S(2)}) copy-start(s32[1,1024]{1,0:T(1,128)} %param.17) | copy-start | bytes 12292
  4.5 6.8 %collective-permute-start.4 = (bf16[768,512]{1,0:T(8,128)(2,1)S(1)}, bf16[768,512]{1,0:T(8,128)(2,1)S(1)}, u32[]{:S(2)}, u32[]{:S(2)}) collective-permute-start(bf16[768,512]{1,0:T(8,128)(2,1)S(1)} %shard_map.130.refs_0_), channel_id=1, source_target_pairs={{0,8},{8,0},{16,24},{24,16},{1,9},{9,1},{17,25},{25,17},{2,10},{10... | collective-permute-start | bytes 2359304 | tf_op jit(solution)/shard_map/ppermute | solution.py:210
  5.6 18.8 %collective-permute-start.12 = (bf16[256,512]{1,0:T(8,128)(2,1)S(1)}, bf16[256,512]{1,0:T(8,128)(2,1)S(1)}, u32[]{:S(2)}, u32[]{:S(2)}) collective-permute-start(bf16[256,512]{1,0:T(8,128)(2,1)S(1)} %shard_map.132.refs_2_.refs_1_), channel_id=1, source_target_pairs={{0,16},{8,24},{16,0},{24,8},{1,17},{9,25},{17,1},{25,9},{2,18},{10... | collective-permute-start | bytes 786440 | tf_op jit(solution)/shard_map/ppermute | solution.py:210
  7.6 6.6 %collective-permute-start.2 = (s16[256,128]{1,0:T(8,128)(2,1)S(1)}, s16[256,128]{1,0:T(8,128)(2,1)S(1)}, u32[]{:S(2)}, u32[]{:S(2)}) collective-permute-start(s16[256,128]{1,0:T(8,128)(2,1)S(1)} %get-tuple-element.24), channel_id=1, source_target_pairs={{0,6},{1,7},{2,4},{3,5},{4,2},{5,3},{6,0},{7,1},{8,14},{9,15},{10,... | collective-permute-start | bytes 196616 | tf_op jit(solution)/shard_map/ppermute | solution.py:210
  11.2 5.7 %collective-permute-start.3 = (s16[256,128]{1,0:T(8,128)(2,1)S(1)}, s16[256,128]{1,0:T(8,128)(2,1)S(1)}, u32[]{:S(2)}, u32[]{:S(2)}) collective-permute-start(s16[256,128]{1,0:T(8,128)(2,1)S(1)} %get-tuple-element.25), channel_id=1, source_target_pairs={{0,4},{1,5},{2,6},{3,7},{4,0},{5,1},{6,2},{7,3},{8,12},{9,13},{10,... | collective-permute-start | bytes 196616 | tf_op jit(solution)/shard_map/ppermute | solution.py:210
  11.6 16.4 %collective-permute-start.13 = (bf16[512,512]{1,0:T(8,128)(2,1)S(1)}, bf16[512,512]{1,0:T(8,128)(2,1)S(1)}, u32[]{:S(2)}, u32[]{:S(2)}) collective-permute-start(bf16[512,512]{1,0:T(8,128)(2,1)S(1)} %shard_map.134.refs_0_.refs_1_), channel_id=1, source_target_pairs={{0,16},{8,24},{16,0},{24,8},{1,17},{9,25},{17,1},{25,9},{2,18},{10... | collective-permute-start | bytes 1572872 | tf_op jit(solution)/shard_map/ppermute | solution.py:210
  12.2 5.4 %collective-permute-start.5 = (s16[256,128]{1,0:T(8,128)(2,1)S(1)}, s16[256,128]{1,0:T(8,128)(2,1)S(1)}, u32[]{:S(2)}, u32[]{:S(2)}) collective-permute-start(s16[256,128]{1,0:T(8,128)(2,1)S(1)} %get-tuple-element.27), channel_id=1, source_target_pairs={{0,2},{1,3},{2,0},{3,1},{4,6},{5,7},{6,4},{7,5},{8,10},{9,11},{10,... | collective-permute-start | bytes 196616 | tf_op jit(solution)/shard_map/ppermute | solution.py:210
  14.1 16.7 %collective-permute-start.7 = (bf16[256,512]{1,0:T(8,128)(2,1)S(1)}, bf16[256,512]{1,0:T(8,128)(2,1)S(1)}, u32[]{:S(2)}, u32[]{:S(2)}) collective-permute-start(bf16[256,512]{1,0:T(8,128)(2,1)S(1)} %shard_map.136.refs_5_), channel_id=1, source_target_pairs={{0,16},{8,24},{16,0},{24,8},{1,17},{9,25},{17,1},{25,9},{2,18},{10... | collective-permute-start | bytes 786440 | tf_op jit(solution)/shard_map/ppermute | solution.py:210
  17.0 7.5 %collective-permute-start.6 = (bf16[1024,512]{1,0:T(8,128)(2,1)S(1)}, bf16[1024,512]{1,0:T(8,128)(2,1)S(1)}, u32[]{:S(2)}, u32[]{:S(2)}) collective-permute-start(bf16[1024,512]{1,0:T(8,128)(2,1)S(1)} %shard_map.135.refs_4_), channel_id=1, source_target_pairs={{0,8},{8,0},{16,24},{24,16},{1,9},{9,1},{17,25},{25,17},{2,10},{10... | collective-permute-start | bytes 3145736 | tf_op jit(solution)/shard_map/ppermute | solution.py:210
  17.7 4.3 %collective-permute-start.8 = (s16[256,128]{1,0:T(8,128)(2,1)S(1)}, s16[256,128]{1,0:T(8,128)(2,1)S(1)}, u32[]{:S(2)}, u32[]{:S(2)}) collective-permute-start(s16[256,128]{1,0:T(8,128)(2,1)S(1)} %shard_map.137.refs_0_.code_ref), channel_id=1, source_target_pairs={{0,1},{1,0},{2,3},{3,2},{4,5},{5,4},{6,7},{7,6},{8,9},{9,8},{10,11... | collective-permute-start | bytes 196616 | tf_op jit(solution)/shard_map/ppermute | solution.py:210
  19.3 7.3 %copy-start.2 = (bf16[1,1024,512]{2,1,0:T(8,128)(2,1)S(1)}, bf16[1,1024,512]{2,1,0:T(8,128)(2,1)}, u32[]{:S(2)}) copy-start(bf16[1,1024,512]{2,1,0:T(8,128)(2,1)} %param.12) | copy-start | bytes 3145732
  19.3 7.3 %copy-start.3 = (bf16[1,1024,512]{2,1,0:T(8,128)(2,1)S(1)}, bf16[1,1024,512]{2,1,0:T(8,128)(2,1)}, u32[]{:S(2)}) copy-start(bf16[1,1024,512]{2,1,0:T(8,128)(2,1)} %param.13) | copy-start | bytes 3145732
  19.8 6.8 %copy-start.1 = (f32[1,1024,512]{2,1,0:T(8,128)S(1)}, f32[1,1024,512]{2,1,0:T(8,128)}, u32[]{:S(2)}) copy-start(f32[1,1024,512]{2,1,0:T(8,128)} %param.11) | copy-start | bytes 6291460
  22.1 8.4 %collective-permute-start.11 = (s16[256,128]{1,0:T(8,128)(2,1)S(1)}, s16[256,128]{1,0:T(8,128)(2,1)S(1)}, u32[]{:S(2)}, u32[]{:S(2)}) collective-permute-start(s16[256,128]{1,0:T(8,128)(2,1)S(1)} %shard_map.139.rest_0_.refs_8_), channel_id=1, source_target_pairs={{0,6},{1,7},{2,4},{3,5},{4,2},{5,3},{6,0},{7,1},{8,14},{9,15},{10,... | collective-permute-start | bytes 196616 | tf_op jit(solution)/shard_map/ppermute | solution.py:210
  24.4 6.0 %collective-permute-start.10 = (s16[256,128]{1,0:T(8,128)(2,1)S(1)}, s16[256,128]{1,0:T(8,128)(2,1)S(1)}, u32[]{:S(2)}, u32[]{:S(2)}) collective-permute-start(s16[256,128]{1,0:T(8,128)(2,1)S(1)} %shard_map.139.rest_0_.refs_8_), channel_id=1, source_target_pairs={{0,4},{1,5},{2,6},{3,7},{4,0},{5,1},{6,2},{7,3},{8,12},{9,13},{10,... | collective-permute-start | bytes 196616 | tf_op jit(solution)/shard_map/ppermute | solution.py:210
  24.4 6.0 %collective-permute-start.9 = (s16[256,128]{1,0:T(8,128)(2,1)S(1)}, s16[256,128]{1,0:T(8,128)(2,1)S(1)}, u32[]{:S(2)}, u32[]{:S(2)}) collective-permute-start(s16[256,128]{1,0:T(8,128)(2,1)S(1)} %shard_map.139.rest_0_.refs_8_), channel_id=1, source_target_pairs={{0,2},{1,3},{2,0},{3,1},{4,6},{5,7},{6,4},{7,5},{8,10},{9,11},{10,... | collective-permute-start | bytes 196616 | tf_op jit(solution)/shard_map/ppermute | solution.py:210
  28.0 2.9 %copy-start.5 = (f32[1024,128]{1,0:T(8,128)S(1)}, f32[1024,128]{1,0:T(8,128)}, u32[]{:S(2)}) copy-start(f32[1024,128]{1,0:T(8,128)} %refs_6_.1) | copy-start | bytes 1572868
  28.0 2.9 %copy-start.6 = (f32[1024,128]{1,0:T(8,128)S(1)}, f32[1024,128]{1,0:T(8,128)}, u32[]{:S(2)}) copy-start(f32[1024,128]{1,0:T(8,128)} %refs_7_.1) | copy-start | bytes 1572868

commit v5 on v4

--- a/solution.py
+++ b/solution.py
@@ -64,43 +64,54 @@
 def adam_step(gradient, weight, first, second):
     moment_one = BETA_ONE * first.astype(jnp.float32) + (1.0 - BETA_ONE) * gradient
     moment_two = BETA_TWO * second.astype(jnp.float32) + (1.0 - BETA_TWO) * gradient * gradient
-    updated = weight - LEARN_RATE * (
-        moment_one / (jnp.sqrt(moment_two) + ADAM_EPSILON) + DECAY_RATE * weight
-    )
+    root = moment_two * lax.rsqrt(moment_two)
+    step = moment_one / (root + ADAM_EPSILON)
+    updated = weight - LEARN_RATE * (step + DECAY_RATE * weight)
     return updated, moment_one.astype(first.dtype), moment_two.astype(second.dtype)
 
 
-def adam_kernel(own_ref, core_ref, chip_ref, weight_ref, first_ref, second_ref, *rest):
-    weight_out, first_out, second_out, head_out = rest[-4:]
-    gradient = own_ref[...] + core_ref[...].astype(jnp.float32) + chip_ref[...].astype(jnp.float32)
-    weight_out[...], first_out[...], second_out[...] = adam_step(
-        gradient, weight_ref[...], first_ref[...], second_ref[...]
-    )
-    head_out[...] = weight_out[:, : head_out.shape[1]]
+def adam_kernel(row, own_ref, core_ref, chip_ref, weight_ref, first_ref, second_ref, *refs):
+    weight_out, first_out, second_out, head_out, weight_new, first_new, second_new, sems = refs[-8:]
+    count = chip_ref.shape[0]
+    stores = []
+    for i in range(count // BLOCK):
+        here, there = slice(i * BLOCK, (i + 1) * BLOCK), slice(row + i * BLOCK, row + (i + 1) * BLOCK)
+        gradient = own_ref[there, :] + core_ref[there, :].astype(jnp.float32) + chip_ref[here, :].astype(jnp.float32)
+        updated, first_new[here, :], second_new[here, :] = adam_step(
+            gradient, weight_ref[there, :], first_ref[there, :], second_ref[there, :]
+        )
+        weight_new[here, :] = updated
+        head_out[here, :] = updated[:, : head_out.shape[1]]
+        for new, out in ((weight_new, weight_out), (first_new, first_out), (second_new, second_out)):
+            stores.append(
+                pltpu.make_async_copy(
+                    new.at[pl.ds(i * BLOCK, BLOCK)], out.at[pl.ds(row + i * BLOCK, BLOCK)], sems.at[len(stores)]
+                )
+            )
+            stores[-1].start()
+    for copy in stores:
+        copy.wait()
 
 
 def adam(own, core, chip, weight, first, second, row, head, outs=(), us=0, after=()):
-    block = 128
-    rows, width = weight.shape
-    count = chip.shape[0]
-    here = pl.BlockSpec((block, width), lambda i: (row // block + i, 0))
+    count, width = chip.shape
     operands = [own, core, chip, weight, first, second]
-    specs = [here, here, pl.BlockSpec((block, width), lambda i: (i, 0)), here, here, here]
-    aliases = {len(operands) + i: i for i in range(len(outs))}
-    operands += list(outs)
-    operands += list(after)
-    specs += [ANY] * (len(outs) + len(after))
     return pl.pallas_call(
-        adam_kernel,
+        functools.partial(adam_kernel, row),
         out_shape=[jax.ShapeDtypeStruct(a.shape, a.dtype) for a in (weight, first, second)]
         + [jax.ShapeDtypeStruct((count, head), weight.dtype)],
-        grid=(count // BLOCK,),
-        in_specs=specs,
-        out_specs=[here] * 3 + [pl.BlockSpec((block, head), lambda i: (i, 0))],
-        input_output_aliases=aliases,
+        in_specs=[VMEM] * len(operands) + [ANY] * (len(outs) + len(after)),
+        out_specs=[ANY] * 3 + [VMEM],
+        input_output_aliases={len(operands) + i: i for i in range(len(outs))},
+        scratch_shapes=[
+            pltpu.VMEM((count, width), weight.dtype),
+            pltpu.VMEM((count, width), first.dtype),
+            pltpu.VMEM((count, width), second.dtype),
+            pltpu.SemaphoreType.DMA((3 * (count // BLOCK),)),
+        ],
         compiler_params=params(),
         cost_estimate=cost(us),
-    )(*operands)
+    )(*operands, *outs, *after)
 
 
 def by_row(exps_ref, at):
@@ -132,16 +143,12 @@
     refs[-1][...] = (total * 8 + top).astype(refs[-1].dtype)
 
 
-def finish_kernel(group, islands, parts, early, *refs):
-    weight_ref, first_ref, second_ref, own_ref, core_ref, chip_ref, ow_ref, om_ref = refs[:8]
-    codes, heads = refs[8:8 + parts], refs[8 + parts:8 + parts + early]
-    weight_out, first_out, second_out, outer_out, momentum_out = refs[8 + parts + early + 3:-7]
-    weight_new, first_new, second_new, outer, momentum, mixed, sems = refs[-7:]
+def outer_kernel(group, islands, parts, early, ow_ref, om_ref, *refs):
+    codes, heads = refs[:parts], refs[parts:parts + early]
+    weight_out, outer_out, momentum_out, tail_out, outer, momentum, mixed, sems = refs[parts + early + 1:]
     where = lax.axis_index("replica") // group
     length = codes[0].shape[0]
-    count = chip_ref.shape[0]
-    last = weight_ref.shape[0] - count
-    width = mixed.shape[1]
+    last, width = mixed.shape
     stores = []
 
     def store(source, target):
@@ -164,6 +171,40 @@
         mixed[at, :] = MIX_SHARE * head[...] + (1.0 - MIX_SHARE) * outer[at, :]
         row += head.shape[0]
     store(mixed, weight_out.at[pl.ds(0, last), pl.ds(0, width)])
+    tail_out[...] = outer[last:, :]
+    for copy in stores:
+        copy.wait()
+
+
+def outer_step(weight, outer_weight, outer_momentum, codes, heads, group, islands):
+    parts, early = len(codes), len(heads)
+    rows, width = outer_weight.shape
+    last = sum(h.shape[0] for h in heads)
+    operands = [outer_weight, outer_momentum, *codes, *heads]
+    return pl.pallas_call(
+        functools.partial(outer_kernel, group, islands, parts, early),
+        out_shape=[jax.ShapeDtypeStruct(a.shape, a.dtype) for a in (weight, outer_weight, outer_momentum)]
+        + [jax.ShapeDtypeStruct((rows - last, width), jnp.float32)],
+        in_specs=[VMEM] * len(operands) + [ANY],
+        out_specs=[ANY] * 3 + [VMEM],
+        input_output_aliases={len(operands): 0},
+        scratch_shapes=[
+            pltpu.VMEM((rows, width), jnp.float32),
+            pltpu.VMEM((rows, width), jnp.float32),
+            pltpu.VMEM((last, width), jnp.float32),
+            pltpu.SemaphoreType.DMA((2 * parts + 1,)),
+        ],
+        compiler_params=params(),
+        cost_estimate=cost(0),
+    )(*operands, weight)
+
+
+def last_kernel(weight_ref, first_ref, second_ref, own_ref, core_ref, chip_ref, outer_ref, *refs):
+    weight_out, first_out, second_out, weight_new, first_new, second_new, sems = refs[3:]
+    count = chip_ref.shape[0]
+    last = weight_ref.shape[0] - count
+    width = outer_ref.shape[1]
+    stores = []
     for i in range(count // BLOCK):
         here, there = slice(i * BLOCK, (i + 1) * BLOCK), slice(last + i * BLOCK, last + (i + 1) * BLOCK)
         gradient = own_ref[there, :] + core_ref[there, :].astype(jnp.float32) + chip_ref[here, :].astype(jnp.float32)
@@ -171,34 +212,32 @@
             gradient, weight_ref[there, :], first_ref[there, :], second_ref[there, :]
         )
         weight_new[here, width:] = updated[:, width:]
-        weight_new[here, :width] = MIX_SHARE * updated[:, :width] + (1.0 - MIX_SHARE) * outer[there, :]
+        weight_new[here, :width] = MIX_SHARE * updated[:, :width] + (1.0 - MIX_SHARE) * outer_ref[here, :]
         for new, out in ((weight_new, weight_out), (first_new, first_out), (second_new, second_out)):
-            store(new.at[pl.ds(i * BLOCK, BLOCK)], out.at[pl.ds(last + i * BLOCK, BLOCK)])
+            stores.append(
+                pltpu.make_async_copy(
+                    new.at[pl.ds(i * BLOCK, BLOCK)], out.at[pl.ds(last + i * BLOCK, BLOCK)], sems.at[len(stores)]
+                )
+            )
+            stores[-1].start()
     for copy in stores:
         copy.wait()
 
 
-def finish(weight, first, second, own, core, chip, outer_weight, outer_momentum, codes, heads, outs, group, islands):
-    parts, early = len(codes), len(heads)
+def last_step(weight, first, second, own, core, chip, outer, outs):
     count, width = chip.shape
-    fragment = outer_weight.shape
-    operands = [weight, first, second, own, core, chip, outer_weight, outer_momentum, *codes, *heads]
+    operands = [weight, first, second, own, core, chip, outer]
     return pl.pallas_call(
-        functools.partial(finish_kernel, group, islands, parts, early),
-        out_shape=[
-            jax.ShapeDtypeStruct(a.shape, a.dtype) for a in (weight, first, second, outer_weight, outer_momentum)
-        ],
+        last_kernel,
+        out_shape=[jax.ShapeDtypeStruct(a.shape, a.dtype) for a in (weight, first, second)],
         in_specs=[VMEM] * len(operands) + [ANY] * 3,
-        out_specs=[ANY] * 5,
+        out_specs=[ANY] * 3,
         input_output_aliases={len(operands) + i: i for i in range(3)},
         scratch_shapes=[
             pltpu.VMEM((count, width), weight.dtype),
             pltpu.VMEM((count, width), first.dtype),
             pltpu.VMEM((count, width), second.dtype),
-            pltpu.VMEM(fragment, jnp.float32),
-            pltpu.VMEM(fragment, jnp.float32),
-            pltpu.VMEM((weight.shape[0] - count, fragment[1]), jnp.float32),
-            pltpu.SemaphoreType.DMA((2 * parts + 1 + 3 * (count // BLOCK),)),
+            pltpu.SemaphoreType.DMA((3 * (count // BLOCK),)),
         ],
         compiler_params=params(),
         cost_estimate=cost(0),
@@ -275,13 +314,9 @@
         compiler_params=params(),
         cost_estimate=cost(0),
     )(mant, *all_lines, sends[0])
-    for row, count in chunks[1:]:
-        sends.append(
-            product(acts, cot, 2, row, count, rows, bf16, shares[1], row - chunks[1][0], after=sends[-1:], us=FILL)
-        )
-    arrived = [swap(part, "fsdp", 2) for part in sends]
-
-    core = product(acts, cot, 1, 0, rows, rows, bf16, after=sends[1:2])
+    sends.append(product(acts, cot, 2, *chunks[1], rows, bf16, shares[1], after=sends[:1], us=FILL))
+
+    core = product(acts, cot, 1, 0, rows, rows, bf16, after=sends[1:], us=FILL)
     codes = list(codes)
     codes[1], _ = lax.optimization_barrier((codes[1], sends[1]))
     codes = codes[:1] + [swap(codes[k], "replica", k * group) for k in range(parts - 1, 0, -1)]
@@ -289,13 +324,16 @@
     code = pl.pallas_call(
         functools.partial(align_kernel, parts),
         out_shape=jax.ShapeDtypeStruct((length, head), wide),
-        in_specs=[VMEM] * parts + [ANY] * 2,
+        in_specs=[VMEM] * parts + [ANY],
         out_specs=VMEM,
         compiler_params=params(),
         cost_estimate=cost(0),
-    )(*codes, core, sends[2])
+    )(*codes, core)
     core = swap(core, "fsdp", 1)
     others = [swap(code, "replica", k) for k in range(1, group)]
+    skip = chunks[2][0] - chunks[1][0]
+    sends.append(product(acts, cot, 2, *chunks[2], rows, bf16, shares[1], skip, after=(code,)))
+    arrived = [swap(part, "fsdp", 2) for part in sends]
     own = product(acts, cot, 0, 0, rows, rows, jnp.float32, after=(code,), us=FILL)
     total = pl.pallas_call(
         functools.partial(join_kernel, group - 1),
@@ -314,8 +352,11 @@
             own, core, part, weight, first, second, row, head, outs, us=FILL, after=() if outs else (total,)
         )
         heads.append(part_head)
-    weight_new, first_new, second_new, outer_new, momentum_new = finish(
-        weight, first, second, own, core, arrived[-1], outer_weight, outer_momentum, codes, heads, outs, group, islands
+    weight_new, outer_new, momentum_new, tail = outer_step(
+        outs[0], outer_weight, outer_momentum, codes, heads, group, islands
+    )
+    weight_new, first_new, second_new = last_step(
+        weight, first, second, own, core, arrived[-1], tail, (weight_new, *outs[1:])
     )
     return (weight_new[None], first_new[None], second_new[None], outer_new, momentum_new)
 

time: 32.9 us -> 32.5 us (0.988)
  Pallas kernels: 8.95 us -> 8.61 us
    ppermute x14, starting transfers between devices: 17.4 us -> 17.1 us  [swap(): return lax.ppermute(x, axis, [(i, i ^ flip) for i in range(size)])]
    pallas_call x3 -> x4, Pallas kernels: 5.81 us -> 5.47 us  [the longest x2 2.98 us: adam(): pl.pallas_call(functools.partial(adam_kernel, row), out_shape=[jax.ShapeD...]
  transfers between devices with their start and end apart: 14 -> 14, of which waited for: 6 -> 6; matrix products, arithmetic and copies ran while one was open for 0% -> 0% of each run, Pallas kernels for 21% -> 23%
where the time goes in v5:
time: 32.5 us; the launch traced here: 32.3 us
  starting transfers between devices  17.1 us (53%)
  Pallas kernels  8.61 us (26%)
  waiting for transfers between devices  5.78 us (18%)
  between operations  0.84 us (3%)
    ppermute x14, starting transfers between devices, swap(): return lax.ppermute(x, axis, [(i, i ^ flip) for i in range(size)])  17.1 us
    ppermute x14, waiting for transfers between devices, swap(): return lax.ppermute(x, axis, [(i, i ^ flip) for i in range(size)])  5.78 us
    pallas_call x2, Pallas kernels, adam(): pl.pallas_call(functools.partial(adam_kernel, row), out_shape=[jax.ShapeD...  2.98 us
    pallas_call x7, Pallas kernels, product(): pl.pallas_call(functools.partial(product_kernel, flip, row, rows, len(sha...  2.53 us
    pallas_call x1, Pallas kernels, last_step(): pl.pallas_call(last_kernel, out_shape=[jax.ShapeDtypeStruct(a.shape, a.dt...  1.27 us
    pallas_call x1, Pallas kernels, outer_step(): pl.pallas_call(functools.partial(outer_kernel, group, islands, parts, ear...  1.23 us
  transfers between devices with their start and end apart: 14, of which 6 were waited for; matrix products, arithmetic and copies ran while one was open for 0% of the time, Pallas kernels for 23%

profile of v5, /device:TPU:0, one launch (start us, length us, event | category | flops | bytes accessed | tf_op | source)
XLA Modules:
  0.0 32.3 jit_solution(15315279178915704002)
XLA Ops:
  0.7 3.0 %collective-permute-start = (s32[8,128]{1,0:T(8,128)}, s32[8,128]{1,0:T(8,128)S(1)}, u32[]{:S(2)}, u32[]{:S(2)}) collective-permute-start(s32[8,128]{1,0:T(8,128)} %bitcast.34), channel_id=1, source_target_pairs={{0,1},{1,0},{2,3},{3,2},{4,5},{5,4},{6,7},{7,6},{8,9},{9,8},{10,11... | collective-permute-start | bytes 12296 | tf_op jit(solution)/shard_map/ppermute | solution.py:249
  3.7 0.3 shard_map.129.refs_0_
  3.9 0.1 collective-permute-start.1
  4.0 0.4 %shard_map.130.refs_0_ = bf16[768,512]{1,0:T(8,128)(2,1)S(1)} custom-call(bf16[256,4096]{1,0:T(8,128)(2,1)S(1)} %bitcast.11, bf16[256,512]{1,0:T(8,128)(2,1)S(1)} %bitcast.27, bf16[256,512]{1,0:T(8,128)(2,1)S(1)} %shard_map.129.refs_0_), custom_call_target="tpu_custom_call" | custom-call | flops 23000000512 | tf_op jit(solution)/shard_map/pallas_call | solution.py:54
  4.4 0.0 copy-start.5
  4.4 0.0 copy-start.8
  4.5 0.6 %collective-permute-start.4 = (bf16[768,512]{1,0:T(8,128)(2,1)S(1)}, bf16[768,512]{1,0:T(8,128)(2,1)S(1)}, u32[]{:S(2)}, u32[]{:S(2)}) collective-permute-start(bf16[768,512]{1,0:T(8,128)(2,1)S(1)} %shard_map.130.refs_0_), channel_id=1, source_target_pairs={{0,8},{8,0},{16,24},{24,16},{1,9},{9,1},{17,25},{25,17},{2,10},{10... | collective-permute-start | bytes 2359304 | tf_op jit(solution)/shard_map/ppermute | solution.py:249
  5.0 0.3 shard_map.131.mine_ref
  5.3 0.2 collective-permute-done.1.other_ref
  5.6 1.6 %collective-permute-start.12 = (bf16[256,512]{1,0:T(8,128)(2,1)S(1)}, bf16[256,512]{1,0:T(8,128)(2,1)S(1)}, u32[]{:S(2)}, u32[]{:S(2)}) collective-permute-start(bf16[256,512]{1,0:T(8,128)(2,1)S(1)} %shard_map.132.refs_2_.refs_1_), channel_id=1, source_target_pairs={{0,16},{8,24},{16,0},{24,8},{1,17},{9,25},{17,1},{25,9},{2,18},{10... | collective-permute-start | bytes 786440 | tf_op jit(solution)/shard_map/ppermute | solution.py:249
  7.2 0.0 collective-permute-done.refs_1_
  7.2 0.4 %shard_map.133 = (s16[256,128]{1,0:T(8,128)(2,1)S(1)}, s16[256,128]{1,0:T(8,128)(2,1)S(1)}, s16[256,128]{1,0:T(8,128)(2,1)S(1)}, s16[256,128]{1,0:T(8,128)(2,1)S(1)}) custom-call(s32[1024,128]{1,0:T(8,128)S(1)} %bitcast.33, s32[8,128]{1,0:T(8,128)S(1)} %bitcast.35, s32[8,128]{1,0:T(8,128)S(1)} %collective-permute-done.refs_1_, ...), custom_call_target="tpu_custom_call" | custom-call | tf_op jit(solution)/shard_map/pallas_call | solution.py:309
  7.6 3.7 %collective-permute-start.2 = (s16[256,128]{1,0:T(8,128)(2,1)S(1)}, s16[256,128]{1,0:T(8,128)(2,1)S(1)}, u32[]{:S(2)}, u32[]{:S(2)}) collective-permute-start(s16[256,128]{1,0:T(8,128)(2,1)S(1)} %get-tuple-element.26), channel_id=1, source_target_pairs={{0,6},{1,7},{2,4},{3,5},{4,2},{5,3},{6,0},{7,1},{8,14},{9,15},{10,... | collective-permute-start | bytes 196616 | tf_op jit(solution)/shard_map/ppermute | solution.py:249
  11.2 0.0 collective-permute-start.3
  11.2 0.0 collective-permute-done.4.refs_0_
  11.2 0.3 %shard_map.134.refs_0_ = bf16[512,512]{1,0:T(8,128)(2,1)S(1)} custom-call(bf16[256,4096]{1,0:T(8,128)(2,1)S(1)} %bitcast.13, bf16[256,512]{1,0:T(8,128)(2,1)S(1)} %bitcast.29, bf16[768,512]{1,0:T(8,128)(2,1)S(1)} %collective-permute-done.4.refs_0_, bf16[256,512]{1,0:T(8,128)(2,1)S(1)} %shard_map.132.refs_2_.refs_1_), custom_call_target="tpu_custom_call" | custom-call | flops 23000000512 | tf_op jit(solution)/shard_map/pallas_call | solution.py:54
  11.6 0.6 %collective-permute-start.13 = (bf16[512,512]{1,0:T(8,128)(2,1)S(1)}, bf16[512,512]{1,0:T(8,128)(2,1)S(1)}, u32[]{:S(2)}, u32[]{:S(2)}) collective-permute-start(bf16[512,512]{1,0:T(8,128)(2,1)S(1)} %shard_map.134.refs_0_), channel_id=1, source_target_pairs={{0,16},{8,24},{16,0},{24,8},{1,17},{9,25},{17,1},{25,9},{2,18},{10... | collective-permute-start | bytes 1572872 | tf_op jit(solution)/shard_map/ppermute | solution.py:249
  12.2 0.8 %collective-permute-start.5 = (s16[256,128]{1,0:T(8,128)(2,1)S(1)}, s16[256,128]{1,0:T(8,128)(2,1)S(1)}, u32[]{:S(2)}, u32[]{:S(2)}) collective-permute-start(s16[256,128]{1,0:T(8,128)(2,1)S(1)} %get-tuple-element.29), channel_id=1, source_target_pairs={{0,2},{1,3},{2,0},{3,1},{4,6},{5,7},{6,4},{7,5},{8,10},{9,11},{10,... | collective-permute-start | bytes 196616 | tf_op jit(solution)/shard_map/ppermute | solution.py:249
  12.9 0.5 %shard_map.135.refs_4_ = bf16[1024,512]{1,0:T(8,128)(2,1)S(1)} custom-call(bf16[256,4096]{1,0:T(8,128)(2,1)S(1)} %bitcast.14, bf16[256,512]{1,0:T(8,128)(2,1)S(1)} %bitcast.30, bf16[512,512]{1,0:T(8,128)(2,1)S(1)} %shard_map.134.refs_0_), custom_call_target="tpu_custom_call" | custom-call | flops 23000000512 | tf_op jit(solution)/shard_map/pallas_call | solution.py:54
  13.4 0.7 %collective-permute-done.2.refs_1_ = s16[256,128]{1,0:T(8,128)(2,1)S(1)} collective-permute-done((s16[256,128]{1,0:T(8,128)(2,1)S(1)}, s16[256,128]{1,0:T(8,128)(2,1)S(1)}, u32[]{:S(2)}, u32[]{:S(2)}) %collective-permute-start.2) | collective-permute-done | bytes 65568 | tf_op jit(solution)/shard_map/ppermute | solution.py:249
  14.1 0.0 collective-permute-start.6
  14.1 2.8 %collective-permute-done.3.refs_2_ = s16[256,128]{1,0:T(8,128)(2,1)S(1)} collective-permute-done((s16[256,128]{1,0:T(8,128)(2,1)S(1)}, s16[256,128]{1,0:T(8,128)(2,1)S(1)}, u32[]{:S(2)}, u32[]{:S(2)}) %collective-permute-start.3) | collective-permute-done | bytes 65568 | tf_op jit(solution)/shard_map/ppermute | solution.py:249
  17.0 0.6 %collective-permute-done.5.refs_3_ = s16[256,128]{1,0:T(8,128)(2,1)S(1)} collective-permute-done((s16[256,128]{1,0:T(8,128)(2,1)S(1)}, s16[256,128]{1,0:T(8,128)(2,1)S(1)}, u32[]{:S(2)}, u32[]{:S(2)}) %collective-permute-start.5) | collective-permute-done | bytes 65568 | tf_op jit(solution)/shard_map/ppermute | solution.py:249
  17.6 0.2 shard_map.136.refs_0_.refs_1_.code_ref
  17.7 1.6 %collective-permute-start.8 = (s16[256,128]{1,0:T(8,128)(2,1)S(1)}, s16[256,128]{1,0:T(8,128)(2,1)S(1)}, u32[]{:S(2)}, u32[]{:S(2)}) collective-permute-start(s16[256,128]{1,0:T(8,128)(2,1)S(1)} %shard_map.136.refs_0_.refs_1_.code_ref), channel_id=1, source_target_pairs={{0,1},{1,0},{2,3},{3,2},{4,5},{5,4},{6,7},{7,6},{8,9},{9,8},{10,11... | collective-permute-start | bytes 196616 | tf_op jit(solution)/shard_map/ppermute | solution.py:249
  19.3 0.5 %shard_map.137.refs_1_.own_ref = f32[1024,512]{1,0:T(8,128)S(1)} custom-call(bf16[256,4096]{1,0:T(8,128)(2,1)S(1)} %bitcast.15, bf16[256,512]{1,0:T(8,128)(2,1)S(1)} %bitcast.31, s16[256,128]{1,0:T(8,128)(2,1)S(1)} %shard_map.136.refs_0_.refs_1_.code_ref), custom_call_target="tpu_custom_call" | custom-call | flops 23000000512 | tf_op jit(solution)/shard_map/pallas_call | solution.py:54
  19.8 0.0 copy-start.1
  19.8 0.0 copy-start.2
  19.8 0.0 copy-start.3
  19.8 0.3 shard_map.138
  20.1 0.8 %collective-permute-start.7 = (bf16[256,512]{1,0:T(8,128)(2,1)S(1)}, bf16[256,512]{1,0:T(8,128)(2,1)S(1)}, u32[]{:S(2)}, u32[]{:S(2)}) collective-permute-start(bf16[256,512]{1,0:T(8,128)(2,1)S(1)} %shard_map.138), channel_id=1, source_target_pairs={{0,16},{8,24},{16,0},{24,8},{1,17},{9,25},{17,1},{25,9},{2,18},{10... | collective-permute-start | bytes 786440 | tf_op jit(solution)/shard_map/ppermute | solution.py:249
  20.9 1.2 %collective-permute-done.8.refs_0_ = s16[256,128]{1,0:T(8,128)(2,1)S(1)} collective-permute-done((s16[256,128]{1,0:T(8,128)(2,1)S(1)}, s16[256,128]{1,0:T(8,128)(2,1)S(1)}, u32[]{:S(2)}, u32[]{:S(2)}) %collective-permute-start.8) | collective-permute-done | bytes 65568 | tf_op jit(solution)/shard_map/ppermute | solution.py:249
  22.1 2.1 %collective-permute-start.11 = (s16[256,128]{1,0:T(8,128)(2,1)S(1)}, s16[256,128]{1,0:T(8,128)(2,1)S(1)}, u32[]{:S(2)}, u32[]{:S(2)}) collective-permute-start(s16[256,128]{1,0:T(8,128)(2,1)S(1)} %shard_map.139.refs_0_), channel_id=1, source_target_pairs={{0,6},{1,7},{2,4},{3,5},{4,2},{5,3},{6,0},{7,1},{8,14},{9,15},{10,... | collective-permute-start | bytes 196616 | tf_op jit(solution)/shard_map/ppermute | solution.py:249
  24.2 0.0 collective-permute-done.12.chip_ref
  24.2 0.0 collective-permute-start.10
  24.2 0.0 collective-permute-done.6.core_ref
  24.2 2.4 %collective-permute-start.9 = (s16[256,128]{1,0:T(8,128)(2,1)S(1)}, s16[256,128]{1,0:T(8,128)(2,1)S(1)}, u32[]{:S(2)}, u32[]{:S(2)}) collective-permute-start(s16[256,128]{1,0:T(8,128)(2,1)S(1)} %shard_map.139.refs_0_), channel_id=1, source_target_pairs={{0,2},{1,3},{2,0},{3,1},{4,6},{5,7},{6,4},{7,5},{8,10},{9,11},{10,... | collective-permute-start | bytes 196616 | tf_op jit(solution)/shard_map/ppermute | solution.py:249
  26.6 1.3 %shard_map.140 = (f32[1024,512]{1,0:T(8,128)}, bf16[1024,512]{1,0:T(8,128)(2,1)}, bf16[1024,512]{1,0:T(8,128)(2,1)}, f32[256,128]{1,0:T(8,128)S(1)}) custom-call(f32[1024,512]{1,0:T(8,128)S(1)} %shard_map.137.refs_1_.own_ref, bf16[1024,512]{1,0:T(8,128)(2,1)S(1)} %collective-permute-done.6.core_ref, bf16[256,512]{1,0:T(8,128)(2,1)S(1)} %collective-permute-done.12.chip_ref, ...), custom_call_target="tpu_custom_call" | custom-call | flops 23000000512 | tf_op jit(solution)/shard_map/pallas_call | solution.py:99
  27.8 0.0 collective-permute-done.13.chip_ref
  27.8 0.0 copy-start.6
  27.8 0.0 copy-start.7
  27.9 1.7 %shard_map.141 = (f32[1024,512]{1,0:T(8,128)}, bf16[1024,512]{1,0:T(8,128)(2,1)}, bf16[1024,512]{1,0:T(8,128)(2,1)}, f32[512,128]{1,0:T(8,128)S(1)}) custom-call(f32[1024,512]{1,0:T(8,128)S(1)} %shard_map.137.refs_1_.own_ref, bf16[1024,512]{1,0:T(8,128)(2,1)S(1)} %collective-permute-done.6.core_ref, ...), custom_call_target="tpu_custom_call", output_to_operand_aliasing={{0}: (6, {}), {1}: (7, {}), {2}: (8, {})} | custom-call | flops 23000000512 | tf_op jit(solution)/shard_map/pallas_call | solution.py:99
  29.6 0.0 collective-permute-done.11.refs_3_
  29.6 0.2 collective-permute-done.10.refs_2_
  29.8 0.0 collective-permute-done.9.refs_1_
  29.8 1.2 %shard_map.142 = (f32[1024,512]{1,0:T(8,128)}, f32[1024,128]{1,0:T(8,128)}, f32[1024,128]{1,0:T(8,128)}, f32[256,128]{1,0:T(8,128)S(1)}) custom-call(f32[1024,128]{1,0:T(8,128)S(1)} %copy-done.6, f32[1024,128]{1,0:T(8,128)S(1)} %copy-done.7, s16[256,128]{1,0:T(8,128)(2,1)S(1)} %shard_map.139.refs_0_, ...), custom_call_target="tpu_custom_call", output_to_operand_aliasing={{0}: (8, {})} | custom-call | tf_op jit(solution)/shard_map/pallas_call | solution.py:184
  31.1 0.0 collective-permute-done.7.chip_ref
  31.1 1.3 %shard_map.143 = (f32[1024,512]{1,0:T(8,128)}, bf16[1024,512]{1,0:T(8,128)(2,1)}, bf16[1024,512]{1,0:T(8,128)(2,1)}) custom-call(f32[1024,512]{1,0:T(8,128)S(1)} %bitcast.19, bf16[1024,512]{1,0:T(8,128)(2,1)S(1)} %bitcast.22, bf16[1024,512]{1,0:T(8,128)(2,1)S(1)} %bitcast.25, ...), custom_call_target="tpu_custom_call", output_to_operand_aliasing={{0}: (7, {}), {1}: (8, {}), {2}: (9, {})} | custom-call | tf_op jit(solution)/shard_map/pallas_call | solution.py:230
  (14 shorter events, 0.1 us)
Async XLA Ops:
  0.6 3.0 %copy-start = (bf16[1,256,4096]{2,1,0:T(8,128)(2,1)S(1)}, bf16[1,256,4096]{2,1,0:T(8,128)(2,1)}, u32[]{:S(2)}) copy-start(bf16[1,256,4096]{2,1,0:T(8,128)(2,1)} %param.9) | copy-start | bytes 6291460
  0.6 3.0 %copy-start.4 = (bf16[1,256,512]{2,1,0:T(8,128)(2,1)S(1)}, bf16[1,256,512]{2,1,0:T(8,128)(2,1)}, u32[]{:S(2)}) copy-start(bf16[1,256,512]{2,1,0:T(8,128)(2,1)} %param.10) | copy-start | bytes 786436
  0.7 6.5 %collective-permute-start = (s32[8,128]{1,0:T(8,128)}, s32[8,128]{1,0:T(8,128)S(1)}, u32[]{:S(2)}, u32[]{:S(2)}) collective-permute-start(s32[8,128]{1,0:T(8,128)} %bitcast.34), channel_id=1, source_target_pairs={{0,1},{1,0},{2,3},{3,2},{4,5},{5,4},{6,7},{7,6},{8,9},{9,8},{10,11... | collective-permute-start | bytes 12296 | tf_op jit(solution)/shard_map/ppermute | solution.py:249
  3.9 1.6 %collective-permute-start.1 = (bf16[256,512]{1,0:T(8,128)(2,1)S(1)}, bf16[256,512]{1,0:T(8,128)(2,1)S(1)}, u32[]{:S(2)}, u32[]{:S(2)}) collective-permute-start(bf16[256,512]{1,0:T(8,128)(2,1)S(1)} %shard_map.129.refs_0_), channel_id=1, source_target_pairs={{0,8},{8,0},{16,24},{24,16},{1,9},{9,1},{17,25},{25,17},{2,10},{10... | collective-permute-start | bytes 786440 | tf_op jit(solution)/shard_map/ppermute | solution.py:249
  4.4 2.7 %copy-start.5 = (s32[1,1024,128]{2,1,0:T(8,128)S(1)}, s32[1,1024,128]{2,1,0:T(8,128)}, u32[]{:S(2)}) copy-start(s32[1,1024,128]{2,1,0:T(8,128)} %param.16) | copy-start | bytes 1572868
  4.4 2.7 %copy-start.8 = (s32[1,1024]{1,0:T(1,128)S(1)}, s32[1,1024]{1,0:T(1,128)}, u32[]{:S(2)}) copy-start(s32[1,1024]{1,0:T(1,128)} %param.17) | copy-start | bytes 12292
  4.5 6.8 %collective-permute-start.4 = (bf16[768,512]{1,0:T(8,128)(2,1)S(1)}, bf16[768,512]{1,0:T(8,128)(2,1)S(1)}, u32[]{:S(2)}, u32[]{:S(2)}) collective-permute-start(bf16[768,512]{1,0:T(8,128)(2,1)S(1)} %shard_map.130.refs_0_), channel_id=1, source_target_pairs={{0,8},{8,0},{16,24},{24,16},{1,9},{9,1},{17,25},{25,17},{2,10},{10... | collective-permute-start | bytes 2359304 | tf_op jit(solution)/shard_map/ppermute | solution.py:249
  5.6 18.6 %collective-permute-start.12 = (bf16[256,512]{1,0:T(8,128)(2,1)S(1)}, bf16[256,512]{1,0:T(8,128)(2,1)S(1)}, u32[]{:S(2)}, u32[]{:S(2)}) collective-permute-start(bf16[256,512]{1,0:T(8,128)(2,1)S(1)} %shard_map.132.refs_2_.refs_1_), channel_id=1, source_target_pairs={{0,16},{8,24},{16,0},{24,8},{1,17},{9,25},{17,1},{25,9},{2,18},{10... | collective-permute-start | bytes 786440 | tf_op jit(solution)/shard_map/ppermute | solution.py:249
  7.6 6.6 %collective-permute-start.2 = (s16[256,128]{1,0:T(8,128)(2,1)S(1)}, s16[256,128]{1,0:T(8,128)(2,1)S(1)}, u32[]{:S(2)}, u32[]{:S(2)}) collective-permute-start(s16[256,128]{1,0:T(8,128)(2,1)S(1)} %get-tuple-element.26), channel_id=1, source_target_pairs={{0,6},{1,7},{2,4},{3,5},{4,2},{5,3},{6,0},{7,1},{8,14},{9,15},{10,... | collective-permute-start | bytes 196616 | tf_op jit(solution)/shard_map/ppermute | solution.py:249
  11.2 5.7 %collective-permute-start.3 = (s16[256,128]{1,0:T(8,128)(2,1)S(1)}, s16[256,128]{1,0:T(8,128)(2,1)S(1)}, u32[]{:S(2)}, u32[]{:S(2)}) collective-permute-start(s16[256,128]{1,0:T(8,128)(2,1)S(1)} %get-tuple-element.27), channel_id=1, source_target_pairs={{0,4},{1,5},{2,6},{3,7},{4,0},{5,1},{6,2},{7,3},{8,12},{9,13},{10,... | collective-permute-start | bytes 196616 | tf_op jit(solution)/shard_map/ppermute | solution.py:249
  11.6 16.2 %collective-permute-start.13 = (bf16[512,512]{1,0:T(8,128)(2,1)S(1)}, bf16[512,512]{1,0:T(8,128)(2,1)S(1)}, u32[]{:S(2)}, u32[]{:S(2)}) collective-permute-start(bf16[512,512]{1,0:T(8,128)(2,1)S(1)} %shard_map.134.refs_0_), channel_id=1, source_target_pairs={{0,16},{8,24},{16,0},{24,8},{1,17},{9,25},{17,1},{25,9},{2,18},{10... | collective-permute-start | bytes 1572872 | tf_op jit(solution)/shard_map/ppermute | solution.py:249
  12.2 5.4 %collective-permute-start.5 = (s16[256,128]{1,0:T(8,128)(2,1)S(1)}, s16[256,128]{1,0:T(8,128)(2,1)S(1)}, u32[]{:S(2)}, u32[]{:S(2)}) collective-permute-start(s16[256,128]{1,0:T(8,128)(2,1)S(1)} %get-tuple-element.29), channel_id=1, source_target_pairs={{0,2},{1,3},{2,0},{3,1},{4,6},{5,7},{6,4},{7,5},{8,10},{9,11},{10,... | collective-permute-start | bytes 196616 | tf_op jit(solution)/shard_map/ppermute | solution.py:249
  14.1 10.0 %collective-permute-start.6 = (bf16[1024,512]{1,0:T(8,128)(2,1)S(1)}, bf16[1024,512]{1,0:T(8,128)(2,1)S(1)}, u32[]{:S(2)}, u32[]{:S(2)}) collective-permute-start(bf16[1024,512]{1,0:T(8,128)(2,1)S(1)} %shard_map.135.refs_4_), channel_id=1, source_target_pairs={{0,8},{8,0},{16,24},{24,16},{1,9},{9,1},{17,25},{25,17},{2,10},{10... | collective-permute-start | bytes 3145736 | tf_op jit(solution)/shard_map/ppermute | solution.py:249
  17.7 4.3 %collective-permute-start.8 = (s16[256,128]{1,0:T(8,128)(2,1)S(1)}, s16[256,128]{1,0:T(8,128)(2,1)S(1)}, u32[]{:S(2)}, u32[]{:S(2)}) collective-permute-start(s16[256,128]{1,0:T(8,128)(2,1)S(1)} %shard_map.136.refs_0_.refs_1_.code_ref), channel_id=1, source_target_pairs={{0,1},{1,0},{2,3},{3,2},{4,5},{5,4},{6,7},{7,6},{8,9},{9,8},{10,11... | collective-permute-start | bytes 196616 | tf_op jit(solution)/shard_map/ppermute | solution.py:249
  19.8 6.8 %copy-start.1 = (f32[1,1024,512]{2,1,0:T(8,128)S(1)}, f32[1,1024,512]{2,1,0:T(8,128)}, u32[]{:S(2)}) copy-start(f32[1,1024,512]{2,1,0:T(8,128)} %param.11) | copy-start | bytes 6291460
  19.8 6.8 %copy-start.2 = (bf16[1,1024,512]{2,1,0:T(8,128)(2,1)S(1)}, bf16[1,1024,512]{2,1,0:T(8,128)(2,1)}, u32[]{:S(2)}) copy-start(bf16[1,1024,512]{2,1,0:T(8,128)(2,1)} %param.12) | copy-start | bytes 3145732
  19.8 6.8 %copy-start.3 = (bf16[1,1024,512]{2,1,0:T(8,128)(2,1)S(1)}, bf16[1,1024,512]{2,1,0:T(8,128)(2,1)}, u32[]{:S(2)}) copy-start(bf16[1,1024,512]{2,1,0:T(8,128)(2,1)} %param.13) | copy-start | bytes 3145732
  20.1 11.0 %collective-permute-start.7 = (bf16[256,512]{1,0:T(8,128)(2,1)S(1)}, bf16[256,512]{1,0:T(8,128)(2,1)S(1)}, u32[]{:S(2)}, u32[]{:S(2)}) collective-permute-start(bf16[256,512]{1,0:T(8,128)(2,1)S(1)} %shard_map.138), channel_id=1, source_target_pairs={{0,16},{8,24},{16,0},{24,8},{1,17},{9,25},{17,1},{25,9},{2,18},{10... | collective-permute-start | bytes 786440 | tf_op jit(solution)/shard_map/ppermute | solution.py:249
  22.1 7.5 %collective-permute-start.11 = (s16[256,128]{1,0:T(8,128)(2,1)S(1)}, s16[256,128]{1,0:T(8,128)(2,1)S(1)}, u32[]{:S(2)}, u32[]{:S(2)}) collective-permute-start(s16[256,128]{1,0:T(8,128)(2,1)S(1)} %shard_map.139.refs_0_), channel_id=1, source_target_pairs={{0,6},{1,7},{2,4},{3,5},{4,2},{5,3},{6,0},{7,1},{8,14},{9,15},{10,... | collective-permute-start | bytes 196616 | tf_op jit(solution)/shard_map/ppermute | solution.py:249
  24.2 5.6 %collective-permute-start.10 = (s16[256,128]{1,0:T(8,128)(2,1)S(1)}, s16[256,128]{1,0:T(8,128)(2,1)S(1)}, u32[]{:S(2)}, u32[]{:S(2)}) collective-permute-start(s16[256,128]{1,0:T(8,128)(2,1)S(1)} %shard_map.139.refs_0_), channel_id=1, source_target_pairs={{0,4},{1,5},{2,6},{3,7},{4,0},{5,1},{6,2},{7,3},{8,12},{9,13},{10,... | collective-permute-start | bytes 196616 | tf_op jit(solution)/shard_map/ppermute | solution.py:249
  24.2 5.6 %collective-permute-start.9 = (s16[256,128]{1,0:T(8,128)(2,1)S(1)}, s16[256,128]{1,0:T(8,128)(2,1)S(1)}, u32[]{:S(2)}, u32[]{:S(2)}) collective-permute-start(s16[256,128]{1,0:T(8,128)(2,1)S(1)} %shard_map.139.refs_0_), channel_id=1, source_target_pairs={{0,2},{1,3},{2,0},{3,1},{4,6},{5,7},{6,4},{7,5},{8,10},{9,11},{10,... | collective-permute-start | bytes 196616 | tf_op jit(solution)/shard_map/ppermute | solution.py:249
  27.8 2.0 %copy-start.6 = (f32[1024,128]{1,0:T(8,128)S(1)}, f32[1024,128]{1,0:T(8,128)}, u32[]{:S(2)}) copy-start(f32[1024,128]{1,0:T(8,128)} %ow_ref.1) | copy-start | bytes 1572868
  27.8 2.0 %copy-start.7 = (f32[1024,128]{1,0:T(8,128)S(1)}, f32[1024,128]{1,0:T(8,128)}, u32[]{:S(2)}) copy-start(f32[1024,128]{1,0:T(8,128)} %om_ref.1) | copy-start | bytes 1572868

commit v6 on v5

--- a/solution.py
+++ b/solution.py
@@ -70,8 +70,8 @@
     return updated, moment_one.astype(first.dtype), moment_two.astype(second.dtype)
 
 
-def adam_kernel(row, own_ref, core_ref, chip_ref, weight_ref, first_ref, second_ref, *refs):
-    weight_out, first_out, second_out, head_out, weight_new, first_new, second_new, sems = refs[-8:]
+def adam_kernel(row, ahead, own_ref, core_ref, chip_ref, weight_ref, first_ref, second_ref, *refs):
+    weight_out, first_out, second_out, head_out, *base, weight_new, first_new, second_new, sems = refs[-8 - (ahead > 0):]
     count = chip_ref.shape[0]
     stores = []
     for i in range(count // BLOCK):
@@ -89,19 +89,22 @@
                 )
             )
             stores[-1].start()
+    if ahead:
+        base[0][...] = own_ref[-ahead:, :] + core_ref[-ahead:, :].astype(jnp.float32)
     for copy in stores:
         copy.wait()
 
 
-def adam(own, core, chip, weight, first, second, row, head, outs=(), us=0, after=()):
+def adam(own, core, chip, weight, first, second, row, head, outs=(), us=0, after=(), ahead=0):
     count, width = chip.shape
     operands = [own, core, chip, weight, first, second]
     return pl.pallas_call(
-        functools.partial(adam_kernel, row),
+        functools.partial(adam_kernel, row, ahead),
         out_shape=[jax.ShapeDtypeStruct(a.shape, a.dtype) for a in (weight, first, second)]
-        + [jax.ShapeDtypeStruct((count, head), weight.dtype)],
+        + [jax.ShapeDtypeStruct((count, head), weight.dtype)]
+        + [jax.ShapeDtypeStruct((ahead, width), jnp.float32)] * (ahead > 0),
         in_specs=[VMEM] * len(operands) + [ANY] * (len(outs) + len(after)),
-        out_specs=[ANY] * 3 + [VMEM],
+        out_specs=[ANY] * 3 + [VMEM] * (1 + (ahead > 0)),
         input_output_aliases={len(operands) + i: i for i in range(len(outs))},
         scratch_shapes=[
             pltpu.VMEM((count, width), weight.dtype),
@@ -199,7 +202,7 @@
     )(*operands, weight)
 
 
-def last_kernel(weight_ref, first_ref, second_ref, own_ref, core_ref, chip_ref, outer_ref, *refs):
+def last_kernel(weight_ref, first_ref, second_ref, base_ref, chip_ref, outer_ref, *refs):
     weight_out, first_out, second_out, weight_new, first_new, second_new, sems = refs[3:]
     count = chip_ref.shape[0]
     last = weight_ref.shape[0] - count
@@ -207,7 +210,7 @@
     stores = []
     for i in range(count // BLOCK):
         here, there = slice(i * BLOCK, (i + 1) * BLOCK), slice(last + i * BLOCK, last + (i + 1) * BLOCK)
-        gradient = own_ref[there, :] + core_ref[there, :].astype(jnp.float32) + chip_ref[here, :].astype(jnp.float32)
+        gradient = base_ref[here, :] + chip_ref[here, :].astype(jnp.float32)
         updated, first_new[here, :], second_new[here, :] = adam_step(
             gradient, weight_ref[there, :], first_ref[there, :], second_ref[there, :]
         )
@@ -224,9 +227,9 @@
         copy.wait()
 
 
-def last_step(weight, first, second, own, core, chip, outer, outs):
+def last_step(weight, first, second, base, chip, outer, outs):
     count, width = chip.shape
-    operands = [weight, first, second, own, core, chip, outer]
+    operands = [weight, first, second, base, chip, outer]
     return pl.pallas_call(
         last_kernel,
         out_shape=[jax.ShapeDtypeStruct(a.shape, a.dtype) for a in (weight, first, second)],
@@ -346,17 +349,16 @@
     received = {k: swap(total, "replica", k * group) for k in range(parts - 1, 0, -1)}
     codes = [total] + [received[k] for k in range(1, parts)]
 
-    outs, heads = (), []
-    for (row, _), part in zip(chunks[:-1], arrived):
-        *outs, part_head = adam(
-            own, core, part, weight, first, second, row, head, outs, us=FILL, after=() if outs else (total,)
-        )
-        heads.append(part_head)
+    *outs, first_head, base = adam(
+        own, core, arrived[0], weight, first, second, 0, head, us=FILL, after=(total,), ahead=chunks[2][1]
+    )
+    *outs, second_head = adam(own, core, arrived[1], weight, first, second, chunks[1][0], head, outs, us=FILL)
+    heads = [first_head, second_head]
     weight_new, outer_new, momentum_new, tail = outer_step(
         outs[0], outer_weight, outer_momentum, codes, heads, group, islands
     )
     weight_new, first_new, second_new = last_step(
-        weight, first, second, own, core, arrived[-1], tail, (weight_new, *outs[1:])
+        weight, first, second, base, arrived[-1], tail, (weight_new, *outs[1:])
     )
     return (weight_new[None], first_new[None], second_new[None], outer_new, momentum_new)
 

time: 32.5 us -> 32.5 us (level)
  no operation moved by 1% of the time
where the time goes in v6:
time: 32.5 us; the launch traced here: 32.3 us
  starting transfers between devices  17.1 us (53%)
  Pallas kernels  8.59 us (26%)
  waiting for transfers between devices  5.77 us (18%)
  between operations  0.84 us (3%)
    ppermute x14, starting transfers between devices, swap(): return lax.ppermute(x, axis, [(i, i ^ flip) for i in range(size)])  17.1 us
    ppermute x14, waiting for transfers between devices, swap(): return lax.ppermute(x, axis, [(i, i ^ flip) for i in range(size)])  5.77 us
    pallas_call x2, Pallas kernels, adam(): pl.pallas_call(functools.partial(adam_kernel, row, ahead), out_shape=[jax...  2.98 us
    pallas_call x7, Pallas kernels, product(): pl.pallas_call(functools.partial(product_kernel, flip, row, rows, len(sha...  2.53 us
    pallas_call x1, Pallas kernels, last_step(): pl.pallas_call(last_kernel, out_shape=[jax.ShapeDtypeStruct(a.shape, a.dt...  1.24 us
    pallas_call x1, Pallas kernels, outer_step(): pl.pallas_call(functools.partial(outer_kernel, group, islands, parts, ear...  1.23 us
  transfers between devices with their start and end apart: 14, of which 6 were waited for; matrix products, arithmetic and copies ran while one was open for 0% of the time, Pallas kernels for 23%

profile of v6, /device:TPU:0, one launch (start us, length us, event | category | flops | bytes accessed | tf_op | source)
XLA Modules:
  0.0 32.3 jit_solution(692652108268069575)
XLA Ops:
  0.7 3.0 %collective-permute-start = (s32[8,128]{1,0:T(8,128)}, s32[8,128]{1,0:T(8,128)S(1)}, u32[]{:S(2)}, u32[]{:S(2)}) collective-permute-start(s32[8,128]{1,0:T(8,128)} %bitcast.34), channel_id=1, source_target_pairs={{0,1},{1,0},{2,3},{3,2},{4,5},{5,4},{6,7},{7,6},{8,9},{9,8},{10,11... | collective-permute-start | bytes 12296 | tf_op jit(solution)/shard_map/ppermute | solution.py:252
  3.7 0.3 shard_map.129.refs_0_
  3.9 0.1 collective-permute-start.1
  4.0 0.4 %shard_map.130.refs_0_ = bf16[768,512]{1,0:T(8,128)(2,1)S(1)} custom-call(bf16[256,4096]{1,0:T(8,128)(2,1)S(1)} %bitcast.11, bf16[256,512]{1,0:T(8,128)(2,1)S(1)} %bitcast.27, bf16[256,512]{1,0:T(8,128)(2,1)S(1)} %shard_map.129.refs_0_), custom_call_target="tpu_custom_call" | custom-call | flops 23000000512 | tf_op jit(solution)/shard_map/pallas_call | solution.py:54
  4.4 0.0 copy-start.5
  4.4 0.0 copy-start.8
  4.5 0.6 %collective-permute-start.4 = (bf16[768,512]{1,0:T(8,128)(2,1)S(1)}, bf16[768,512]{1,0:T(8,128)(2,1)S(1)}, u32[]{:S(2)}, u32[]{:S(2)}) collective-permute-start(bf16[768,512]{1,0:T(8,128)(2,1)S(1)} %shard_map.130.refs_0_), channel_id=1, source_target_pairs={{0,8},{8,0},{16,24},{24,16},{1,9},{9,1},{17,25},{25,17},{2,10},{10... | collective-permute-start | bytes 2359304 | tf_op jit(solution)/shard_map/ppermute | solution.py:252
  5.0 0.3 shard_map.131.mine_ref
  5.3 0.2 collective-permute-done.1.other_ref
  5.6 1.6 %collective-permute-start.7 = (bf16[256,512]{1,0:T(8,128)(2,1)S(1)}, bf16[256,512]{1,0:T(8,128)(2,1)S(1)}, u32[]{:S(2)}, u32[]{:S(2)}) collective-permute-start(bf16[256,512]{1,0:T(8,128)(2,1)S(1)} %shard_map.132.refs_2_.refs_1_), channel_id=1, source_target_pairs={{0,16},{8,24},{16,0},{24,8},{1,17},{9,25},{17,1},{25,9},{2,18},{10... | collective-permute-start | bytes 786440 | tf_op jit(solution)/shard_map/ppermute | solution.py:252
  7.2 0.0 collective-permute-done.refs_1_
  7.2 0.4 %shard_map.133 = (s16[256,128]{1,0:T(8,128)(2,1)S(1)}, s16[256,128]{1,0:T(8,128)(2,1)S(1)}, s16[256,128]{1,0:T(8,128)(2,1)S(1)}, s16[256,128]{1,0:T(8,128)(2,1)S(1)}) custom-call(s32[1024,128]{1,0:T(8,128)S(1)} %bitcast.33, s32[8,128]{1,0:T(8,128)S(1)} %bitcast.35, s32[8,128]{1,0:T(8,128)S(1)} %collective-permute-done.refs_1_, ...), custom_call_target="tpu_custom_call" | custom-call | tf_op jit(solution)/shard_map/pallas_call | solution.py:312
  7.6 3.7 %collective-permute-start.2 = (s16[256,128]{1,0:T(8,128)(2,1)S(1)}, s16[256,128]{1,0:T(8,128)(2,1)S(1)}, u32[]{:S(2)}, u32[]{:S(2)}) collective-permute-start(s16[256,128]{1,0:T(8,128)(2,1)S(1)} %get-tuple-element.27), channel_id=1, source_target_pairs={{0,6},{1,7},{2,4},{3,5},{4,2},{5,3},{6,0},{7,1},{8,14},{9,15},{10,... | collective-permute-start | bytes 196616 | tf_op jit(solution)/shard_map/ppermute | solution.py:252
  11.2 0.0 collective-permute-start.3
  11.2 0.0 collective-permute-done.4.refs_0_
  11.2 0.3 %shard_map.134.refs_0_ = bf16[512,512]{1,0:T(8,128)(2,1)S(1)} custom-call(bf16[256,4096]{1,0:T(8,128)(2,1)S(1)} %bitcast.13, bf16[256,512]{1,0:T(8,128)(2,1)S(1)} %bitcast.29, bf16[768,512]{1,0:T(8,128)(2,1)S(1)} %collective-permute-done.4.refs_0_, bf16[256,512]{1,0:T(8,128)(2,1)S(1)} %shard_map.132.refs_2_.refs_1_), custom_call_target="tpu_custom_call" | custom-call | flops 23000000512 | tf_op jit(solution)/shard_map/pallas_call | solution.py:54
  11.6 0.6 %collective-permute-start.13 = (bf16[512,512]{1,0:T(8,128)(2,1)S(1)}, bf16[512,512]{1,0:T(8,128)(2,1)S(1)}, u32[]{:S(2)}, u32[]{:S(2)}) collective-permute-start(bf16[512,512]{1,0:T(8,128)(2,1)S(1)} %shard_map.134.refs_0_), channel_id=1, source_target_pairs={{0,16},{8,24},{16,0},{24,8},{1,17},{9,25},{17,1},{25,9},{2,18},{10... | collective-permute-start | bytes 1572872 | tf_op jit(solution)/shard_map/ppermute | solution.py:252
  12.2 0.8 %collective-permute-start.5 = (s16[256,128]{1,0:T(8,128)(2,1)S(1)}, s16[256,128]{1,0:T(8,128)(2,1)S(1)}, u32[]{:S(2)}, u32[]{:S(2)}) collective-permute-start(s16[256,128]{1,0:T(8,128)(2,1)S(1)} %get-tuple-element.30), channel_id=1, source_target_pairs={{0,2},{1,3},{2,0},{3,1},{4,6},{5,7},{6,4},{7,5},{8,10},{9,11},{10,... | collective-permute-start | bytes 196616 | tf_op jit(solution)/shard_map/ppermute | solution.py:252
  12.9 0.5 %shard_map.135.refs_4_ = bf16[1024,512]{1,0:T(8,128)(2,1)S(1)} custom-call(bf16[256,4096]{1,0:T(8,128)(2,1)S(1)} %bitcast.14, bf16[256,512]{1,0:T(8,128)(2,1)S(1)} %bitcast.30, bf16[512,512]{1,0:T(8,128)(2,1)S(1)} %shard_map.134.refs_0_), custom_call_target="tpu_custom_call" | custom-call | flops 23000000512 | tf_op jit(solution)/shard_map/pallas_call | solution.py:54
  13.4 0.7 %collective-permute-done.2.refs_1_ = s16[256,128]{1,0:T(8,128)(2,1)S(1)} collective-permute-done((s16[256,128]{1,0:T(8,128)(2,1)S(1)}, s16[256,128]{1,0:T(8,128)(2,1)S(1)}, u32[]{:S(2)}, u32[]{:S(2)}) %collective-permute-start.2) | collective-permute-done | bytes 65568 | tf_op jit(solution)/shard_map/ppermute | solution.py:252
  14.1 0.0 collective-permute-start.6
  14.1 2.8 %collective-permute-done.3.refs_2_ = s16[256,128]{1,0:T(8,128)(2,1)S(1)} collective-permute-done((s16[256,128]{1,0:T(8,128)(2,1)S(1)}, s16[256,128]{1,0:T(8,128)(2,1)S(1)}, u32[]{:S(2)}, u32[]{:S(2)}) %collective-permute-start.3) | collective-permute-done | bytes 65568 | tf_op jit(solution)/shard_map/ppermute | solution.py:252
  17.0 0.6 %collective-permute-done.5.refs_3_ = s16[256,128]{1,0:T(8,128)(2,1)S(1)} collective-permute-done((s16[256,128]{1,0:T(8,128)(2,1)S(1)}, s16[256,128]{1,0:T(8,128)(2,1)S(1)}, u32[]{:S(2)}, u32[]{:S(2)}) %collective-permute-start.5) | collective-permute-done | bytes 65568 | tf_op jit(solution)/shard_map/ppermute | solution.py:252
  17.6 0.2 shard_map.136.refs_0_.code_ref.refs_1_
  17.7 1.6 %collective-permute-start.8 = (s16[256,128]{1,0:T(8,128)(2,1)S(1)}, s16[256,128]{1,0:T(8,128)(2,1)S(1)}, u32[]{:S(2)}, u32[]{:S(2)}) collective-permute-start(s16[256,128]{1,0:T(8,128)(2,1)S(1)} %shard_map.136.refs_0_.code_ref.refs_1_), channel_id=1, source_target_pairs={{0,1},{1,0},{2,3},{3,2},{4,5},{5,4},{6,7},{7,6},{8,9},{9,8},{10,11... | collective-permute-start | bytes 196616 | tf_op jit(solution)/shard_map/ppermute | solution.py:252
  19.3 0.5 %shard_map.137.refs_1_.own_ref = f32[1024,512]{1,0:T(8,128)S(1)} custom-call(bf16[256,4096]{1,0:T(8,128)(2,1)S(1)} %bitcast.15, bf16[256,512]{1,0:T(8,128)(2,1)S(1)} %bitcast.31, s16[256,128]{1,0:T(8,128)(2,1)S(1)} %shard_map.136.refs_0_.code_ref.refs_1_), custom_call_target="tpu_custom_call" | custom-call | flops 23000000512 | tf_op jit(solution)/shard_map/pallas_call | solution.py:54
  19.8 0.0 copy-start.1
  19.8 0.0 copy-start.2
  19.8 0.0 copy-start.3
  19.8 0.3 shard_map.140
  20.1 0.8 %collective-permute-start.9 = (bf16[256,512]{1,0:T(8,128)(2,1)S(1)}, bf16[256,512]{1,0:T(8,128)(2,1)S(1)}, u32[]{:S(2)}, u32[]{:S(2)}) collective-permute-start(bf16[256,512]{1,0:T(8,128)(2,1)S(1)} %shard_map.140), channel_id=1, source_target_pairs={{0,16},{8,24},{16,0},{24,8},{1,17},{9,25},{17,1},{25,9},{2,18},{10... | collective-permute-start | bytes 786440 | tf_op jit(solution)/shard_map/ppermute | solution.py:252
  20.9 1.2 %collective-permute-done.8.refs_0_ = s16[256,128]{1,0:T(8,128)(2,1)S(1)} collective-permute-done((s16[256,128]{1,0:T(8,128)(2,1)S(1)}, s16[256,128]{1,0:T(8,128)(2,1)S(1)}, u32[]{:S(2)}, u32[]{:S(2)}) %collective-permute-start.8) | collective-permute-done | bytes 65568 | tf_op jit(solution)/shard_map/ppermute | solution.py:252
  22.1 2.1 %collective-permute-start.12 = (s16[256,128]{1,0:T(8,128)(2,1)S(1)}, s16[256,128]{1,0:T(8,128)(2,1)S(1)}, u32[]{:S(2)}, u32[]{:S(2)}) collective-permute-start(s16[256,128]{1,0:T(8,128)(2,1)S(1)} %shard_map.138.refs_0_), channel_id=1, source_target_pairs={{0,6},{1,7},{2,4},{3,5},{4,2},{5,3},{6,0},{7,1},{8,14},{9,15},{10,... | collective-permute-start | bytes 196616 | tf_op jit(solution)/shard_map/ppermute | solution.py:252
  24.2 0.0 collective-permute-done.7.chip_ref
  24.2 0.0 collective-permute-start.11
  24.2 0.0 collective-permute-done.6.core_ref
  24.2 2.4 %collective-permute-start.10 = (s16[256,128]{1,0:T(8,128)(2,1)S(1)}, s16[256,128]{1,0:T(8,128)(2,1)S(1)}, u32[]{:S(2)}, u32[]{:S(2)}) collective-permute-start(s16[256,128]{1,0:T(8,128)(2,1)S(1)} %shard_map.138.refs_0_), channel_id=1, source_target_pairs={{0,2},{1,3},{2,0},{3,1},{4,6},{5,7},{6,4},{7,5},{8,10},{9,11},{10,... | collective-permute-start | bytes 196616 | tf_op jit(solution)/shard_map/ppermute | solution.py:252
  26.6 1.3 %shard_map.139 = (f32[1024,512]{1,0:T(8,128)}, bf16[1024,512]{1,0:T(8,128)(2,1)}, bf16[1024,512]{1,0:T(8,128)(2,1)}, f32[256,128]{1,0:T(8,128)S(1)}, f32[256,512]{1,0:T(8,128)S(1)}) custom-call(f32[1024,512]{1,0:T(8,128)S(1)} %shard_map.137.refs_1_.own_ref, bf16[1024,512]{1,0:T(8,128)(2,1)S(1)} %collective-permute-done.6.core_ref, ...), custom_call_target="tpu_custom_call" | custom-call | flops 23000000512 | tf_op jit(solution)/shard_map/pallas_call | solution.py:101
  27.8 0.0 collective-permute-done.13.chip_ref
  27.8 0.0 copy-start.6
  27.8 0.0 copy-start.7
  27.9 1.7 %shard_map.141 = (f32[1024,512]{1,0:T(8,128)}, bf16[1024,512]{1,0:T(8,128)(2,1)}, bf16[1024,512]{1,0:T(8,128)(2,1)}, f32[512,128]{1,0:T(8,128)S(1)}) custom-call(f32[1024,512]{1,0:T(8,128)S(1)} %shard_map.137.refs_1_.own_ref, bf16[1024,512]{1,0:T(8,128)(2,1)S(1)} %collective-permute-done.6.core_ref, ...), custom_call_target="tpu_custom_call", output_to_operand_aliasing={{0}: (6, {}), {1}: (7, {}), {2}: (8, {})} | custom-call | flops 23000000512 | tf_op jit(solution)/shard_map/pallas_call | solution.py:101
  29.6 0.0 collective-permute-done.12.refs_3_
  29.6 0.2 collective-permute-done.11.refs_2_
  29.8 0.0 collective-permute-done.10.refs_1_
  29.8 1.2 %shard_map.142 = (f32[1024,512]{1,0:T(8,128)}, f32[1024,128]{1,0:T(8,128)}, f32[1024,128]{1,0:T(8,128)}, f32[256,128]{1,0:T(8,128)S(1)}) custom-call(f32[1024,128]{1,0:T(8,128)S(1)} %copy-done.6, f32[1024,128]{1,0:T(8,128)S(1)} %copy-done.7, s16[256,128]{1,0:T(8,128)(2,1)S(1)} %shard_map.138.refs_0_, ...), custom_call_target="tpu_custom_call", output_to_operand_aliasing={{0}: (8, {})} | custom-call | tf_op jit(solution)/shard_map/pallas_call | solution.py:187
  31.1 0.0 collective-permute-done.9.chip_ref
  31.1 1.2 %shard_map.143 = (f32[1024,512]{1,0:T(8,128)}, bf16[1024,512]{1,0:T(8,128)(2,1)}, bf16[1024,512]{1,0:T(8,128)(2,1)}) custom-call(f32[1024,512]{1,0:T(8,128)S(1)} %bitcast.19, bf16[1024,512]{1,0:T(8,128)(2,1)S(1)} %bitcast.22, bf16[1024,512]{1,0:T(8,128)(2,1)S(1)} %bitcast.25, ...), custom_call_target="tpu_custom_call", output_to_operand_aliasing={{0}: (6, {}), {1}: (7, {}), {2}: (8, {})} | custom-call | tf_op jit(solution)/shard_map/pallas_call | solution.py:233
  (14 shorter events, 0.1 us)
Async XLA Ops:
  0.6 3.0 %copy-start = (bf16[1,256,4096]{2,1,0:T(8,128)(2,1)S(1)}, bf16[1,256,4096]{2,1,0:T(8,128)(2,1)}, u32[]{:S(2)}) copy-start(bf16[1,256,4096]{2,1,0:T(8,128)(2,1)} %param.9) | copy-start | bytes 6291460
  0.6 3.0 %copy-start.4 = (bf16[1,256,512]{2,1,0:T(8,128)(2,1)S(1)}, bf16[1,256,512]{2,1,0:T(8,128)(2,1)}, u32[]{:S(2)}) copy-start(bf16[1,256,512]{2,1,0:T(8,128)(2,1)} %param.10) | copy-start | bytes 786436
  0.7 6.5 %collective-permute-start = (s32[8,128]{1,0:T(8,128)}, s32[8,128]{1,0:T(8,128)S(1)}, u32[]{:S(2)}, u32[]{:S(2)}) collective-permute-start(s32[8,128]{1,0:T(8,128)} %bitcast.34), channel_id=1, source_target_pairs={{0,1},{1,0},{2,3},{3,2},{4,5},{5,4},{6,7},{7,6},{8,9},{9,8},{10,11... | collective-permute-start | bytes 12296 | tf_op jit(solution)/shard_map/ppermute | solution.py:252
  3.9 1.6 %collective-permute-start.1 = (bf16[256,512]{1,0:T(8,128)(2,1)S(1)}, bf16[256,512]{1,0:T(8,128)(2,1)S(1)}, u32[]{:S(2)}, u32[]{:S(2)}) collective-permute-start(bf16[256,512]{1,0:T(8,128)(2,1)S(1)} %shard_map.129.refs_0_), channel_id=1, source_target_pairs={{0,8},{8,0},{16,24},{24,16},{1,9},{9,1},{17,25},{25,17},{2,10},{10... | collective-permute-start | bytes 786440 | tf_op jit(solution)/shard_map/ppermute | solution.py:252
  4.4 2.7 %copy-start.5 = (s32[1,1024,128]{2,1,0:T(8,128)S(1)}, s32[1,1024,128]{2,1,0:T(8,128)}, u32[]{:S(2)}) copy-start(s32[1,1024,128]{2,1,0:T(8,128)} %param.16) | copy-start | bytes 1572868
  4.4 2.7 %copy-start.8 = (s32[1,1024]{1,0:T(1,128)S(1)}, s32[1,1024]{1,0:T(1,128)}, u32[]{:S(2)}) copy-start(s32[1,1024]{1,0:T(1,128)} %param.17) | copy-start | bytes 12292
  4.5 6.8 %collective-permute-start.4 = (bf16[768,512]{1,0:T(8,128)(2,1)S(1)}, bf16[768,512]{1,0:T(8,128)(2,1)S(1)}, u32[]{:S(2)}, u32[]{:S(2)}) collective-permute-start(bf16[768,512]{1,0:T(8,128)(2,1)S(1)} %shard_map.130.refs_0_), channel_id=1, source_target_pairs={{0,8},{8,0},{16,24},{24,16},{1,9},{9,1},{17,25},{25,17},{2,10},{10... | collective-permute-start | bytes 2359304 | tf_op jit(solution)/shard_map/ppermute | solution.py:252
  5.6 18.6 %collective-permute-start.7 = (bf16[256,512]{1,0:T(8,128)(2,1)S(1)}, bf16[256,512]{1,0:T(8,128)(2,1)S(1)}, u32[]{:S(2)}, u32[]{:S(2)}) collective-permute-start(bf16[256,512]{1,0:T(8,128)(2,1)S(1)} %shard_map.132.refs_2_.refs_1_), channel_id=1, source_target_pairs={{0,16},{8,24},{16,0},{24,8},{1,17},{9,25},{17,1},{25,9},{2,18},{10... | collective-permute-start | bytes 786440 | tf_op jit(solution)/shard_map/ppermute | solution.py:252
  7.6 6.6 %collective-permute-start.2 = (s16[256,128]{1,0:T(8,128)(2,1)S(1)}, s16[256,128]{1,0:T(8,128)(2,1)S(1)}, u32[]{:S(2)}, u32[]{:S(2)}) collective-permute-start(s16[256,128]{1,0:T(8,128)(2,1)S(1)} %get-tuple-element.27), channel_id=1, source_target_pairs={{0,6},{1,7},{2,4},{3,5},{4,2},{5,3},{6,0},{7,1},{8,14},{9,15},{10,... | collective-permute-start | bytes 196616 | tf_op jit(solution)/shard_map/ppermute | solution.py:252
  11.2 5.7 %collective-permute-start.3 = (s16[256,128]{1,0:T(8,128)(2,1)S(1)}, s16[256,128]{1,0:T(8,128)(2,1)S(1)}, u32[]{:S(2)}, u32[]{:S(2)}) collective-permute-start(s16[256,128]{1,0:T(8,128)(2,1)S(1)} %get-tuple-element.28), channel_id=1, source_target_pairs={{0,4},{1,5},{2,6},{3,7},{4,0},{5,1},{6,2},{7,3},{8,12},{9,13},{10,... | collective-permute-start | bytes 196616 | tf_op jit(solution)/shard_map/ppermute | solution.py:252
  11.6 16.2 %collective-permute-start.13 = (bf16[512,512]{1,0:T(8,128)(2,1)S(1)}, bf16[512,512]{1,0:T(8,128)(2,1)S(1)}, u32[]{:S(2)}, u32[]{:S(2)}) collective-permute-start(bf16[512,512]{1,0:T(8,128)(2,1)S(1)} %shard_map.134.refs_0_), channel_id=1, source_target_pairs={{0,16},{8,24},{16,0},{24,8},{1,17},{9,25},{17,1},{25,9},{2,18},{10... | collective-permute-start | bytes 1572872 | tf_op jit(solution)/shard_map/ppermute | solution.py:252
  12.2 5.4 %collective-permute-start.5 = (s16[256,128]{1,0:T(8,128)(2,1)S(1)}, s16[256,128]{1,0:T(8,128)(2,1)S(1)}, u32[]{:S(2)}, u32[]{:S(2)}) collective-permute-start(s16[256,128]{1,0:T(8,128)(2,1)S(1)} %get-tuple-element.30), channel_id=1, source_target_pairs={{0,2},{1,3},{2,0},{3,1},{4,6},{5,7},{6,4},{7,5},{8,10},{9,11},{10,... | collective-permute-start | bytes 196616 | tf_op jit(solution)/shard_map/ppermute | solution.py:252
  14.1 10.0 %collective-permute-start.6 = (bf16[1024,512]{1,0:T(8,128)(2,1)S(1)}, bf16[1024,512]{1,0:T(8,128)(2,1)S(1)}, u32[]{:S(2)}, u32[]{:S(2)}) collective-permute-start(bf16[1024,512]{1,0:T(8,128)(2,1)S(1)} %shard_map.135.refs_4_), channel_id=1, source_target_pairs={{0,8},{8,0},{16,24},{24,16},{1,9},{9,1},{17,25},{25,17},{2,10},{10... | collective-permute-start | bytes 3145736 | tf_op jit(solution)/shard_map/ppermute | solution.py:252
  17.7 4.3 %collective-permute-start.8 = (s16[256,128]{1,0:T(8,128)(2,1)S(1)}, s16[256,128]{1,0:T(8,128)(2,1)S(1)}, u32[]{:S(2)}, u32[]{:S(2)}) collective-permute-start(s16[256,128]{1,0:T(8,128)(2,1)S(1)} %shard_map.136.refs_0_.code_ref.refs_1_), channel_id=1, source_target_pairs={{0,1},{1,0},{2,3},{3,2},{4,5},{5,4},{6,7},{7,6},{8,9},{9,8},{10,11... | collective-permute-start | bytes 196616 | tf_op jit(solution)/shard_map/ppermute | solution.py:252
  19.8 6.8 %copy-start.1 = (f32[1,1024,512]{2,1,0:T(8,128)S(1)}, f32[1,1024,512]{2,1,0:T(8,128)}, u32[]{:S(2)}) copy-start(f32[1,1024,512]{2,1,0:T(8,128)} %param.11) | copy-start | bytes 6291460
  19.8 6.8 %copy-start.2 = (bf16[1,1024,512]{2,1,0:T(8,128)(2,1)S(1)}, bf16[1,1024,512]{2,1,0:T(8,128)(2,1)}, u32[]{:S(2)}) copy-start(bf16[1,1024,512]{2,1,0:T(8,128)(2,1)} %param.12) | copy-start | bytes 3145732
  19.8 6.8 %copy-start.3 = (bf16[1,1024,512]{2,1,0:T(8,128)(2,1)S(1)}, bf16[1,1024,512]{2,1,0:T(8,128)(2,1)}, u32[]{:S(2)}) copy-start(bf16[1,1024,512]{2,1,0:T(8,128)(2,1)} %param.13) | copy-start | bytes 3145732
  20.1 11.0 %collective-permute-start.9 = (bf16[256,512]{1,0:T(8,128)(2,1)S(1)}, bf16[256,512]{1,0:T(8,128)(2,1)S(1)}, u32[]{:S(2)}, u32[]{:S(2)}) collective-permute-start(bf16[256,512]{1,0:T(8,128)(2,1)S(1)} %shard_map.140), channel_id=1, source_target_pairs={{0,16},{8,24},{16,0},{24,8},{1,17},{9,25},{17,1},{25,9},{2,18},{10... | collective-permute-start | bytes 786440 | tf_op jit(solution)/shard_map/ppermute | solution.py:252
  22.1 7.5 %collective-permute-start.12 = (s16[256,128]{1,0:T(8,128)(2,1)S(1)}, s16[256,128]{1,0:T(8,128)(2,1)S(1)}, u32[]{:S(2)}, u32[]{:S(2)}) collective-permute-start(s16[256,128]{1,0:T(8,128)(2,1)S(1)} %shard_map.138.refs_0_), channel_id=1, source_target_pairs={{0,6},{1,7},{2,4},{3,5},{4,2},{5,3},{6,0},{7,1},{8,14},{9,15},{10,... | collective-permute-start | bytes 196616 | tf_op jit(solution)/shard_map/ppermute | solution.py:252
  24.2 5.6 %collective-permute-start.11 = (s16[256,128]{1,0:T(8,128)(2,1)S(1)}, s16[256,128]{1,0:T(8,128)(2,1)S(1)}, u32[]{:S(2)}, u32[]{:S(2)}) collective-permute-start(s16[256,128]{1,0:T(8,128)(2,1)S(1)} %shard_map.138.refs_0_), channel_id=1, source_target_pairs={{0,4},{1,5},{2,6},{3,7},{4,0},{5,1},{6,2},{7,3},{8,12},{9,13},{10,... | collective-permute-start | bytes 196616 | tf_op jit(solution)/shard_map/ppermute | solution.py:252
  24.2 5.6 %collective-permute-start.10 = (s16[256,128]{1,0:T(8,128)(2,1)S(1)}, s16[256,128]{1,0:T(8,128)(2,1)S(1)}, u32[]{:S(2)}, u32[]{:S(2)}) collective-permute-start(s16[256,128]{1,0:T(8,128)(2,1)S(1)} %shard_map.138.refs_0_), channel_id=1, source_target_pairs={{0,2},{1,3},{2,0},{3,1},{4,6},{5,7},{6,4},{7,5},{8,10},{9,11},{10,... | collective-permute-start | bytes 196616 | tf_op jit(solution)/shard_map/ppermute | solution.py:252
  27.8 2.0 %copy-start.6 = (f32[1024,128]{1,0:T(8,128)S(1)}, f32[1024,128]{1,0:T(8,128)}, u32[]{:S(2)}) copy-start(f32[1024,128]{1,0:T(8,128)} %ow_ref.1) | copy-start | bytes 1572868
  27.8 2.0 %copy-start.7 = (f32[1024,128]{1,0:T(8,128)S(1)}, f32[1024,128]{1,0:T(8,128)}, u32[]{:S(2)}) copy-start(f32[1024,128]{1,0:T(8,128)} %om_ref.1) | copy-start | bytes 1572868
